TPU v7x, 128 devices: a whole 4x4x4 slice. The times are simulated.
128 devices in a mesh: expert: 32 (over y, x, core), dp: 4 (over z).
Axes of the slice: x: 4, y: 4, z: 4, core: 2. Of those that a mesh axis runs over, the one named last changes fastest.
Arguments:
- tokens: bfloat16 [4096, 7168], P('expert', 'dp'), may hold values from -6 to 6
- grad_out: bfloat16 [4096, 7168], P('expert', 'dp'), may hold values from -6 to 6
- routing: int32 [4096, 2], P('expert'), may hold values from 0 to 15, all different within a row; in each aligned block of 128 rows (0 to 127, 128 to 255, ...) at most 24 rows name the same one
- route_weight: float32 [4096, 2], P('expert'), may hold values from 0.2 to 1
- gate_weight: bfloat16 [7168, 32768], P('dp', 'expert'), may hold values from -0.0625 to 0.0625
- up_weight: bfloat16 [7168, 32768], P('dp', 'expert'), may hold values from -0.0625 to 0.0625
- down_weight: bfloat16 [32768, 7168], P('expert', 'dp'), may hold values from -0.125 to 0.125
Outputs:
- grad_tokens: bfloat16 [4096, 7168], P('expert', 'dp')
- grad_gate: bfloat16 [7168, 32768], P('dp', 'expert')
- grad_up: bfloat16 [7168, 32768], P('dp', 'expert')
- grad_down: bfloat16 [32768, 7168], P('expert', 'dp')
Inputs may be any that keep to these rules, and one draw needn't show every extreme that they name: `routing`: each row names 2 different experts. In the rows of one index of expert (aligned blocks of 128 rows) no expert is named by more than 24 rows, and in some of these blocks one expert is named by exactly 24 rows.
All inputs are finite; a program needn't handle non-finite values.
Results may differ from a plain program's by a relative error of at most 0.012.
Values may be sent and summed in bfloat16 or wider, within the bound.
No kernel may reach another device: no remote copies, remote signals or barrier semaphores. Data moves between devices by JAX's collectives and lax.ppermute only.
A program may use at most 128 MiB of HBM per device.

v0:
```python
import jax
import jax.numpy as jnp
from jax import lax
from jax.sharding import PartitionSpec as P


def contract(first_arr, second_arr, first_dim, second_dim):
    return lax.dot_general(
        first_arr,
        second_arr,
        (((first_dim,), (second_dim,)), ((), ())),
        preferred_element_type=jnp.float32,
    )


def swiglu_backward(gate_sum, up_sum, back_sum):
    sigma = jax.nn.sigmoid(gate_sum)
    active = gate_sum * sigma
    hidden = (active * up_sum).astype(jnp.bfloat16)
    d_up = (back_sum * active).astype(jnp.bfloat16)
    d_gate = (back_sum * up_sum * sigma * (1.0 + gate_sum * (1.0 - sigma))).astype(jnp.bfloat16)
    return (hidden, d_gate, d_up)


def slot_places(routing, expert_count, capacity):
    flat_ids = routing.reshape(-1)
    onehot = (flat_ids[:, None] == jnp.arange(expert_count, dtype=jnp.int32)[None, :]).astype(
        jnp.int32
    )
    before = jnp.cumsum(onehot, axis=0) - onehot
    position = jnp.sum(before * onehot, axis=1)
    return flat_ids * capacity + position


def body(tokens, grad_out, routing, route_weight, gate_weight, up_weight, down_weight):
    owners = lax.axis_size("expert")
    expert_count = owners // 2
    tile_count = owners // expert_count
    tok_rows = tokens.shape[0]
    top_routes = routing.shape[1]
    capacity = 4 * ((3 * tok_rows * top_routes // (2 * expert_count) + 3) // 4)
    feat_width = tokens.shape[1]
    slot_index = slot_places(routing, expert_count, capacity)
    source = jnp.arange(slot_index.shape[0], dtype=jnp.int32) // top_routes
    scaled = (route_weight.reshape(-1)[:, None] * grad_out[source].astype(jnp.float32)).astype(
        jnp.bfloat16
    )
    blank_rows = jnp.zeros((2, expert_count * capacity, feat_width), jnp.bfloat16)
    packed = blank_rows.at[0, slot_index].set(tokens[source]).at[1, slot_index].set(scaled)
    outgoing = jnp.repeat(packed.reshape(2, expert_count, capacity, feat_width), tile_count, axis=1)
    arrived = lax.all_to_all(outgoing, "expert", split_axis=1, concat_axis=1, tiled=True)
    routed = arrived.reshape(2, owners * capacity, feat_width)
    x_rows = routed[0]
    g_rows = routed[1]
    part_gate = contract(x_rows, gate_weight, 1, 0)
    part_up = contract(x_rows, up_weight, 1, 0)
    part_back = contract(g_rows, down_weight, 1, 1)
    gate_sum, up_sum, back_sum = lax.psum((part_gate, part_up, part_back), "dp")
    hidden, d_gate, d_up = swiglu_backward(gate_sum, up_sum, back_sum)
    grad_gate = contract(x_rows, d_gate, 0, 0).astype(jnp.bfloat16)
    grad_up = contract(x_rows, d_up, 0, 0).astype(jnp.bfloat16)
    grad_down = contract(hidden, g_rows, 0, 0).astype(jnp.bfloat16)
    input_rows = contract(d_gate, gate_weight, 1, 1) + contract(d_up, up_weight, 1, 1)
    returned = lax.all_to_all(
        input_rows.reshape(owners, capacity, feat_width).astype(jnp.bfloat16),
        "expert",
        split_axis=0,
        concat_axis=0,
        tiled=True,
    ).astype(jnp.float32)
    summed = jnp.sum(returned.reshape(expert_count, tile_count, capacity, feat_width), axis=1)
    slot_rows = summed.reshape(expert_count * capacity, feat_width)
    grad_tokens = (
        jnp.zeros((tok_rows, feat_width), jnp.float32)
        .at[source]
        .add(slot_rows[slot_index])
        .astype(jnp.bfloat16)
    )
    return (grad_tokens, grad_gate, grad_up, grad_down)


def solution(mesh):
    placed = (
        P("expert", "dp"),
        P("expert", "dp"),
        P("expert", None),
        P("expert", None),
        P("dp", "expert"),
        P("dp", "expert"),
        P("expert", "dp"),
    )
    return jax.shard_map(
        body,
        mesh=mesh,
        in_specs=placed,
        out_specs=(P("expert", "dp"), P("dp", "expert"), P("dp", "expert"), P("expert", "dp")),
        check_vma=False,
    )
```

profile of v0, /device:TPU:2, one launch (start us, length us, event | category | flops | bytes accessed | tf_op | source)
XLA Modules:
  0.0 418.8 jit_solution(4292559281418946598)
XLA Ops:
  7.2 0.0 copy-start
  7.2 0.0 all-reduce.5.cloned.1.call-start
  7.2 0.8 copy.22
  8.1 0.1 eq.29
  8.2 0.1 eq.25
  8.3 0.7 broadcast_multiply_fusion
  9.0 0.6 reduce-window.6
  9.6 0.2 slice_reduce_fusion
  9.9 0.1 copy.21
  10.0 0.1 mul.52
  10.1 0.1 fusion.7
  10.3 0.0 copy-done
  10.3 0.0 copy-start.2
  10.3 2.3 gather_fusion
  12.5 0.0 copy-done.2
  12.6 1.3 gather_fusion.1
  13.9 0.0 copy-done.12
  13.9 0.1 copy.25
  14.0 0.1 mul.54
  14.2 1.1 multiply_convert_fusion.3
  15.3 0.2 broadcast_in_dim.7
  15.5 31.5 %scatter_fusion = bf16[2,384,1792]{2,1,0:T(8,128)(2,1)S(1)} fusion(bf16[2,384,1792]{2,1,0:T(8,128)(2,1)S(1)} %broadcast_in_dim.7, s32[256]{0:T(256)S(1)} %bitcast.51, bf16[256,1792]{1,0:T(8,128)(2,1)} %gather_fusion), kind=kCustom, calls=%fused_computation.3 | custom fusion | bytes 2754560 | tf_op jit(solution)/shard_map/scatter | solution.py:49
  47.0 31.5 %scatter_fusion.1 = bf16[2,384,1792]{2,1,0:T(8,128)(2,1)S(1)} fusion(bf16[2,384,1792]{2,1,0:T(8,128)(2,1)S(1)} %scatter_fusion, s32[256]{0:T(256)S(1)} %bitcast.50, bf16[256,1792]{1,0:T(8,128)(2,1)} %multiply_convert_fusion.3), kind=kCustom, calls=%fused_computation.4 | custom fusion | bytes 2754560 | tf_op jit(solution)/shard_map/scatter | solution.py:49
  78.5 0.2 copy.26
  78.7 0.4 broadcast_in_dim.8
  79.1 71.3 %all_to_all.10 = bf16[2,32,24,1792]{3,2,0,1:T(8,128)(2,1)S(1)} all-to-all(bf16[2,32,24,1792]{3,2,0,1:T(8,128)(2,1)S(1)} %bitcast.49), channel_id=1, replica_groups=mesh['expert'=32,'dp'=4] {'expert'}, dimensions={1} | all-to-all | bytes 11010048 | tf_op jit(solution)/shard_map/all_to_all | solution.py:51
  150.4 0.4 fusion.10
  150.8 0.0 copy-start.7
  150.8 0.0 copy-start.5
  150.8 3.5 copy-done.16
  154.3 4.7 %fusion.12 = f32[768,1024]{1,0:T(8,128)} fusion(bf16[768,1792]{1,0:T(8,128)(2,1)S(1)} %bitcast.54, bf16[1792,1024]{1,0:T(8,128)(2,1)S(1)} %copy-done.16), kind=kOutput, calls=%fused_computation.45 | convolution fusion | flops 2818572288 | bytes 9568256 | tf_op jit(solution)/shard_map/dot_general | solution.py:8
  158.9 0.0 copy-done.7
  158.9 0.0 copy-done.14
  158.9 4.7 %fusion.13 = f32[768,1024]{1,0:T(8,128)} fusion(bf16[768,1792]{1,0:T(8,128)(2,1)S(1)} %bitcast.55, bf16[1792,1024]{1,0:T(8,128)(2,1)S(1)} %copy-done.14), kind=kOutput, calls=%fused_computation.46 | convolution fusion | flops 2818572288 | bytes 9568256 | tf_op jit(solution)/shard_map/dot_general | solution.py:8
  163.6 0.0 copy-done.5
  163.6 0.0 copy-done.13
  163.6 4.7 %fusion.11 = f32[768,1024]{1,0:T(8,128)} fusion(bf16[768,1792]{1,0:T(8,128)(2,1)S(1)} %bitcast.52, bf16[1024,1792]{1,0:T(8,128)(2,1)S(1)} %copy-done.13), kind=kOutput, calls=%fused_computation.44 | convolution fusion | flops 2818572288 | bytes 9568256 | tf_op jit(solution)/shard_map/dot_general | solution.py:8
  168.3 0.0 all-reduce.5.cloned.1.call-update
  168.3 178.6 %all-reduce.5.cloned.1.call-done = (f32[768,1024]{1,0:T(8,128)}, f32[768,1024]{1,0:T(8,128)}, f32[768,1024]{1,0:T(8,128)}) async-done(((f32[768,1024]{1,0:T(8,128)}, f32[768,1024]{1,0:T(8,128)}, f32[768,1024]{1,0:T(8,128)}), (f32[768,1024]{1,0:T(8,128)}, f32[768,1024]{1,0:T(8,128)}, f32[768,1024]{1,0:T(8,128)})) %all-reduce.5.cloned.1.call-update) | async-done | bytes 9437200 | tf_op jit(solution)/shard_map/psum | solution.py:58
  347.0 4.8 %multiply_convert_fusion.1 = (bf16[768,1024]{1,0:T(8,128)(2,1)S(1)}, bf16[768,1024]{1,0:T(8,128)(2,1)S(1)}) fusion(f32[768,1024]{1,0:T(8,128)} %get-tuple-element.5, f32[768,1024]{1,0:T(8,128)} %get-tuple-element.4, f32[768,1024]{1,0:T(8,128)} %get-tuple-element.6), kind=kLoop, calls=%fused_computation.12 | loop fusion | flops 10223616 | bytes 12582912 | tf_op jit(solution)/shard_map/convert_element_type | solution.py:20
  351.8 0.0 copy-start.9
  351.8 0.0 copy-start.11
  351.8 0.0 copy-done.15
  351.8 0.0 copy-start.17
  351.9 3.0 fusion.14
  354.9 0.0 copy-done.9
  354.9 0.0 copy-done.11
  354.9 0.1 copy-done.17
  355.0 4.5 %add_convert_fusion = bf16[768,1792]{1,0:T(8,128)(2,1)} fusion(f32[768,1792]{1,0:T(8,128)S(1)} %fusion.14, bf16[768,1024]{1,0:T(8,128)(2,1)S(1)} %get-tuple-element.9, bf16[1792,1024]{1,0:T(8,128)(2,1)S(1)} %copy-done.17), kind=kOutput, calls=%fused_computation.7 | convolution fusion | flops 2821324800 | bytes 13500416 | tf_op jit(solution)/shard_map/dot_general | solution.py:8
  359.5 7.4 %all-to-all-start.1 = ((bf16[32,24,1792]{2,1,0:T(8,128)(2,1)}), bf16[32,24,1792]{2,1,0:T(8,128)(2,1)S(1)}, u32[]{:S(2)}, u32[]{:S(2)}) async-start(bf16[32,24,1792]{2,1,0:T(8,128)(2,1)} %bitcast.58), calls=%async_computation.1 | async-start | bytes 5505024 | tf_op jit(solution)/shard_map/all_to_all | solution.py:64
  366.9 0.0 copy-start.8
  366.9 0.0 copy-start.10
  366.9 7.3 %convolution_convert_fusion.1 = bf16[1792,1024]{1,0:T(8,128)(2,1)} fusion(bf16[768,1792]{1,0:T(8,128)(2,1)} %bitcast.56, bf16[768,1024]{1,0:T(8,128)(2,1)} %copy-done.11), kind=kOutput, calls=%fused_computation.9 | convolution fusion | flops 2820407296 | bytes 7995392 | tf_op jit(solution)/shard_map/dot_general | solution.py:8
  374.2 0.0 copy-done.8
  374.2 0.0 copy-done.10
  374.2 0.0 copy-start.4
  374.2 0.0 copy-start.6
  374.3 4.5 %convolution_convert_fusion.2 = bf16[1792,1024]{1,0:T(8,128)(2,1)} fusion(bf16[768,1792]{1,0:T(8,128)(2,1)S(1)} %bitcast.57, bf16[768,1024]{1,0:T(8,128)(2,1)S(1)} %copy-done.10), kind=kOutput, calls=%fused_computation.10 | convolution fusion | flops 2820407296 | bytes 7995392 | tf_op jit(solution)/shard_map/dot_general | solution.py:8
  378.8 0.0 copy-start.1
  378.8 4.8 %convolution_convert_fusion = bf16[1024,1792]{1,0:T(8,128)(2,1)} fusion(bf16[768,1792]{1,0:T(8,128)(2,1)S(1)} %bitcast.53, f32[768,1024]{1,0:T(8,128)S(1)} %copy-done.4, f32[768,1024]{1,0:T(8,128)S(1)} %copy-done.3), kind=kOutput, calls=%fused_computation.8 | convolution fusion | flops 2825125888 | bytes 12713984 | tf_op jit(solution)/shard_map/dot_general | solution.py:8
  383.6 18.6 %all-to-all-done.1 = bf16[32,24,1792]{2,1,0:T(8,128)(2,1)S(1)} async-done(((bf16[32,24,1792]{2,1,0:T(8,128)(2,1)}), bf16[32,24,1792]{2,1,0:T(8,128)(2,1)S(1)}, u32[]{:S(2)}, u32[]{:S(2)}) %all-to-all-start.1) | async-done | bytes 2752544 | tf_op jit(solution)/shard_map/all_to_all | solution.py:64
  402.2 2.0 convert_reduce_fusion
  404.2 6.9 %scatter_custom_fusion.2 = f32[128,1792]{1,0:T(8,128)S(1)} fusion(s32[256]{0:T(256)S(1)} %bitcast.63, f32[384,1792]{1,0:T(8,128)} %bitcast.59, s32[1024]{0:T(1024)S(1)} %pad_clamp_fusion, f32[]{:T(128)} %constant.14.clone.1), kind=kCustom, calls=%fused_computation.16 | custom fusion | flops 458752 | bytes 918016 | tf_op jit(solution)/shard_map/scatter-add | solution.py:76
  411.2 0.8 convert_element_type.49
  (18 shorter events, 0.1 us)
Async XLA Ops:
  7.2 3.1 copy-start
  7.2 339.8 %all-reduce.5.cloned.1.call-start = ((), (), s32[]{:S(2)}) async-start(), calls=%async_computation.2 | async-start | bytes 18874368 | tf_op jit(solution)/shard_map/psum | solution.py:58
  10.3 2.3 copy-start.2
  12.6 1.4 copy-start.12
  150.4 3.9 copy-start.16
  150.8 8.2 %copy-start.7 = (bf16[1,32,24,1792]{3,2,0,1:T(8,128)(2,1)}, bf16[1,32,24,1792]{3,2,0,1:T(8,128)(2,1)S(1)}, u32[]{:S(2)}) copy-start(bf16[1,32,24,1792]{3,2,0,1:T(8,128)(2,1)S(1)} %get-tuple-element.12) | copy-start | bytes 8257540
  150.8 12.9 %copy-start.5 = (bf16[1,32,24,1792]{3,2,0,1:T(8,128)(2,1)}, bf16[1,32,24,1792]{3,2,0,1:T(8,128)(2,1)S(1)}, u32[]{:S(2)}) copy-start(bf16[1,32,24,1792]{3,2,0,1:T(8,128)(2,1)S(1)} %get-tuple-element.11) | copy-start | bytes 8257540
  154.3 4.7 %copy-start.14 = (bf16[1792,1024]{1,0:T(8,128)(2,1)S(1)}, bf16[1792,1024]{1,0:T(8,128)(2,1)}, u32[]{:S(2)}) copy-start(bf16[1792,1024]{1,0:T(8,128)(2,1)} %param.11) | copy-start | bytes 11010052
  158.9 4.7 %copy-start.13 = (bf16[1024,1792]{1,0:T(8,128)(2,1)S(1)}, bf16[1024,1792]{1,0:T(8,128)(2,1)}, u32[]{:S(2)}) copy-start(bf16[1024,1792]{1,0:T(8,128)(2,1)} %param.13) | copy-start | bytes 11010052
  347.0 4.9 %copy-start.15 = (bf16[1792,1024]{1,0:T(8,128)(2,1)S(1)}, bf16[1792,1024]{1,0:T(8,128)(2,1)}, u32[]{:S(2)}) copy-start(bf16[1792,1024]{1,0:T(8,128)(2,1)} %param.11) | copy-start | bytes 11010052
  351.8 3.1 copy-start.9
  351.8 3.1 copy-start.11
  351.8 3.2 copy-start.17
  359.5 42.7 %all-to-all-start.1 = ((bf16[32,24,1792]{2,1,0:T(8,128)(2,1)}), bf16[32,24,1792]{2,1,0:T(8,128)(2,1)S(1)}, u32[]{:S(2)}, u32[]{:S(2)}) async-start(bf16[32,24,1792]{2,1,0:T(8,128)(2,1)} %bitcast.58), calls=%async_computation.1 | async-start | bytes 5505024 | tf_op jit(solution)/shard_map/all_to_all | solution.py:64
  366.9 7.3 %copy-start.8 = (bf16[1,32,24,1792]{3,2,0,1:T(8,128)(2,1)S(1)}, bf16[1,32,24,1792]{3,2,0,1:T(8,128)(2,1)}, u32[]{:S(2)}) copy-start(bf16[1,32,24,1792]{3,2,0,1:T(8,128)(2,1)} %copy-done.7) | copy-start | bytes 8257540
  366.9 7.3 %copy-start.10 = (bf16[768,1024]{1,0:T(8,128)(2,1)S(1)}, bf16[768,1024]{1,0:T(8,128)(2,1)}, u32[]{:S(2)}) copy-start(bf16[768,1024]{1,0:T(8,128)(2,1)} %copy-done.9) | copy-start | bytes 4718596
  374.2 4.6 %copy-start.3 = (f32[768,1024]{1,0:T(8,128)S(1)}, f32[768,1024]{1,0:T(8,128)}, u32[]{:S(2)}) copy-start(f32[768,1024]{1,0:T(8,128)} %get-tuple-element.4) | copy-start | bytes 9437188
  374.2 4.6 %copy-start.4 = (f32[768,1024]{1,0:T(8,128)S(1)}, f32[768,1024]{1,0:T(8,128)}, u32[]{:S(2)}) copy-start(f32[768,1024]{1,0:T(8,128)} %get-tuple-element.6) | copy-start | bytes 9437188
  374.2 4.5 %copy-start.6 = (bf16[1,32,24,1792]{3,2,0,1:T(8,128)(2,1)S(1)}, bf16[1,32,24,1792]{3,2,0,1:T(8,128)(2,1)}, u32[]{:S(2)}) copy-start(bf16[1,32,24,1792]{3,2,0,1:T(8,128)(2,1)} %copy-done.5) | copy-start | bytes 8257540
  378.8 33.2 %copy-start.1 = (bf16[128,1792]{1,0:T(8,128)(2,1)S(1)}, bf16[128,1792]{1,0:T(8,128)(2,1)}, u32[]{:S(2)}) copy-start(bf16[128,1792]{1,0:T(8,128)(2,1)} %param.7) | copy-start | bytes 1376260
Sparse Core Ops, SparseCore 0:
  168.5 178.4 all-reduce.4
where the time goes:
time: 423 us; the launch traced here: 419 us
  waiting for transfers between devices  197 us (47%)
  local copies, waits for them, and re-layouts  73.2 us (17%)
  blocking collectives  71.3 us (17%)
  matrix products  38.1 us (9%)
  other arithmetic  17.2 us (4%)
  between operations  14.3 us (3%)
  starting transfers between devices  7.46 us (2%)
    psum x1, waiting for transfers between devices, body(): gate_sum, up_sum, back_sum = lax.psum((part_gate, part_up, part_back), 'dp')  179 us
    all_to_all x1, blocking collectives, body(): lax.all_to_all(outgoing, 'expert', split_axis=1, concat_axis=1, tiled=True)  71.3 us
    scatter x2, local copies, waits for them, and re-layouts, body(): blank_rows.at[0, slot_index].set(tokens[source]).at[1, slot_index]  63 us
    dot_general x8, matrix products, contract(): lax.dot_general(first_arr, second_arr, (((first_dim,), (second_dim,)), ((...  38.1 us
    all_to_all x1, waiting for transfers between devices, body(): lax.all_to_all(input_rows.reshape(owners, capacity, feat_width).astype(jn...  18.6 us
  transfers between devices with their start and end apart: 2, of which 2 were waited for; matrix products, arithmetic and copies ran while one was open for 4% of the time, Pallas kernels for 0%

commit v1 on v0

v1 whole, which is shorter than its diff:
```python
import jax
import jax.numpy as jnp
from jax import lax
from jax.sharding import PartitionSpec as P


def contract(first_arr, second_arr, first_dim, second_dim, kind=jnp.float32):
    return lax.dot_general(
        first_arr,
        second_arr,
        (((first_dim,), (second_dim,)), ((), ())),
        preferred_element_type=jnp.float32,
    ).astype(kind)


def swiglu_backward(gate_sum, up_sum, back_sum):
    sigma = jax.nn.sigmoid(gate_sum)
    active = gate_sum * sigma
    hidden = (active * up_sum).astype(jnp.bfloat16)
    d_up = (back_sum * active).astype(jnp.bfloat16)
    d_gate = (back_sum * up_sum * sigma * (1.0 + gate_sum * (1.0 - sigma))).astype(jnp.bfloat16)
    return (hidden, d_gate, d_up)


def slot_places(routing, expert_count, capacity):
    flat_ids = routing.reshape(-1)
    count = flat_ids.shape[0]
    onehot = flat_ids[:, None] == jnp.arange(expert_count, dtype=jnp.int32)[None, :]
    places = jnp.arange(count, dtype=jnp.int32)
    earlier = (places[None, :] < places[:, None]).astype(jnp.bfloat16)
    before = contract(earlier, onehot.astype(jnp.bfloat16), 1, 0)
    position = jnp.sum(jnp.where(onehot, before, 0.0), axis=1).astype(jnp.int32)
    return (flat_ids * capacity + position).reshape(routing.shape)


def ring_pairs(size, shift):
    return [(i, (i + shift) % size) for i in range(size)]


def rows_at(arrays, start, rows):
    return jnp.stack([lax.dynamic_slice_in_dim(a, start, rows, axis=0) for a in arrays])


def ring_scatter(arrays, ring, axis):
    me = lax.axis_index(axis)
    block = arrays[0].shape[0] // ring
    half = block // 2
    up, down = ring_pairs(ring, 1), ring_pairs(ring, -1)

    def part(offset, which):
        return rows_at(arrays, ((me + offset) % ring) * block + which * half, half)

    far_up = lax.ppermute(part(2, 0), axis, up)
    far_down = lax.ppermute(part(2, 1), axis, down)
    near_up = lax.ppermute(part(1, 1), axis, up)
    near_down = lax.ppermute(part(3, 0), axis, down)
    sum_up = part(1, 0).astype(jnp.float32) + far_up.astype(jnp.float32)
    sum_down = part(3, 1).astype(jnp.float32) + far_down.astype(jnp.float32)
    last_up = lax.ppermute(sum_up.astype(jnp.bfloat16), axis, up)
    last_down = lax.ppermute(sum_down.astype(jnp.bfloat16), axis, down)
    first = part(0, 0).astype(jnp.float32) + last_up.astype(jnp.float32) + near_down.astype(jnp.float32)
    second = part(0, 1).astype(jnp.float32) + last_down.astype(jnp.float32) + near_up.astype(jnp.float32)
    return first, second


def ring_gather(first, second, ring, axis):
    me = lax.axis_index(axis)
    half = first.shape[1]
    block = 2 * half
    up, down = ring_pairs(ring, 1), ring_pairs(ring, -1)
    left_first = lax.ppermute(first, axis, up)
    right_second = lax.ppermute(second, axis, down)
    left_second = lax.ppermute(second, axis, up)
    right_first = lax.ppermute(first, axis, down)
    far_first = lax.ppermute(left_first, axis, up)
    far_second = lax.ppermute(right_second, axis, down)
    whole = []
    for i in range(first.shape[0]):
        full = jnp.zeros((ring * block,) + first.shape[2:], first.dtype)
        for offset, head, tail in (
            (0, first, second),
            (3, left_first, left_second),
            (1, right_first, right_second),
            (2, far_first, far_second),
        ):
            start = ((me + offset) % ring) * block
            full = lax.dynamic_update_slice_in_dim(full, head[i], start, axis=0)
            full = lax.dynamic_update_slice_in_dim(full, tail[i], start + half, axis=0)
        whole.append(full)
    return whole


def body(tokens, grad_out, routing, route_weight, gate_weight, up_weight, down_weight):
    owners = lax.axis_size("expert")
    ring = lax.axis_size("dp")
    expert_count = owners // 2
    tok_rows, feat_width = tokens.shape
    top_routes = routing.shape[1]
    capacity = 4 * ((3 * tok_rows * top_routes // (2 * expert_count) + 3) // 4)
    slot_count = expert_count * capacity
    same_core = [[2 * chip + core for chip in range(expert_count)] for core in range(2)]
    other_core = [(i, i ^ 1) for i in range(owners)]

    slot_index = slot_places(routing, expert_count, capacity)
    slots = jnp.arange(slot_count, dtype=jnp.int32)
    match = slots[:, None, None] == slot_index[None]
    chosen = jnp.any(match, axis=2).astype(jnp.bfloat16)
    slot_weight = jnp.sum(jnp.where(match, route_weight[None], 0.0), axis=(1, 2))

    def dispatch(rows):
        return lax.all_to_all(
            rows.reshape(expert_count, capacity, feat_width),
            "expert",
            split_axis=0,
            concat_axis=0,
            axis_index_groups=same_core,
            tiled=True,
        ).reshape(slot_count, feat_width)

    x_slots = contract(chosen, tokens, 1, 0, jnp.bfloat16)
    x_own = dispatch(x_slots)
    g_slots = (contract(chosen, grad_out, 1, 0) * slot_weight[:, None]).astype(jnp.bfloat16)
    g_own = dispatch(g_slots)
    x_other = lax.ppermute(x_own, "expert", other_core)
    g_other = lax.ppermute(g_own, "expert", other_core)
    x_rows = jnp.concatenate([x_own, x_other])
    g_rows = jnp.concatenate([g_own, g_other])

    part_gate = contract(x_rows, gate_weight, 1, 0, jnp.bfloat16)
    part_up = contract(x_rows, up_weight, 1, 0, jnp.bfloat16)
    gate_up = ring_scatter((part_gate, part_up), ring, "dp")
    part_back = contract(g_rows, down_weight, 1, 1, jnp.bfloat16)
    back = ring_scatter((part_back,), ring, "dp")
    halves = [swiglu_backward(gu[0], gu[1], b[0]) for gu, b in zip(gate_up, back)]
    d_gate, d_up = ring_gather(*[jnp.stack(h[1:]) for h in halves], ring, "dp")
    (hidden,) = ring_gather(*[h[0][None] for h in halves], ring, "dp")

    input_rows = contract(d_gate, gate_weight, 1, 1) + contract(d_up, up_weight, 1, 1)
    from_other = lax.ppermute(input_rows[slot_count:].astype(jnp.bfloat16), "expert", other_core)
    slot_rows = (input_rows[:slot_count] + from_other.astype(jnp.float32)).astype(jnp.bfloat16)
    returned = dispatch(slot_rows)
    grad_tokens = contract(chosen, returned, 0, 0, jnp.bfloat16)
    grad_gate = contract(x_rows, d_gate, 0, 0, jnp.bfloat16)
    grad_up = contract(x_rows, d_up, 0, 0, jnp.bfloat16)
    grad_down = contract(hidden, g_rows, 0, 0, jnp.bfloat16)
    return (grad_tokens, grad_gate, grad_up, grad_down)


def solution(mesh):
    placed = (
        P("expert", "dp"),
        P("expert", "dp"),
        P("expert", None),
        P("expert", None),
        P("dp", "expert"),
        P("dp", "expert"),
        P("expert", "dp"),
    )
    return jax.shard_map(
        body,
        mesh=mesh,
        in_specs=placed,
        out_specs=(P("expert", "dp"), P("dp", "expert"), P("dp", "expert"), P("expert", "dp")),
        check_vma=False,
    )
```

time: 423 us -> 211 us (0.50)
  waiting for transfers between devices: 197 us -> 99.9 us
  blocking collectives: 71.3 us -> 0 us
  local copies, waits for them, and re-layouts: 73.2 us -> 2.74 us
  starting transfers between devices: 7.46 us -> 55.9 us
  between operations: 14.3 us -> 1.21 us
  other arithmetic: 17.2 us -> 4.64 us
  matrix products: 38.1 us -> 43.3 us
    psum x1 -> x0, waiting for transfers between devices: 179 us -> none  [body(): gate_sum, up_sum, back_sum = lax.psum((part_gate, part_up, part_back), 'dp')]
    all_to_all x1 -> x0, blocking collectives: 71.3 us -> none  [body(): lax.all_to_all(outgoing, 'expert', split_axis=1, concat_axis=1, tiled=True)]
    scatter x2 -> x0, local copies, waits for them, and re-layouts: 63 us -> none  [body(): blank_rows.at[0, slot_index].set(tokens[source]).at[1, slot_index]]
    ppermute x0 -> x27, waiting for transfers between devices: none -> 58.8 us  [the longest x2 11.3 us: ring_gather(): left_first = lax.ppermute(first, axis, up)]
    ppermute x0 -> x27, starting transfers between devices: none -> 34.7 us  [the longest x2 7.39 us: ring_scatter(): near_down = lax.ppermute(part(3, 0), axis, down)]
    all_to_all x1 -> x3, waiting for transfers between devices: 18.6 us -> 41.1 us  [dispatch(): lax.all_to_all(rows.reshape(expert_count, capacity, feat_width), 'expert'...]
    all_to_all x1 -> x3, starting transfers between devices: 7.42 us -> 21.2 us  [dispatch(): lax.all_to_all(rows.reshape(expert_count, capacity, feat_width), 'expert'...]
    scatter-add x1 -> x0, other arithmetic: 6.93 us -> none  [body(): grad_tokens = jnp.zeros((tok_rows, feat_width), jnp.float32).at[source].a...]
  transfers between devices with their start and end apart: 2 -> 30, of which waited for: 2 -> 15; matrix products, arithmetic and copies ran while one was open for 4% -> 21% of each run, Pallas kernels for 0% -> 0%
where the time goes in v1:
time: 211 us; the launch traced here: 208 us
  waiting for transfers between devices  99.9 us (47%)
  starting transfers between devices  55.9 us (26%)
  matrix products  43.3 us (21%)
  other arithmetic  4.64 us (2%)
  local copies, waits for them, and re-layouts  2.74 us (1%)
    dot_general x12, matrix products, contract(): lax.dot_general(first_arr, second_arr, (((first_dim,), (second_dim,)), ((...  43.3 us
    all_to_all x3, waiting for transfers between devices, dispatch(): lax.all_to_all(rows.reshape(expert_count, capacity, feat_width), 'expert'...  41.1 us
    all_to_all x3, starting transfers between devices, dispatch(): lax.all_to_all(rows.reshape(expert_count, capacity, feat_width), 'expert'...  21.2 us
    ppermute x2, waiting for transfers between devices, ring_gather(): left_first = lax.ppermute(first, axis, up)  11.3 us
    ppermute x2, waiting for transfers between devices, ring_scatter(): last_up = lax.ppermute(sum_up.astype(jnp.bfloat16), axis, up)  10.7 us
    ppermute x2, waiting for transfers between devices, ring_scatter(): far_up = lax.ppermute(part(2, 0), axis, up)  10.6 us
    ppermute x2, waiting for transfers between devices, ring_scatter(): far_down = lax.ppermute(part(2, 1), axis, down)  9.56 us
    ppermute x2, starting transfers between devices, ring_scatter(): near_down = lax.ppermute(part(3, 0), axis, down)  7.39 us
  transfers between devices with their start and end apart: 30, of which 15 were waited for; matrix products, arithmetic and copies ran while one was open for 21% of the time, Pallas kernels for 0%

profile of v1, /device:TPU:2, one launch (start us, length us, event | category | flops | bytes accessed | tf_op | source)
XLA Modules:
  0.0 207.6 jit_solution(7330915242636267534)
XLA Ops:
  0.6 0.8 copy.21
  1.5 0.1 eq.58
  1.6 0.2 fusion.4
  1.8 0.1 convert_element_type.166
  2.0 0.7 multiply_add_fusion
  2.8 1.6 convolution_convert_fusion.3
  4.4 7.6 %all-to-all-start.1 = ((bf16[16,24,1792]{2,1,0:T(8,128)(2,1)}), bf16[16,24,1792]{2,1,0:T(8,128)(2,1)S(1)}, u32[]{:S(2)}, u32[]{:S(2)}) async-start(bf16[16,24,1792]{2,1,0:T(8,128)(2,1)} %bitcast.7), calls=%async_computation.1 | async-start | bytes 2752512 | tf_op jit(solution)/shard_map/all_to_all | solution.py:111
  12.0 0.1 select_reduce_fusion
  12.2 19.2 %all-to-all-done.1 = bf16[16,24,1792]{2,1,0:T(8,128)(2,1)S(1)} async-done(((bf16[16,24,1792]{2,1,0:T(8,128)(2,1)}), bf16[16,24,1792]{2,1,0:T(8,128)(2,1)S(1)}, u32[]{:S(2)}, u32[]{:S(2)}) %all-to-all-start.1) | async-done | bytes 1376288 | tf_op jit(solution)/shard_map/all_to_all | solution.py:111
  31.4 1.6 fusion
  33.0 6.0 %all-to-all-start = ((bf16[16,24,1792]{2,1,0:T(8,128)(2,1)}), bf16[16,24,1792]{2,1,0:T(8,128)(2,1)S(1)}, u32[]{:S(2)}, u32[]{:S(2)}) async-start(bf16[16,24,1792]{2,1,0:T(8,128)(2,1)} %bitcast), calls=%async_computation | async-start | bytes 2752512 | tf_op jit(solution)/shard_map/all_to_all | solution.py:111
  39.0 21.0 %all-to-all-done = bf16[16,24,1792]{2,1,0:T(8,128)(2,1)S(1)} async-done(((bf16[16,24,1792]{2,1,0:T(8,128)(2,1)}), bf16[16,24,1792]{2,1,0:T(8,128)(2,1)S(1)}, u32[]{:S(2)}, u32[]{:S(2)}) %all-to-all-start) | async-done | bytes 1376288 | tf_op jit(solution)/shard_map/all_to_all | solution.py:111
  60.0 6.0 %convolution_convert_fusion.5 = bf16[768,1024]{1,0:T(8,128)(2,1)S(1)} fusion(bf16[1792,1024]{1,0:T(8,128)(2,1)} %param.12, bf16[384,1792]{1,0:T(8,128)(2,1)} %collective-permute-done.4, bf16[384,1792]{1,0:T(8,128)(2,1)S(1)} %bitcast.248), kind=kOutput, calls=%fused_computation.15 | convolution fusion | flops 2824863744 | bytes 7995392 | tf_op jit(solution)/shard_map/dot_general | solution.py:8
  66.0 4.4 %convolution_convert_fusion.6 = bf16[768,1024]{1,0:T(8,128)(2,1)S(1)} fusion(bf16[1792,1024]{1,0:T(8,128)(2,1)S(1)} %copy-done.12, bf16[384,1792]{1,0:T(8,128)(2,1)} %collective-permute-done.4, bf16[384,1792]{1,0:T(8,128)(2,1)S(1)} %bitcast.249), kind=kOutput, calls=%fused_computation.16 | convolution fusion | flops 2824863744 | bytes 7995392 | tf_op jit(solution)/shard_map/dot_general | solution.py:8
  70.4 0.4 dynamic-slice_bitcast_fusion.6
  70.9 4.1 %collective-permute-start.7 = (bf16[2,96,1024]{2,1,0:T(8,128)(2,1)S(1)}, bf16[2,96,1024]{2,1,0:T(8,128)(2,1)S(1)}, u32[]{:S(2)}, u32[]{:S(2)}) collective-permute-start(bf16[2,96,1024]{2,1,0:T(8,128)(2,1)S(1)} %pad_maximum_fusion.7), channel_id=1, source_target_pairs={{0,3},{1,0},{2,1},{3,2},{4,7},{5,4},{6,5},{7,6},{8,11},{9,8},{10,9... | collective-permute-start | bytes 1179656 | tf_op jit(solution)/shard_map/ppermute | solution.py:56
  75.2 3.0 %fusion.3 = bf16[768,1024]{1,0:T(8,128)(2,1)S(1)} fusion(bf16[1024,1792]{1,0:T(8,128)(2,1)S(1)} %copy-done.10, bf16[384,1792]{1,0:T(8,128)(2,1)S(1)} %collective-permute-done, bf16[384,1792]{1,0:T(8,128)(2,1)S(1)} %bitcast.253), kind=kOutput, calls=%fused_computation.14 | convolution fusion | flops 2824863744 | bytes 7995392 | tf_op jit(solution)/shard_map/dot_general | solution.py:8
  78.2 3.3 %collective-permute-start.3 = (bf16[1,96,1024]{2,1,0:T(8,128)(2,1)S(1)}, bf16[1,96,1024]{2,1,0:T(8,128)(2,1)S(1)}, u32[]{:S(2)}, u32[]{:S(2)}) collective-permute-start(bf16[1,96,1024]{2,1,0:T(8,128)(2,1)S(1)} %get-tuple-element.32), channel_id=1, source_target_pairs={{0,3},{1,0},{2,1},{3,2},{4,7},{5,4},{6,5},{7,6},{8,11},{9,8},{10,9... | collective-permute-start | bytes 589832 | tf_op jit(solution)/shard_map/ppermute | solution.py:56
  81.7 6.5 %collective-permute-done.5 = bf16[2,96,1024]{2,1,0:T(8,128)(2,1)S(1)} collective-permute-done((bf16[2,96,1024]{2,1,0:T(8,128)(2,1)S(1)}, bf16[2,96,1024]{2,1,0:T(8,128)(2,1)S(1)}, u32[]{:S(2)}, u32[]{:S(2)}) %collective-permute-start.5) | collective-permute-done | bytes 393248 | tf_op jit(solution)/shard_map/ppermute | solution.py:53
  88.2 0.1 add_convert_fusion.1
  88.4 4.1 %collective-permute-done.1 = bf16[1,96,1024]{2,1,0:T(8,128)(2,1)S(1)} collective-permute-done((bf16[1,96,1024]{2,1,0:T(8,128)(2,1)S(1)}, bf16[1,96,1024]{2,1,0:T(8,128)(2,1)S(1)}, u32[]{:S(2)}, u32[]{:S(2)}) %collective-permute-start.1) | collective-permute-done | bytes 196640 | tf_op jit(solution)/shard_map/ppermute | solution.py:53
  92.5 6.0 %collective-permute-done.11 = bf16[2,96,1024]{2,1,0:T(8,128)(2,1)S(1)} collective-permute-done((bf16[2,96,1024]{2,1,0:T(8,128)(2,1)S(1)}, bf16[2,96,1024]{2,1,0:T(8,128)(2,1)S(1)}, u32[]{:S(2)}, u32[]{:S(2)}) %collective-permute-start.11) | collective-permute-done | bytes 393248 | tf_op jit(solution)/shard_map/ppermute | solution.py:54
  98.5 0.1 add_convert_fusion
  98.7 3.5 %collective-permute-start.12 = (bf16[2,96,1024]{2,1,0:T(8,128)(2,1)S(1)}, bf16[2,96,1024]{2,1,0:T(8,128)(2,1)S(1)}, u32[]{:S(2)}, u32[]{:S(2)}) collective-permute-start(bf16[2,96,1024]{2,1,0:T(8,128)(2,1)S(1)} %add_convert_fusion), channel_id=1, source_target_pairs={{0,3},{1,0},{2,1},{3,2},{4,7},{5,4},{6,5},{7,6},{8,11},{9,8},{10,9... | collective-permute-start | bytes 1179656 | tf_op jit(solution)/shard_map/ppermute | solution.py:60
  102.2 7.1 %collective-permute-done.6 = bf16[2,96,1024]{2,1,0:T(8,128)(2,1)S(1)} collective-permute-done((bf16[2,96,1024]{2,1,0:T(8,128)(2,1)S(1)}, bf16[2,96,1024]{2,1,0:T(8,128)(2,1)S(1)}, u32[]{:S(2)}, u32[]{:S(2)}) %collective-permute-start.6) | collective-permute-done | bytes 393248 | tf_op jit(solution)/shard_map/ppermute | solution.py:59
  109.3 0.2 convert_add_fusion.1
  109.5 3.6 %collective-permute-done.2 = bf16[1,96,1024]{2,1,0:T(8,128)(2,1)S(1)} collective-permute-done((bf16[1,96,1024]{2,1,0:T(8,128)(2,1)S(1)}, bf16[1,96,1024]{2,1,0:T(8,128)(2,1)S(1)}, u32[]{:S(2)}, u32[]{:S(2)}) %collective-permute-start.2) | collective-permute-done | bytes 196640 | tf_op jit(solution)/shard_map/ppermute | solution.py:59
  113.1 0.2 broadcast.33.clone
  113.3 0.2 fusion.32
  113.6 3.2 %collective-permute-start.8 = (bf16[1,96,1024]{2,1,0:T(8,128)(2,1)S(1)}, bf16[1,96,1024]{2,1,0:T(8,128)(2,1)S(1)}, u32[]{:S(2)}, u32[]{:S(2)}) collective-permute-start(bf16[1,96,1024]{2,1,0:T(8,128)(2,1)S(1)} %get-tuple-element.12), channel_id=1, source_target_pairs={{0,3},{1,0},{2,1},{3,2},{4,7},{5,4},{6,5},{7,6},{8,11},{9,8},{10,9... | collective-permute-start | bytes 589832 | tf_op jit(solution)/shard_map/ppermute | solution.py:54
  116.8 0.2 convert_add_fusion
  117.0 3.5 %collective-permute-done.8 = bf16[1,96,1024]{2,1,0:T(8,128)(2,1)S(1)} collective-permute-done((bf16[1,96,1024]{2,1,0:T(8,128)(2,1)S(1)}, bf16[1,96,1024]{2,1,0:T(8,128)(2,1)S(1)}, u32[]{:S(2)}, u32[]{:S(2)}) %collective-permute-start.8) | collective-permute-done | bytes 196640 | tf_op jit(solution)/shard_map/ppermute | solution.py:54
  120.6 3.8 %collective-permute-start.9 = (bf16[1,96,1024]{2,1,0:T(8,128)(2,1)S(1)}, bf16[1,96,1024]{2,1,0:T(8,128)(2,1)S(1)}, u32[]{:S(2)}, u32[]{:S(2)}) collective-permute-start(bf16[1,96,1024]{2,1,0:T(8,128)(2,1)S(1)} %fusion.5), channel_id=1, source_target_pairs={{0,3},{1,0},{2,1},{3,2},{4,7},{5,4},{6,5},{7,6},{8,11},{9,8},{10,9... | collective-permute-start | bytes 589832 | tf_op jit(solution)/shard_map/ppermute | solution.py:60
  124.4 0.2 broadcast.33.clone.1
  124.6 0.2 fusion.30
  124.8 2.8 %collective-permute-done.9 = bf16[1,96,1024]{2,1,0:T(8,128)(2,1)S(1)} collective-permute-done((bf16[1,96,1024]{2,1,0:T(8,128)(2,1)S(1)}, bf16[1,96,1024]{2,1,0:T(8,128)(2,1)S(1)}, u32[]{:S(2)}, u32[]{:S(2)}) %collective-permute-start.9) | collective-permute-done | bytes 196640 | tf_op jit(solution)/shard_map/ppermute | solution.py:60
  127.6 0.6 multiply_convert_fusion.3
  128.3 0.2 broadcast.33.clone.2
  128.5 0.1 fusion.31
  128.6 3.8 %collective-permute-start.16 = (bf16[2,96,1024]{2,1,0:T(8,128)(2,1)S(1)}, bf16[2,96,1024]{2,1,0:T(8,128)(2,1)S(1)}, u32[]{:S(2)}, u32[]{:S(2)}) collective-permute-start(bf16[2,96,1024]{2,1,0:T(8,128)(2,1)S(1)} %pad_maximum_fusion.10), channel_id=1, source_target_pairs={{0,3},{1,0},{2,1},{3,2},{4,7},{5,4},{6,5},{7,6},{8,11},{9,8},{10,9... | collective-permute-start | bytes 1179656 | tf_op jit(solution)/shard_map/ppermute | solution.py:74
  132.5 3.2 %collective-permute-start.17 = (bf16[2,96,1024]{2,1,0:T(8,128)(2,1)S(1)}, bf16[2,96,1024]{2,1,0:T(8,128)(2,1)S(1)}, u32[]{:S(2)}, u32[]{:S(2)}) collective-permute-start(bf16[2,96,1024]{2,1,0:T(8,128)(2,1)S(1)} %pad_maximum_fusion.11), channel_id=1, source_target_pairs={{0,3},{1,0},{2,1},{3,2},{4,7},{5,4},{6,5},{7,6},{8,11},{9,8},{10,9... | collective-permute-start | bytes 1179656 | tf_op jit(solution)/shard_map/ppermute | solution.py:72
  135.7 0.3 fusion.35
  136.0 6.0 %collective-permute-done.14 = bf16[2,96,1024]{2,1,0:T(8,128)(2,1)S(1)} collective-permute-done((bf16[2,96,1024]{2,1,0:T(8,128)(2,1)S(1)}, bf16[2,96,1024]{2,1,0:T(8,128)(2,1)S(1)}, u32[]{:S(2)}, u32[]{:S(2)}) %collective-permute-start.14) | collective-permute-done | bytes 393248 | tf_op jit(solution)/shard_map/ppermute | solution.py:71
  142.0 2.0 collective-permute-start.24
  144.1 6.4 %collective-permute-done.15 = bf16[2,96,1024]{2,1,0:T(8,128)(2,1)S(1)} collective-permute-done((bf16[2,96,1024]{2,1,0:T(8,128)(2,1)S(1)}, bf16[2,96,1024]{2,1,0:T(8,128)(2,1)S(1)}, u32[]{:S(2)}, u32[]{:S(2)}) %collective-permute-start.15) | collective-permute-done | bytes 393248 | tf_op jit(solution)/shard_map/ppermute | solution.py:73
  150.5 1.0 collective-permute-start.18
  151.5 2.5 %collective-permute-start.19 = (bf16[2,96,1024]{2,1,0:T(8,128)(2,1)S(1)}, bf16[2,96,1024]{2,1,0:T(8,128)(2,1)S(1)}, u32[]{:S(2)}, u32[]{:S(2)}) collective-permute-start(bf16[2,96,1024]{2,1,0:T(8,128)(2,1)S(1)} %collective-permute-done.17), channel_id=1, source_target_pairs={{0,3},{1,0},{2,1},{3,2},{4,7},{5,4},{6,5},{7,6},{8,11},{9,8},{10,9... | collective-permute-start | bytes 1179656 | tf_op jit(solution)/shard_map/ppermute | solution.py:76
  154.1 5.3 %collective-permute-done.21 = bf16[1,96,1024]{2,1,0:T(8,128)(2,1)S(1)} collective-permute-done((bf16[1,96,1024]{2,1,0:T(8,128)(2,1)S(1)}, bf16[1,96,1024]{2,1,0:T(8,128)(2,1)S(1)}, u32[]{:S(2)}, u32[]{:S(2)}) %collective-permute-start.21) | collective-permute-done | bytes 196640 | tf_op jit(solution)/shard_map/ppermute | solution.py:71
  159.5 1.4 collective-permute-start.23
  160.9 0.6 collective-permute-start.25
  161.5 4.5 %collective-permute-done.18 = bf16[2,96,1024]{2,1,0:T(8,128)(2,1)S(1)} collective-permute-done((bf16[2,96,1024]{2,1,0:T(8,128)(2,1)S(1)}, bf16[2,96,1024]{2,1,0:T(8,128)(2,1)S(1)}, u32[]{:S(2)}, u32[]{:S(2)}) %collective-permute-start.18) | collective-permute-done | bytes 393248 | tf_op jit(solution)/shard_map/ppermute | solution.py:75
  166.0 1.7 collective-permute-start.26
  167.8 3.1 %fusion.51 = f32[768,1792]{1,0:T(8,128)S(1)} fusion(bf16[768,1024]{1,0:T(8,128)(2,1)S(1)} %get-tuple-element.37, bf16[1792,1024]{1,0:T(8,128)(2,1)S(1)} %copy-done.11), kind=kOutput, calls=%fused_computation.142 | convolution fusion | flops 2818572288 | bytes 10747904 | tf_op jit(solution)/shard_map/dot_general | solution.py:8
  170.9 3.1 %convolution_add_fusion = f32[768,1792]{1,0:T(8,128)S(1)} fusion(f32[768,1792]{1,0:T(8,128)S(1)} %fusion.51, bf16[768,1024]{1,0:T(8,128)(2,1)S(1)} %get-tuple-element.36, bf16[1792,1024]{1,0:T(8,128)(2,1)S(1)} %copy-done.12), kind=kOutput, calls=%fused_computation.3 | convolution fusion | flops 2819948544 | bytes 16252928 | tf_op jit(solution)/shard_map/dot_general | solution.py:8
  174.0 0.1 slice.175
  174.1 0.1 collective-permute-start.20
  174.4 2.9 %collective-permute-done.20 = bf16[384,1792]{1,0:T(8,128)(2,1)S(1)} collective-permute-done((bf16[384,1792]{1,0:T(8,128)(2,1)S(1)}, bf16[384,1792]{1,0:T(8,128)(2,1)S(1)}, u32[]{:S(2)}, u32[]{:S(2)}) %collective-permute-start.20) | collective-permute-done | bytes 1376288 | tf_op jit(solution)/shard_map/ppermute | solution.py:139
  177.3 1.4 fusion.1
  178.7 7.6 %all-to-all-start.2 = ((bf16[16,24,1792]{2,1,0:T(8,128)(2,1)}), bf16[16,24,1792]{2,1,0:T(8,128)(2,1)S(1)}, u32[]{:S(2)}, u32[]{:S(2)}) async-start(bf16[16,24,1792]{2,1,0:T(8,128)(2,1)} %bitcast.46), calls=%async_computation.2 | async-start | bytes 2752512 | tf_op jit(solution)/shard_map/all_to_all | solution.py:111
  186.3 7.2 %convolution_convert_fusion = bf16[1024,1792]{1,0:T(8,128)(2,1)} fusion(bf16[768,1024]{1,0:T(8,128)(2,1)} %copy-done.2, bf16[384,1792]{1,0:T(8,128)(2,1)} %copy-done.13, bf16[384,1792]{1,0:T(8,128)(2,1)} %bitcast.254), kind=kOutput, calls=%fused_computation | convolution fusion | flops 2825912320 | bytes 7995392 | tf_op jit(solution)/shard_map/dot_general | solution.py:8
  193.5 6.0 %convolution_convert_fusion.2 = bf16[1792,1024]{1,0:T(8,128)(2,1)} fusion(bf16[768,1024]{1,0:T(8,128)(2,1)S(1)} %get-tuple-element.36, bf16[384,1792]{1,0:T(8,128)(2,1)} %collective-permute-done.4, bf16[384,1792]{1,0:T(8,128)(2,1)S(1)} %bitcast.250), kind=kOutput, calls=%fused_computation.2 | convolution fusion | flops 2825912320 | bytes 7995392 | tf_op jit(solution)/shard_map/dot_general | solution.py:8
  199.5 5.9 %convolution_convert_fusion.1 = bf16[1792,1024]{1,0:T(8,128)(2,1)} fusion(bf16[768,1024]{1,0:T(8,128)(2,1)S(1)} %copy-done.4, bf16[384,1792]{1,0:T(8,128)(2,1)} %collective-permute-done.4, bf16[384,1792]{1,0:T(8,128)(2,1)S(1)} %bitcast.251), kind=kOutput, calls=%fused_computation.1 | convolution fusion | flops 2825912320 | bytes 7995392 | tf_op jit(solution)/shard_map/dot_general | solution.py:8
  205.4 0.9 all-to-all-done.2
  206.3 1.2 convolution_convert_fusion.4
  (80 shorter events, 1.3 us)
Async XLA Ops:
  0.6 2.2 %copy-start = (bf16[128,1792]{1,0:T(8,128)(2,1)S(1)}, bf16[128,1792]{1,0:T(8,128)(2,1)}, u32[]{:S(2)}) copy-start(bf16[128,1792]{1,0:T(8,128)(2,1)} %param.7) | copy-start | bytes 1376260
  4.4 7.6 %copy-start.9 = (f32[128,2]{0,1:T(2,128)S(1)}, f32[128,2]{0,1:T(2,128)}, u32[]{:S(2)}) copy-start(f32[128,2]{0,1:T(2,128)} %param.10) | copy-start | bytes 3076
  4.4 27.0 %copy-start.8 = (bf16[128,1792]{1,0:T(8,128)(2,1)S(1)}, bf16[128,1792]{1,0:T(8,128)(2,1)}, u32[]{:S(2)}) copy-start(bf16[128,1792]{1,0:T(8,128)(2,1)} %param.8) | copy-start | bytes 1376260
  4.4 26.9 %all-to-all-start.1 = ((bf16[16,24,1792]{2,1,0:T(8,128)(2,1)}), bf16[16,24,1792]{2,1,0:T(8,128)(2,1)S(1)}, u32[]{:S(2)}, u32[]{:S(2)}) async-start(bf16[16,24,1792]{2,1,0:T(8,128)(2,1)} %bitcast.7), calls=%async_computation.1 | async-start | bytes 2752512 | tf_op jit(solution)/shard_map/all_to_all | solution.py:111
  31.3 34.6 %copy-start.5 = (bf16[16,24,1792]{2,1,0:T(8,128)(2,1)}, bf16[16,24,1792]{2,1,0:T(8,128)(2,1)S(1)}, u32[]{:S(2)}) copy-start(bf16[16,24,1792]{2,1,0:T(8,128)(2,1)S(1)} %all-to-all-done.1) | copy-start | bytes 4128772
  31.3 28.6 %collective-permute-start.4 = (bf16[384,1792]{1,0:T(8,128)(2,1)S(1)}, bf16[384,1792]{1,0:T(8,128)(2,1)}, u32[]{:S(2)}, u32[]{:S(2)}) collective-permute-start(bf16[384,1792]{1,0:T(8,128)(2,1)S(1)} %bitcast.247), channel_id=1, source_target_pairs={{0,4},{4,0},{8,12},{12,8},{16,20},{20,16},{24,28},{28,24},{32,36},... | collective-permute-start | bytes 4128776 | tf_op jit(solution)/shard_map/ppermute | solution.py:124
  33.0 27.0 %all-to-all-start = ((bf16[16,24,1792]{2,1,0:T(8,128)(2,1)}), bf16[16,24,1792]{2,1,0:T(8,128)(2,1)S(1)}, u32[]{:S(2)}, u32[]{:S(2)}) async-start(bf16[16,24,1792]{2,1,0:T(8,128)(2,1)} %bitcast), calls=%async_computation | async-start | bytes 2752512 | tf_op jit(solution)/shard_map/all_to_all | solution.py:111
  59.9 15.2 %copy-start.7 = (bf16[16,24,1792]{2,1,0:T(8,128)(2,1)}, bf16[16,24,1792]{2,1,0:T(8,128)(2,1)S(1)}, u32[]{:S(2)}) copy-start(bf16[16,24,1792]{2,1,0:T(8,128)(2,1)S(1)} %all-to-all-done) | copy-start | bytes 4128772
  59.9 6.0 %copy-start.12 = (bf16[1792,1024]{1,0:T(8,128)(2,1)S(1)}, bf16[1792,1024]{1,0:T(8,128)(2,1)}, u32[]{:S(2)}) copy-start(bf16[1792,1024]{1,0:T(8,128)(2,1)} %param.11) | copy-start | bytes 11010052
  59.9 15.2 %collective-permute-start = (bf16[384,1792]{1,0:T(8,128)(2,1)S(1)}, bf16[384,1792]{1,0:T(8,128)(2,1)S(1)}, u32[]{:S(2)}, u32[]{:S(2)}) collective-permute-start(bf16[384,1792]{1,0:T(8,128)(2,1)S(1)} %bitcast.252), channel_id=1, source_target_pairs={{0,4},{4,0},{8,12},{12,8},{16,20},{20,16},{24,28},{28,24},{32,36},... | collective-permute-start | bytes 4128776 | tf_op jit(solution)/shard_map/ppermute | solution.py:125
  70.4 4.8 %copy-start.10 = (bf16[1024,1792]{1,0:T(8,128)(2,1)S(1)}, bf16[1024,1792]{1,0:T(8,128)(2,1)}, u32[]{:S(2)}) copy-start(bf16[1024,1792]{1,0:T(8,128)(2,1)} %param.13) | copy-start | bytes 11010052
  70.9 27.8 %collective-permute-start.7 = (bf16[2,96,1024]{2,1,0:T(8,128)(2,1)S(1)}, bf16[2,96,1024]{2,1,0:T(8,128)(2,1)S(1)}, u32[]{:S(2)}, u32[]{:S(2)}) collective-permute-start(bf16[2,96,1024]{2,1,0:T(8,128)(2,1)S(1)} %pad_maximum_fusion.7), channel_id=1, source_target_pairs={{0,3},{1,0},{2,1},{3,2},{4,7},{5,4},{6,5},{7,6},{8,11},{9,8},{10,9... | collective-permute-start | bytes 1179656 | tf_op jit(solution)/shard_map/ppermute | solution.py:56
  75.0 13.2 %collective-permute-start.5 = (bf16[2,96,1024]{2,1,0:T(8,128)(2,1)S(1)}, bf16[2,96,1024]{2,1,0:T(8,128)(2,1)S(1)}, u32[]{:S(2)}, u32[]{:S(2)}) collective-permute-start(bf16[2,96,1024]{2,1,0:T(8,128)(2,1)S(1)} %pad_maximum_fusion.6), channel_id=1, source_target_pairs={{0,1},{1,2},{2,3},{3,0},{4,5},{5,6},{6,7},{7,4},{8,9},{9,10},{10,1... | collective-permute-start | bytes 1179656 | tf_op jit(solution)/shard_map/ppermute | solution.py:53
  75.1 3.1 %copy-start.13 = (bf16[384,1792]{1,0:T(8,128)(2,1)}, bf16[384,1792]{1,0:T(8,128)(2,1)S(1)}, u32[]{:S(2)}) copy-start(bf16[384,1792]{1,0:T(8,128)(2,1)S(1)} %collective-permute-done) | copy-start | bytes 4128772
  78.2 31.2 %collective-permute-start.3 = (bf16[1,96,1024]{2,1,0:T(8,128)(2,1)S(1)}, bf16[1,96,1024]{2,1,0:T(8,128)(2,1)S(1)}, u32[]{:S(2)}, u32[]{:S(2)}) collective-permute-start(bf16[1,96,1024]{2,1,0:T(8,128)(2,1)S(1)} %get-tuple-element.32), channel_id=1, source_target_pairs={{0,3},{1,0},{2,1},{3,2},{4,7},{5,4},{6,5},{7,6},{8,11},{9,8},{10,9... | collective-permute-start | bytes 589832 | tf_op jit(solution)/shard_map/ppermute | solution.py:56
  81.5 10.9 %collective-permute-start.1 = (bf16[1,96,1024]{2,1,0:T(8,128)(2,1)S(1)}, bf16[1,96,1024]{2,1,0:T(8,128)(2,1)S(1)}, u32[]{:S(2)}, u32[]{:S(2)}) collective-permute-start(bf16[1,96,1024]{2,1,0:T(8,128)(2,1)S(1)} %get-tuple-element.31), channel_id=1, source_target_pairs={{0,1},{1,2},{2,3},{3,0},{4,5},{5,6},{6,7},{7,4},{8,9},{9,10},{10,1... | collective-permute-start | bytes 589832 | tf_op jit(solution)/shard_map/ppermute | solution.py:53
  81.6 35.3 %collective-permute-start.13 = (bf16[2,96,1024]{2,1,0:T(8,128)(2,1)S(1)}, bf16[2,96,1024]{2,1,0:T(8,128)(2,1)S(1)}, u32[]{:S(2)}, u32[]{:S(2)}) collective-permute-start(bf16[2,96,1024]{2,1,0:T(8,128)(2,1)S(1)} %pad_maximum_fusion.9), channel_id=1, source_target_pairs={{0,1},{1,2},{2,3},{3,0},{4,5},{5,6},{6,7},{7,4},{8,9},{9,10},{10,1... | collective-permute-start | bytes 1179656 | tf_op jit(solution)/shard_map/ppermute | solution.py:55
  88.2 10.3 %collective-permute-start.11 = (bf16[2,96,1024]{2,1,0:T(8,128)(2,1)S(1)}, bf16[2,96,1024]{2,1,0:T(8,128)(2,1)S(1)}, u32[]{:S(2)}, u32[]{:S(2)}) collective-permute-start(bf16[2,96,1024]{2,1,0:T(8,128)(2,1)S(1)} %pad_maximum_fusion.8), channel_id=1, source_target_pairs={{0,3},{1,0},{2,1},{3,2},{4,7},{5,4},{6,5},{7,6},{8,11},{9,8},{10,9... | collective-permute-start | bytes 1179656 | tf_op jit(solution)/shard_map/ppermute | solution.py:54
  92.4 16.9 %collective-permute-start.6 = (bf16[2,96,1024]{2,1,0:T(8,128)(2,1)S(1)}, bf16[2,96,1024]{2,1,0:T(8,128)(2,1)S(1)}, u32[]{:S(2)}, u32[]{:S(2)}) collective-permute-start(bf16[2,96,1024]{2,1,0:T(8,128)(2,1)S(1)} %add_convert_fusion.1), channel_id=1, source_target_pairs={{0,1},{1,2},{2,3},{3,0},{4,5},{5,6},{6,7},{7,4},{8,9},{9,10},{10,1... | collective-permute-start | bytes 1179656 | tf_op jit(solution)/shard_map/ppermute | solution.py:59
  98.5 14.6 %collective-permute-start.2 = (bf16[1,96,1024]{2,1,0:T(8,128)(2,1)S(1)}, bf16[1,96,1024]{2,1,0:T(8,128)(2,1)S(1)}, u32[]{:S(2)}, u32[]{:S(2)}) collective-permute-start(bf16[1,96,1024]{2,1,0:T(8,128)(2,1)S(1)} %fusion.7), channel_id=1, source_target_pairs={{0,1},{1,2},{2,3},{3,0},{4,5},{5,6},{6,7},{7,4},{8,9},{9,10},{10,1... | collective-permute-start | bytes 589832 | tf_op jit(solution)/shard_map/ppermute | solution.py:59
  98.7 18.2 %collective-permute-start.12 = (bf16[2,96,1024]{2,1,0:T(8,128)(2,1)S(1)}, bf16[2,96,1024]{2,1,0:T(8,128)(2,1)S(1)}, u32[]{:S(2)}, u32[]{:S(2)}) collective-permute-start(bf16[2,96,1024]{2,1,0:T(8,128)(2,1)S(1)} %add_convert_fusion), channel_id=1, source_target_pairs={{0,3},{1,0},{2,1},{3,2},{4,7},{5,4},{6,5},{7,6},{8,11},{9,8},{10,9... | collective-permute-start | bytes 1179656 | tf_op jit(solution)/shard_map/ppermute | solution.py:60
  113.5 11.2 %collective-permute-start.10 = (bf16[1,96,1024]{2,1,0:T(8,128)(2,1)S(1)}, bf16[1,96,1024]{2,1,0:T(8,128)(2,1)S(1)}, u32[]{:S(2)}, u32[]{:S(2)}) collective-permute-start(bf16[1,96,1024]{2,1,0:T(8,128)(2,1)S(1)} %get-tuple-element.11), channel_id=1, source_target_pairs={{0,1},{1,2},{2,3},{3,0},{4,5},{5,6},{6,7},{7,4},{8,9},{9,10},{10,1... | collective-permute-start | bytes 589832 | tf_op jit(solution)/shard_map/ppermute | solution.py:55
  113.6 7.0 %collective-permute-start.8 = (bf16[1,96,1024]{2,1,0:T(8,128)(2,1)S(1)}, bf16[1,96,1024]{2,1,0:T(8,128)(2,1)S(1)}, u32[]{:S(2)}, u32[]{:S(2)}) collective-permute-start(bf16[1,96,1024]{2,1,0:T(8,128)(2,1)S(1)} %get-tuple-element.12), channel_id=1, source_target_pairs={{0,3},{1,0},{2,1},{3,2},{4,7},{5,4},{6,5},{7,6},{8,11},{9,8},{10,9... | collective-permute-start | bytes 589832 | tf_op jit(solution)/shard_map/ppermute | solution.py:54
  120.6 6.9 %collective-permute-start.9 = (bf16[1,96,1024]{2,1,0:T(8,128)(2,1)S(1)}, bf16[1,96,1024]{2,1,0:T(8,128)(2,1)S(1)}, u32[]{:S(2)}, u32[]{:S(2)}) collective-permute-start(bf16[1,96,1024]{2,1,0:T(8,128)(2,1)S(1)} %fusion.5), channel_id=1, source_target_pairs={{0,3},{1,0},{2,1},{3,2},{4,7},{5,4},{6,5},{7,6},{8,11},{9,8},{10,9... | collective-permute-start | bytes 589832 | tf_op jit(solution)/shard_map/ppermute | solution.py:60
  128.2 13.8 %collective-permute-start.14 = (bf16[2,96,1024]{2,1,0:T(8,128)(2,1)S(1)}, bf16[2,96,1024]{2,1,0:T(8,128)(2,1)S(1)}, u32[]{:S(2)}, u32[]{:S(2)}) collective-permute-start(bf16[2,96,1024]{2,1,0:T(8,128)(2,1)S(1)} %pad_maximum_fusion.10), channel_id=1, source_target_pairs={{0,1},{1,2},{2,3},{3,0},{4,5},{5,6},{6,7},{7,4},{8,9},{9,10},{10,1... | collective-permute-start | bytes 1179656 | tf_op jit(solution)/shard_map/ppermute | solution.py:71
  128.6 21.9 %collective-permute-start.16 = (bf16[2,96,1024]{2,1,0:T(8,128)(2,1)S(1)}, bf16[2,96,1024]{2,1,0:T(8,128)(2,1)S(1)}, u32[]{:S(2)}, u32[]{:S(2)}) collective-permute-start(bf16[2,96,1024]{2,1,0:T(8,128)(2,1)S(1)} %pad_maximum_fusion.10), channel_id=1, source_target_pairs={{0,3},{1,0},{2,1},{3,2},{4,7},{5,4},{6,5},{7,6},{8,11},{9,8},{10,9... | collective-permute-start | bytes 1179656 | tf_op jit(solution)/shard_map/ppermute | solution.py:74
  132.4 18.0 %collective-permute-start.15 = (bf16[2,96,1024]{2,1,0:T(8,128)(2,1)S(1)}, bf16[2,96,1024]{2,1,0:T(8,128)(2,1)S(1)}, u32[]{:S(2)}, u32[]{:S(2)}) collective-permute-start(bf16[2,96,1024]{2,1,0:T(8,128)(2,1)S(1)} %pad_maximum_fusion.11), channel_id=1, source_target_pairs={{0,1},{1,2},{2,3},{3,0},{4,5},{5,6},{6,7},{7,4},{8,9},{9,10},{10,1... | collective-permute-start | bytes 1179656 | tf_op jit(solution)/shard_map/ppermute | solution.py:73
  132.5 19.0 %collective-permute-start.17 = (bf16[2,96,1024]{2,1,0:T(8,128)(2,1)S(1)}, bf16[2,96,1024]{2,1,0:T(8,128)(2,1)S(1)}, u32[]{:S(2)}, u32[]{:S(2)}) collective-permute-start(bf16[2,96,1024]{2,1,0:T(8,128)(2,1)S(1)} %pad_maximum_fusion.11), channel_id=1, source_target_pairs={{0,3},{1,0},{2,1},{3,2},{4,7},{5,4},{6,5},{7,6},{8,11},{9,8},{10,9... | collective-permute-start | bytes 1179656 | tf_op jit(solution)/shard_map/ppermute | solution.py:72
  135.7 38.5 %collective-permute-start.22 = (bf16[1,96,1024]{2,1,0:T(8,128)(2,1)S(1)}, bf16[1,96,1024]{2,1,0:T(8,128)(2,1)S(1)}, u32[]{:S(2)}, u32[]{:S(2)}) collective-permute-start(bf16[1,96,1024]{2,1,0:T(8,128)(2,1)S(1)} %get-tuple-element.34), channel_id=1, source_target_pairs={{0,1},{1,2},{2,3},{3,0},{4,5},{5,6},{6,7},{7,4},{8,9},{9,10},{10,1... | collective-permute-start | bytes 589832 | tf_op jit(solution)/shard_map/ppermute | solution.py:73
  142.0 18.9 %collective-permute-start.24 = (bf16[1,96,1024]{2,1,0:T(8,128)(2,1)S(1)}, bf16[1,96,1024]{2,1,0:T(8,128)(2,1)S(1)}, u32[]{:S(2)}, u32[]{:S(2)}) collective-permute-start(bf16[1,96,1024]{2,1,0:T(8,128)(2,1)S(1)} %get-tuple-element.34), channel_id=1, source_target_pairs={{0,3},{1,0},{2,1},{3,2},{4,7},{5,4},{6,5},{7,6},{8,11},{9,8},{10,9... | collective-permute-start | bytes 589832 | tf_op jit(solution)/shard_map/ppermute | solution.py:72
  150.4 9.1 %collective-permute-start.21 = (bf16[1,96,1024]{2,1,0:T(8,128)(2,1)S(1)}, bf16[1,96,1024]{2,1,0:T(8,128)(2,1)S(1)}, u32[]{:S(2)}, u32[]{:S(2)}) collective-permute-start(bf16[1,96,1024]{2,1,0:T(8,128)(2,1)S(1)} %get-tuple-element.33), channel_id=1, source_target_pairs={{0,1},{1,2},{2,3},{3,0},{4,5},{5,6},{6,7},{7,4},{8,9},{9,10},{10,1... | collective-permute-start | bytes 589832 | tf_op jit(solution)/shard_map/ppermute | solution.py:71
  150.4 17.4 %copy-start.11 = (bf16[1792,1024]{1,0:T(8,128)(2,1)S(1)}, bf16[1792,1024]{1,0:T(8,128)(2,1)}, u32[]{:S(2)}) copy-start(bf16[1792,1024]{1,0:T(8,128)(2,1)} %param.12) | copy-start | bytes 11010052
  150.5 15.5 %collective-permute-start.18 = (bf16[2,96,1024]{2,1,0:T(8,128)(2,1)S(1)}, bf16[2,96,1024]{2,1,0:T(8,128)(2,1)S(1)}, u32[]{:S(2)}, u32[]{:S(2)}) collective-permute-start(bf16[2,96,1024]{2,1,0:T(8,128)(2,1)S(1)} %collective-permute-done.14), channel_id=1, source_target_pairs={{0,1},{1,2},{2,3},{3,0},{4,5},{5,6},{6,7},{7,4},{8,9},{9,10},{10,1... | collective-permute-start | bytes 1179656 | tf_op jit(solution)/shard_map/ppermute | solution.py:75
  151.5 16.2 %collective-permute-start.19 = (bf16[2,96,1024]{2,1,0:T(8,128)(2,1)S(1)}, bf16[2,96,1024]{2,1,0:T(8,128)(2,1)S(1)}, u32[]{:S(2)}, u32[]{:S(2)}) collective-permute-start(bf16[2,96,1024]{2,1,0:T(8,128)(2,1)S(1)} %collective-permute-done.17), channel_id=1, source_target_pairs={{0,3},{1,0},{2,1},{3,2},{4,7},{5,4},{6,5},{7,6},{8,11},{9,8},{10,9... | collective-permute-start | bytes 1179656 | tf_op jit(solution)/shard_map/ppermute | solution.py:76
  159.5 14.8 %collective-permute-start.23 = (bf16[1,96,1024]{2,1,0:T(8,128)(2,1)S(1)}, bf16[1,96,1024]{2,1,0:T(8,128)(2,1)S(1)}, u32[]{:S(2)}, u32[]{:S(2)}) collective-permute-start(bf16[1,96,1024]{2,1,0:T(8,128)(2,1)S(1)} %get-tuple-element.33), channel_id=1, source_target_pairs={{0,3},{1,0},{2,1},{3,2},{4,7},{5,4},{6,5},{7,6},{8,11},{9,8},{10,9... | collective-permute-start | bytes 589832 | tf_op jit(solution)/shard_map/ppermute | solution.py:74
  160.9 13.5 %collective-permute-start.25 = (bf16[1,96,1024]{2,1,0:T(8,128)(2,1)S(1)}, bf16[1,96,1024]{2,1,0:T(8,128)(2,1)S(1)}, u32[]{:S(2)}, u32[]{:S(2)}) collective-permute-start(bf16[1,96,1024]{2,1,0:T(8,128)(2,1)S(1)} %collective-permute-done.21), channel_id=1, source_target_pairs={{0,1},{1,2},{2,3},{3,0},{4,5},{5,6},{6,7},{7,4},{8,9},{9,10},{10,1... | collective-permute-start | bytes 589832 | tf_op jit(solution)/shard_map/ppermute | solution.py:75
  166.0 8.4 %collective-permute-start.26 = (bf16[1,96,1024]{2,1,0:T(8,128)(2,1)S(1)}, bf16[1,96,1024]{2,1,0:T(8,128)(2,1)S(1)}, u32[]{:S(2)}, u32[]{:S(2)}) collective-permute-start(bf16[1,96,1024]{2,1,0:T(8,128)(2,1)S(1)} %collective-permute-done.24), channel_id=1, source_target_pairs={{0,3},{1,0},{2,1},{3,2},{4,7},{5,4},{6,5},{7,6},{8,11},{9,8},{10,9... | collective-permute-start | bytes 589832 | tf_op jit(solution)/shard_map/ppermute | solution.py:76
  167.8 3.1 %copy-start.3 = (bf16[768,1024]{1,0:T(8,128)(2,1)}, bf16[768,1024]{1,0:T(8,128)(2,1)S(1)}, u32[]{:S(2)}) copy-start(bf16[768,1024]{1,0:T(8,128)(2,1)S(1)} %get-tuple-element.37) | copy-start | bytes 4718596
  174.1 3.2 %collective-permute-start.20 = (bf16[384,1792]{1,0:T(8,128)(2,1)S(1)}, bf16[384,1792]{1,0:T(8,128)(2,1)S(1)}, u32[]{:S(2)}, u32[]{:S(2)}) collective-permute-start(bf16[384,1792]{1,0:T(8,128)(2,1)S(1)} %slice.175), channel_id=1, source_target_pairs={{0,4},{4,0},{8,12},{12,8},{16,20},{20,16},{24,28},{28,24},{32,36},... | collective-permute-start | bytes 4128776 | tf_op jit(solution)/shard_map/ppermute | solution.py:139
  174.4 4.3 %copy-start.2 = (bf16[768,1024]{1,0:T(8,128)(2,1)}, bf16[768,1024]{1,0:T(8,128)(2,1)S(1)}, u32[]{:S(2)}) copy-start(bf16[768,1024]{1,0:T(8,128)(2,1)S(1)} %bitcast_dynamic-update-slice_fusion) | copy-start | bytes 4718596
  178.7 27.6 %all-to-all-start.2 = ((bf16[16,24,1792]{2,1,0:T(8,128)(2,1)}), bf16[16,24,1792]{2,1,0:T(8,128)(2,1)S(1)}, u32[]{:S(2)}, u32[]{:S(2)}) async-start(bf16[16,24,1792]{2,1,0:T(8,128)(2,1)} %bitcast.46), calls=%async_computation.2 | async-start | bytes 2752512 | tf_op jit(solution)/shard_map/all_to_all | solution.py:111
  186.3 7.3 %copy-start.6 = (bf16[16,24,1792]{2,1,0:T(8,128)(2,1)S(1)}, bf16[16,24,1792]{2,1,0:T(8,128)(2,1)}, u32[]{:S(2)}) copy-start(bf16[16,24,1792]{2,1,0:T(8,128)(2,1)} %copy-done.5) | copy-start | bytes 4128772
  193.5 6.0 %copy-start.4 = (bf16[768,1024]{1,0:T(8,128)(2,1)S(1)}, bf16[768,1024]{1,0:T(8,128)(2,1)}, u32[]{:S(2)}) copy-start(bf16[768,1024]{1,0:T(8,128)(2,1)} %copy-done.3) | copy-start | bytes 4718596
  199.5 8.1 %copy-start.1 = (bf16[128,1792]{1,0:T(8,128)(2,1)S(1)}, bf16[128,1792]{1,0:T(8,128)(2,1)}, u32[]{:S(2)}) copy-start(bf16[128,1792]{1,0:T(8,128)(2,1)} %param.7) | copy-start | bytes 1376260

commit v2 on v0

v2 whole, which is shorter than its diff:
```python
import jax
import jax.numpy as jnp
from jax import lax
from jax.sharding import PartitionSpec as P


def contract(first_arr, second_arr, first_dim, second_dim, kind=jnp.float32):
    return lax.dot_general(
        first_arr,
        second_arr,
        (((first_dim,), (second_dim,)), ((), ())),
        preferred_element_type=jnp.float32,
    ).astype(kind)


def swiglu_backward(gate_sum, up_sum, back_sum):
    sigma = jax.nn.sigmoid(gate_sum)
    active = gate_sum * sigma
    hidden = (active * up_sum).astype(jnp.bfloat16)
    d_up = (back_sum * active).astype(jnp.bfloat16)
    d_gate = (back_sum * up_sum * sigma * (1.0 + gate_sum * (1.0 - sigma))).astype(jnp.bfloat16)
    return (hidden, d_gate, d_up)


def slot_places(routing, expert_count, capacity):
    flat_ids = routing.reshape(-1)
    count = flat_ids.shape[0]
    onehot = flat_ids[:, None] == jnp.arange(expert_count, dtype=jnp.int32)[None, :]
    places = jnp.arange(count, dtype=jnp.int32)
    earlier = (places[None, :] < places[:, None]).astype(jnp.bfloat16)
    before = contract(earlier, onehot.astype(jnp.bfloat16), 1, 0)
    position = jnp.sum(jnp.where(onehot, before, 0.0), axis=1).astype(jnp.int32)
    return (flat_ids * capacity + position).reshape(routing.shape)


def after(array, *earlier):
    return lax.optimization_barrier((array,) + earlier)[0]


def ring_pairs(size, shift):
    return [(i, (i + shift) % size) for i in range(size)]


def wide(array):
    return array.astype(jnp.float32)


class Ring:
    def __init__(self, axis):
        self.axis = axis
        self.size = lax.axis_size(axis)
        self.me = lax.axis_index(axis)

    def up(self, array):
        return lax.ppermute(array, self.axis, [(i, (i + 1) % self.size) for i in range(self.size)])

    def down(self, array):
        return lax.ppermute(array, self.axis, [(i, (i - 1) % self.size) for i in range(self.size)])

    def place(self, offset, rows):
        return ((self.me + offset) % self.size) * rows

    def scatter(self, arrays):
        rows = arrays[0].shape[0] // 2
        block = rows // self.size

        def part(offset, which):
            start = which * rows + self.place(offset, block)
            return jnp.stack([lax.dynamic_slice_in_dim(a, start, block, axis=0) for a in arrays])

        far_own = self.up(part(2, 0))
        far_other = self.down(part(2, 1))
        to_right = [wide(part(1, 0)) + wide(far_own), wide(part(1, 1))]
        to_left = [wide(part(3, 0)), wide(part(3, 1)) + wide(far_other)]
        from_left = self.up(jnp.stack(to_right, axis=1).astype(jnp.bfloat16))
        from_right = self.down(jnp.stack(to_left, axis=1).astype(jnp.bfloat16))
        mine = jnp.stack([part(0, 0), part(0, 1)], axis=1)
        return wide(mine) + wide(from_left) + wide(from_right), (far_own, far_other)

    def assemble(self, pieces, i):
        block = pieces[0].shape[1]
        full = jnp.zeros((block * self.size,) + pieces[0].shape[2:], pieces[0].dtype)
        for offset, rows in zip((0, 3, 1, 2), pieces):
            full = lax.dynamic_update_slice_in_dim(full, rows[i], self.place(offset, block), axis=0)
        return full


def body(tokens, grad_out, routing, route_weight, gate_weight, up_weight, down_weight):
    owners = lax.axis_size("expert")
    experts = owners // 2
    tok_rows, width = tokens.shape
    top_routes = routing.shape[1]
    capacity = 4 * ((3 * tok_rows * top_routes // (2 * experts) + 3) // 4)
    ring = Ring("dp")
    same_core = [[2 * chip + core for chip in range(experts)] for core in range(2)]
    other_core = [(i, i ^ 1) for i in range(owners)]

    def exchange(rows):
        return lax.all_to_all(
            rows.reshape(experts, -1, width),
            "expert",
            split_axis=0,
            concat_axis=0,
            axis_index_groups=same_core,
            tiled=True,
        ).reshape(rows.shape)

    def swap_cores(rows):
        return lax.ppermute(rows, "expert", other_core)

    slot_index = slot_places(routing, experts, capacity)
    ids = jnp.arange(experts * capacity, dtype=jnp.int32)
    match = ids[:, None, None] == slot_index[None]
    choose = jnp.any(match, axis=2).astype(jnp.bfloat16)
    slot_weight = jnp.sum(jnp.where(match, route_weight[None], 0.0), axis=(1, 2))

    x_own = exchange(contract(choose, tokens, 1, 0, jnp.bfloat16))
    x_rows = jnp.concatenate([x_own, swap_cores(x_own)])
    g_slots = (contract(choose, grad_out, 1, 0) * slot_weight[:, None]).astype(jnp.bfloat16)
    g_own = exchange(after(g_slots, x_own))
    part_gate = contract(x_rows, gate_weight, 1, 0, jnp.bfloat16)
    part_up = contract(x_rows, up_weight, 1, 0, jnp.bfloat16)
    gate_up, mark = ring.scatter((part_gate, part_up))
    g_own = after(g_own, *mark)
    g_rows = jnp.concatenate([g_own, swap_cores(g_own)])
    back, _ = ring.scatter((contract(g_rows, down_weight, 1, 1, jnp.bfloat16),))
    hidden, d_gate, d_up = swiglu_backward(gate_up[0], gate_up[1], back[0])

    mine = jnp.stack([d_gate, d_up])
    left_other, right_other = ring.up(mine[:, 1]), ring.down(mine[:, 1])
    mine_own = after(mine[:, 0], left_other, right_other)
    left_own = ring.up(mine_own)
    far_other = ring.down(right_other)
    right_own = ring.down(after(mine_own, far_other))
    far_own = ring.up(left_own)

    def input_grad(pieces):
        cots = ring.assemble(pieces, 0), ring.assemble(pieces, 1)
        return cots, contract(cots[0], gate_weight, 1, 1) + contract(cots[1], up_weight, 1, 1)

    cots_other, rows_other = input_grad((mine[:, 1], left_other, right_other, far_other))
    from_other = swap_cores(rows_other.astype(jnp.bfloat16))
    cots_own, rows_own = input_grad(
        (mine_own, left_own, after(right_own, rows_other), after(far_own, rows_other))
    )
    total = (rows_own + wide(from_other)).astype(jnp.bfloat16)
    returned = exchange(total)
    hid_mine = after(hidden, total)
    hid_left, hid_right = ring.up(hid_mine), ring.down(hid_mine)
    hid_far_own, hid_far_other = ring.up(hid_left[0]), ring.down(hid_right[1])
    hidden = jnp.concatenate(
        [
            ring.assemble([p[None] for p in (hid_mine[i], hid_left[i], hid_right[i], far)], 0)
            for i, far in enumerate((hid_far_own, hid_far_other))
        ]
    )
    d_gate, d_up = [after(jnp.concatenate(pair), total) for pair in zip(cots_own, cots_other)]
    grad_gate = contract(x_rows, d_gate, 0, 0, jnp.bfloat16)
    grad_up = contract(x_rows, d_up, 0, 0, jnp.bfloat16)
    grad_down = contract(hidden, g_rows, 0, 0, jnp.bfloat16)
    grad_tokens = contract(choose, returned, 0, 0, jnp.bfloat16)
    return (grad_tokens, grad_gate, grad_up, grad_down)


def solution(mesh):
    placed = (
        P("expert", "dp"),
        P("expert", "dp"),
        P("expert", None),
        P("expert", None),
        P("dp", "expert"),
        P("dp", "expert"),
        P("expert", "dp"),
    )
    return jax.shard_map(
        body,
        mesh=mesh,
        in_specs=placed,
        out_specs=(P("expert", "dp"), P("dp", "expert"), P("dp", "expert"), P("expert", "dp")),
        check_vma=False,
    )
```

time: 423 us -> 187 us (0.44)
  waiting for transfers between devices: 197 us -> 61.5 us
  local copies, waits for them, and re-layouts: 73.2 us -> 10.6 us
  blocking collectives: 71.3 us -> 26.6 us
  starting transfers between devices: 7.46 us -> 36.9 us
  between operations: 14.3 us -> 1.26 us
  other arithmetic: 17.2 us -> 8.6 us
    psum x1 -> x0, waiting for transfers between devices: 179 us -> none  [body(): gate_sum, up_sum, back_sum = lax.psum((part_gate, part_up, part_back), 'dp')]
    scatter x2 -> x0, local copies, waits for them, and re-layouts: 63 us -> none  [body(): blank_rows.at[0, slot_index].set(tokens[source]).at[1, slot_index]]
    ppermute x0 -> x21, waiting for transfers between devices: none -> 56.1 us  [the longest x9 33.8 us: down(): lax.ppermute(array, self.axis, [(i, (i - 1) % self.size) for i in range(s...]
    all_to_all x1, blocking collectives: 71.3 us -> 26.6 us  [exchange(): lax.all_to_all(rows.reshape(experts, -1, width), 'expert', split_axis=0,...]
    ppermute x0 -> x21, starting transfers between devices: none -> 24.6 us  [the longest x9 14.7 us: down(): lax.ppermute(array, self.axis, [(i, (i - 1) % self.size) for i in range(s...]
    all_to_all x1 -> x2, waiting for transfers between devices: 18.6 us -> 5.38 us  [exchange(): lax.all_to_all(rows.reshape(experts, -1, width), 'expert', split_axis=0,...]
    scatter-add x1 -> x0, other arithmetic: 6.93 us -> none  [body(): grad_tokens = jnp.zeros((tok_rows, feat_width), jnp.float32).at[source].a...]
    all_to_all x1 -> x2, starting transfers between devices: 7.42 us -> 12.2 us  [exchange(): lax.all_to_all(rows.reshape(experts, -1, width), 'expert', split_axis=0,...]
  transfers between devices with their start and end apart: 2 -> 23, of which waited for: 2 -> 11; matrix products, arithmetic and copies ran while one was open for 4% -> 28% of each run, Pallas kernels for 0% -> 0%
where the time goes in v2:
time: 187 us; the launch traced here: 186 us
  waiting for transfers between devices  61.5 us (33%)
  matrix products  40.6 us (22%)
  starting transfers between devices  36.9 us (20%)
  blocking collectives  26.6 us (14%)
  local copies, waits for them, and re-layouts  10.6 us (6%)
  other arithmetic  8.6 us (5%)
    dot_general x14, matrix products, contract(): lax.dot_general(first_arr, second_arr, (((first_dim,), (second_dim,)), ((...  40.6 us
    ppermute x9, waiting for transfers between devices, down(): lax.ppermute(array, self.axis, [(i, (i - 1) % self.size) for i in range(s...  33.8 us
    all_to_all x1, blocking collectives, exchange(): lax.all_to_all(rows.reshape(experts, -1, width), 'expert', split_axis=0,...  26.6 us
    ppermute x9, waiting for transfers between devices, up(): lax.ppermute(array, self.axis, [(i, (i + 1) % self.size) for i in range(s...  22.3 us
    ppermute x9, starting transfers between devices, down(): lax.ppermute(array, self.axis, [(i, (i - 1) % self.size) for i in range(s...  14.7 us
    all_to_all x2, starting transfers between devices, exchange(): lax.all_to_all(rows.reshape(experts, -1, width), 'expert', split_axis=0,...  12.2 us
    ppermute x9, starting transfers between devices, up(): lax.ppermute(array, self.axis, [(i, (i + 1) % self.size) for i in range(s...  9.83 us
    all_to_all x2, waiting for transfers between devices, exchange(): lax.all_to_all(rows.reshape(experts, -1, width), 'expert', split_axis=0,...  5.38 us
  transfers between devices with their start and end apart: 23, of which 11 were waited for; matrix products, arithmetic and copies ran while one was open for 28% of the time, Pallas kernels for 0%

profile of v2, /device:TPU:2, one launch (start us, length us, event | category | flops | bytes accessed | tf_op | source)
XLA Modules:
  0.0 186.0 jit_solution(7195091843903900502)
XLA Ops:
  0.7 0.9 copy.21
  1.5 0.1 eq.70
  1.7 0.2 fusion.4
  1.9 0.1 convert_element_type.155
  2.1 0.7 multiply_add_fusion
  2.9 0.5 convolution_convert_fusion.3
  3.4 26.6 %all_to_all.15 = bf16[16,24,1792]{2,1,0:T(8,128)(2,1)S(1)} all-to-all(bf16[16,24,1792]{2,1,0:T(8,128)(2,1)S(1)} %bitcast.185), channel_id=1, replica_groups={{0,8,16,24,32,40,48,56,64,72,80,88,96,104,112,120},{4,12,20,28,36,44,52..., dimensions={0} | all-to-all | bytes 2752512 | tf_op jit(solution)/shard_map/all_to_all | solution.py:99
  29.9 0.1 select_reduce_fusion
  30.1 1.6 fusion
  31.7 5.0 %all-to-all-start.1 = ((bf16[16,24,1792]{2,1,0:T(8,128)(2,1)}), bf16[16,24,1792]{2,1,0:T(8,128)(2,1)S(1)}, u32[]{:S(2)}, u32[]{:S(2)}) async-start(bf16[16,24,1792]{2,1,0:T(8,128)(2,1)} %bitcast.2), calls=%async_computation.1 | async-start | bytes 2752512 | tf_op jit(solution)/shard_map/all_to_all | solution.py:99
  36.7 5.6 %convolution_convert_fusion.6 = bf16[768,1024]{1,0:T(8,128)(2,1)S(1)} fusion(bf16[1792,1024]{1,0:T(8,128)(2,1)} %param.12, bf16[384,1792]{1,0:T(8,128)(2,1)} %collective-permute-done, bf16[384,1792]{1,0:T(8,128)(2,1)S(1)} %bitcast.187), kind=kOutput, calls=%fused_computation.12 | convolution fusion | flops 2824863744 | bytes 7995392 | tf_op jit(solution)/shard_map/dot_general | solution.py:8
  42.3 4.3 %convolution_convert_fusion.7 = bf16[768,1024]{1,0:T(8,128)(2,1)S(1)} fusion(bf16[1792,1024]{1,0:T(8,128)(2,1)S(1)} %copy-done.16, bf16[384,1792]{1,0:T(8,128)(2,1)} %collective-permute-done, bf16[384,1792]{1,0:T(8,128)(2,1)S(1)} %bitcast.188), kind=kOutput, calls=%fused_computation.13 | convolution fusion | flops 2824863744 | bytes 7995392 | tf_op jit(solution)/shard_map/dot_general | solution.py:8
  46.7 1.3 dynamic-slice_bitcast_fusion.10
  48.0 2.0 %collective-permute-start.1 = (bf16[2,96,1024]{2,1,0:T(8,128)(2,1)S(1)}, bf16[2,96,1024]{2,1,0:T(8,128)(2,1)S(1)}, u32[]{:S(2)}, u32[]{:S(2)}) collective-permute-start(bf16[2,96,1024]{2,1,0:T(8,128)(2,1)S(1)} %pad_maximum_fusion.5), channel_id=1, source_target_pairs={{0,1},{1,2},{2,3},{3,0},{4,5},{5,6},{6,7},{7,4},{8,9},{9,10},{10,1... | collective-permute-start | bytes 1179656 | tf_op jit(solution)/shard_map/ppermute | solution.py:55
  50.1 2.2 %collective-permute-start.2 = (bf16[2,96,1024]{2,1,0:T(8,128)(2,1)S(1)}, bf16[2,96,1024]{2,1,0:T(8,128)(2,1)}, u32[]{:S(2)}, u32[]{:S(2)}) collective-permute-start(bf16[2,96,1024]{2,1,0:T(8,128)(2,1)S(1)} %pad_maximum_fusion.6), channel_id=1, source_target_pairs={{0,3},{1,0},{2,1},{3,2},{4,7},{5,4},{6,5},{7,6},{8,11},{9,8},{10,9... | collective-permute-start | bytes 1179656 | tf_op jit(solution)/shard_map/ppermute | solution.py:58
  52.3 5.4 %all-to-all-done.1 = bf16[16,24,1792]{2,1,0:T(8,128)(2,1)S(1)} async-done(((bf16[16,24,1792]{2,1,0:T(8,128)(2,1)}), bf16[16,24,1792]{2,1,0:T(8,128)(2,1)S(1)}, u32[]{:S(2)}, u32[]{:S(2)}) %all-to-all-start.1) | async-done | bytes 1376288 | tf_op jit(solution)/shard_map/all_to_all | solution.py:99
  57.6 4.0 %collective-permute-done.1 = bf16[2,96,1024]{2,1,0:T(8,128)(2,1)S(1)} collective-permute-done((bf16[2,96,1024]{2,1,0:T(8,128)(2,1)S(1)}, bf16[2,96,1024]{2,1,0:T(8,128)(2,1)S(1)}, u32[]{:S(2)}, u32[]{:S(2)}) %collective-permute-start.1) | collective-permute-done | bytes 393248 | tf_op jit(solution)/shard_map/ppermute | solution.py:55
  61.6 0.7 copy-done.12
  62.4 1.3 fusion.10
  63.7 1.1 pad_maximum_fusion.3
  64.8 2.5 %collective-permute-start.9 = (bf16[2,2,96,1024]{3,2,1,0:T(8,128)(2,1)S(1)}, bf16[2,2,96,1024]{3,2,1,0:T(8,128)(2,1)S(1)}, u32[]{:S(2)}, u32[]{:S(2)}) collective-permute-start(bf16[2,2,96,1024]{3,2,1,0:T(8,128)(2,1)S(1)} %pad_maximum_fusion.3), channel_id=1, source_target_pairs={{0,3},{1,0},{2,1},{3,2},{4,7},{5,4},{6,5},{7,6},{8,11},{9,8},{10,9... | collective-permute-start | bytes 2359304 | tf_op jit(solution)/shard_map/ppermute | solution.py:58
  67.9 1.7 copy-done.15
  69.6 3.0 %convolution_convert_fusion.5 = bf16[768,1024]{1,0:T(8,128)(2,1)S(1)} fusion(bf16[768,1792]{1,0:T(8,128)(2,1)S(1)} %constant_dynamic-update-slice_fusion.4, bf16[1024,1792]{1,0:T(8,128)(2,1)S(1)} %copy-done.15), kind=kOutput, calls=%fused_computation.11 | convolution fusion | flops 2819358720 | bytes 7995392 | tf_op jit(solution)/shard_map/dot_general | solution.py:8
  72.8 1.6 collective-permute-start.6
  74.4 0.5 collective-permute-start.4
  75.1 14.0 %collective-permute-done.6 = bf16[1,96,1024]{2,1,0:T(8,128)(2,1)S(1)} collective-permute-done((bf16[1,96,1024]{2,1,0:T(8,128)(2,1)S(1)}, bf16[1,96,1024]{2,1,0:T(8,128)(2,1)S(1)}, u32[]{:S(2)}, u32[]{:S(2)}) %collective-permute-start.6) | collective-permute-done | bytes 196640 | tf_op jit(solution)/shard_map/ppermute | solution.py:58
  89.1 3.7 %collective-permute-done.4 = bf16[1,96,1024]{2,1,0:T(8,128)(2,1)S(1)} collective-permute-done((bf16[1,96,1024]{2,1,0:T(8,128)(2,1)S(1)}, bf16[1,96,1024]{2,1,0:T(8,128)(2,1)S(1)}, u32[]{:S(2)}, u32[]{:S(2)}) %collective-permute-start.4) | collective-permute-done | bytes 196640 | tf_op jit(solution)/shard_map/ppermute | solution.py:55
  92.8 0.1 fusion.17
  92.9 0.3 collective-permute-start.7
  93.3 2.1 %collective-permute-start.5 = (bf16[1,2,96,1024]{3,2,1,0:T(8,128)(2,1)S(1)}, bf16[1,2,96,1024]{3,2,1,0:T(8,128)(2,1)S(1)}, u32[]{:S(2)}, u32[]{:S(2)}) collective-permute-start(bf16[1,2,96,1024]{3,2,1,0:T(8,128)(2,1)S(1)} %pad_maximum_fusion.8), channel_id=1, source_target_pairs={{0,1},{1,2},{2,3},{3,0},{4,5},{5,6},{6,7},{7,4},{8,9},{9,10},{10,1... | collective-permute-start | bytes 1179656 | tf_op jit(solution)/shard_map/ppermute | solution.py:55
  95.3 0.4 convert_add_fusion
  95.7 1.0 fusion.5
  96.7 6.9 %collective-permute-done.7 = bf16[1,2,96,1024]{3,2,1,0:T(8,128)(2,1)S(1)} collective-permute-done((bf16[1,2,96,1024]{3,2,1,0:T(8,128)(2,1)S(1)}, bf16[1,2,96,1024]{3,2,1,0:T(8,128)(2,1)S(1)}, u32[]{:S(2)}, u32[]{:S(2)}) %collective-permute-start.7) | collective-permute-done | bytes 393248 | tf_op jit(solution)/shard_map/ppermute | solution.py:58
  103.6 1.3 collective-permute-done.5
  105.0 0.5 multiply_convert_fusion
  105.5 0.2 collective-permute-start.11
  105.8 1.9 %collective-permute-start.10 = (bf16[2,96,1024]{2,1,0:T(8,128)(2,1)S(1)}, bf16[2,96,1024]{2,1,0:T(8,128)(2,1)S(1)}, u32[]{:S(2)}, u32[]{:S(2)}) collective-permute-start(bf16[2,96,1024]{2,1,0:T(8,128)(2,1)S(1)} %get-tuple-element.48), channel_id=1, source_target_pairs={{0,1},{1,2},{2,3},{3,0},{4,5},{5,6},{6,7},{7,4},{8,9},{9,10},{10,1... | collective-permute-start | bytes 1179656 | tf_op jit(solution)/shard_map/ppermute | solution.py:55
  107.9 7.2 %collective-permute-done.11 = bf16[2,96,1024]{2,1,0:T(8,128)(2,1)S(1)} collective-permute-done((bf16[2,96,1024]{2,1,0:T(8,128)(2,1)S(1)}, bf16[2,96,1024]{2,1,0:T(8,128)(2,1)S(1)}, u32[]{:S(2)}, u32[]{:S(2)}) %collective-permute-start.11) | collective-permute-done | bytes 393248 | tf_op jit(solution)/shard_map/ppermute | solution.py:58
  115.1 1.4 collective-permute-done.10
  116.5 0.3 collective-permute-start.12
  117.0 3.0 %collective-permute-start.13 = (bf16[2,96,1024]{2,1,0:T(8,128)(2,1)S(1)}, bf16[2,96,1024]{2,1,0:T(8,128)(2,1)S(1)}, u32[]{:S(2)}, u32[]{:S(2)}) collective-permute-start(bf16[2,96,1024]{2,1,0:T(8,128)(2,1)S(1)} %collective-permute-done.11), channel_id=1, source_target_pairs={{0,3},{1,0},{2,1},{3,2},{4,7},{5,4},{6,5},{7,6},{8,11},{9,8},{10,9... | collective-permute-start | bytes 1179656 | tf_op jit(solution)/shard_map/ppermute | solution.py:58
  120.1 5.6 %collective-permute-done.13 = bf16[2,96,1024]{2,1,0:T(8,128)(2,1)S(1)} collective-permute-done((bf16[2,96,1024]{2,1,0:T(8,128)(2,1)S(1)}, bf16[2,96,1024]{2,1,0:T(8,128)(2,1)S(1)}, u32[]{:S(2)}, u32[]{:S(2)}) %collective-permute-start.13) | collective-permute-done | bytes 393248 | tf_op jit(solution)/shard_map/ppermute | solution.py:58
  125.8 3.7 %collective-permute-start.14 = (bf16[2,96,1024]{2,1,0:T(8,128)(2,1)S(1)}, bf16[2,96,1024]{2,1,0:T(8,128)(2,1)S(1)}, u32[]{:S(2)}, u32[]{:S(2)}) collective-permute-start(bf16[2,96,1024]{2,1,0:T(8,128)(2,1)S(1)} %get-tuple-element.16), channel_id=1, source_target_pairs={{0,3},{1,0},{2,1},{3,2},{4,7},{5,4},{6,5},{7,6},{8,11},{9,8},{10,9... | collective-permute-start | bytes 1179656 | tf_op jit(solution)/shard_map/ppermute | solution.py:58
  129.5 1.6 fusion.33
  131.2 0.3 copy-done.17
  131.6 1.6 convolution_add_fusion.1
  133.3 6.9 %collective-permute-done.15 = bf16[2,96,1024]{2,1,0:T(8,128)(2,1)S(1)} collective-permute-done((bf16[2,96,1024]{2,1,0:T(8,128)(2,1)S(1)}, bf16[2,96,1024]{2,1,0:T(8,128)(2,1)S(1)}, u32[]{:S(2)}, u32[]{:S(2)}) %collective-permute-start.15) | collective-permute-done | bytes 393248 | tf_op jit(solution)/shard_map/ppermute | solution.py:55
  140.4 1.3 pad_maximum_fusion.1
  141.7 1.6 fusion.34
  143.3 1.6 convolution_add_fusion
  145.0 1.3 add_convert_fusion
  146.3 2.0 %collective-permute-start.17 = (bf16[2,96,1024]{2,1,0:T(8,128)(2,1)}, bf16[2,96,1024]{2,1,0:T(8,128)(2,1)}, u32[]{:S(2)}, u32[]{:S(2)}) collective-permute-start(bf16[2,96,1024]{2,1,0:T(8,128)(2,1)} %fusion.5), channel_id=1, source_target_pairs={{0,1},{1,2},{2,3},{3,0},{4,5},{5,6},{6,7},{7,4},{8,9},{9,10},{10,1... | collective-permute-start | bytes 1179656 | tf_op jit(solution)/shard_map/ppermute | solution.py:55
  148.3 7.3 %all-to-all-start.2 = ((bf16[16,24,1792]{2,1,0:T(8,128)(2,1)}), bf16[16,24,1792]{2,1,0:T(8,128)(2,1)S(1)}, u32[]{:S(2)}, u32[]{:S(2)}) async-start(bf16[16,24,1792]{2,1,0:T(8,128)(2,1)} %bitcast.52), calls=%async_computation.2 | async-start | bytes 2752512 | tf_op jit(solution)/shard_map/all_to_all | solution.py:99
  155.6 7.2 %convolution_convert_fusion.2 = bf16[1792,1024]{1,0:T(8,128)(2,1)} fusion(bf16[768,1024]{1,0:T(8,128)(2,1)} %pad_maximum_fusion.1, bf16[384,1792]{1,0:T(8,128)(2,1)} %collective-permute-done, bf16[384,1792]{1,0:T(8,128)(2,1)} %bitcast.189), kind=kOutput, calls=%fused_computation.2 | convolution fusion | flops 2825912320 | bytes 7995392 | tf_op jit(solution)/shard_map/dot_general | solution.py:8
  162.9 5.9 %convolution_convert_fusion.1 = bf16[1792,1024]{1,0:T(8,128)(2,1)} fusion(bf16[768,1024]{1,0:T(8,128)(2,1)S(1)} %pad_maximum_fusion.2, bf16[384,1792]{1,0:T(8,128)(2,1)} %collective-permute-done, bf16[384,1792]{1,0:T(8,128)(2,1)S(1)} %bitcast.190), kind=kOutput, calls=%fused_computation.1 | convolution fusion | flops 2825912320 | bytes 7995392 | tf_op jit(solution)/shard_map/dot_general | solution.py:8
  168.8 1.1 bitcast_dynamic-update-slice_fusion
  170.0 0.9 bitcast_dynamic-update-slice_fusion.1
  171.0 1.3 collective-permute-start.20
  172.3 0.9 slice_bitcast_fusion.3
  173.2 0.9 collective-permute-start.19
  174.1 1.0 constant_dynamic-update-slice_fusion.3
  175.2 5.0 %collective-permute-done.19 = bf16[96,1024]{1,0:T(8,128)(2,1)S(1)} collective-permute-done((bf16[96,1024]{1,0:T(8,128)(2,1)S(1)}, bf16[96,1024]{1,0:T(8,128)(2,1)S(1)}, u32[]{:S(2)}, u32[]{:S(2)}) %collective-permute-start.19) | collective-permute-done | bytes 196640 | tf_op jit(solution)/shard_map/ppermute | solution.py:55
  180.3 4.5 %convolution_convert_fusion = bf16[1024,1792]{1,0:T(8,128)(2,1)} fusion(bf16[768,1792]{1,0:T(8,128)(2,1)S(1)} %copy-done.10, bf16[384,1024]{1,0:T(8,128)(2,1)S(1)} %constant_dynamic-update-slice_fusion, bf16[384,1024]{1,0:T(8,128)(2,1)S(1)} %constant_dynamic-update-slice_fusion.2), kind=kOutput, calls=%fused_computation | convolution fusion | flops 2823553024 | bytes 7995392 | tf_op jit(solution)/shard_map/dot_general | solution.py:8
  184.8 1.2 convolution_convert_fusion.4
  (89 shorter events, 2.3 us)
Async XLA Ops:
  0.6 2.2 %copy-start = (bf16[128,1792]{1,0:T(8,128)(2,1)S(1)}, bf16[128,1792]{1,0:T(8,128)(2,1)}, u32[]{:S(2)}) copy-start(bf16[128,1792]{1,0:T(8,128)(2,1)} %param.7) | copy-start | bytes 1376260
  0.6 29.3 %copy-start.14 = (f32[128,2]{0,1:T(2,128)S(1)}, f32[128,2]{0,1:T(2,128)}, u32[]{:S(2)}) copy-start(f32[128,2]{0,1:T(2,128)} %param.10) | copy-start | bytes 3076
  0.7 29.4 %copy-start.11 = (bf16[128,1792]{1,0:T(8,128)(2,1)S(1)}, bf16[128,1792]{1,0:T(8,128)(2,1)}, u32[]{:S(2)}) copy-start(bf16[128,1792]{1,0:T(8,128)(2,1)} %param.8) | copy-start | bytes 1376260
  29.9 12.3 %copy-start.2 = (bf16[16,24,1792]{2,1,0:T(8,128)(2,1)}, bf16[16,24,1792]{2,1,0:T(8,128)(2,1)S(1)}, u32[]{:S(2)}) copy-start(bf16[16,24,1792]{2,1,0:T(8,128)(2,1)S(1)} %all_to_all.15) | copy-start | bytes 4128772
  29.9 6.7 %collective-permute-start = (bf16[384,1792]{1,0:T(8,128)(2,1)S(1)}, bf16[384,1792]{1,0:T(8,128)(2,1)}, u32[]{:S(2)}, u32[]{:S(2)}) collective-permute-start(bf16[384,1792]{1,0:T(8,128)(2,1)S(1)} %bitcast.186), channel_id=1, source_target_pairs={{0,4},{4,0},{8,12},{12,8},{16,20},{20,16},{24,28},{28,24},{32,36},... | collective-permute-start | bytes 4128776 | tf_op jit(solution)/shard_map/ppermute | solution.py:109
  31.7 25.9 %all-to-all-start.1 = ((bf16[16,24,1792]{2,1,0:T(8,128)(2,1)}), bf16[16,24,1792]{2,1,0:T(8,128)(2,1)S(1)}, u32[]{:S(2)}, u32[]{:S(2)}) async-start(bf16[16,24,1792]{2,1,0:T(8,128)(2,1)} %bitcast.2), calls=%async_computation.1 | async-start | bytes 2752512 | tf_op jit(solution)/shard_map/all_to_all | solution.py:99
  36.7 5.6 %copy-start.16 = (bf16[1792,1024]{1,0:T(8,128)(2,1)S(1)}, bf16[1792,1024]{1,0:T(8,128)(2,1)}, u32[]{:S(2)}) copy-start(bf16[1792,1024]{1,0:T(8,128)(2,1)} %param.11) | copy-start | bytes 11010052
  48.0 13.6 %collective-permute-start.1 = (bf16[2,96,1024]{2,1,0:T(8,128)(2,1)S(1)}, bf16[2,96,1024]{2,1,0:T(8,128)(2,1)S(1)}, u32[]{:S(2)}, u32[]{:S(2)}) collective-permute-start(bf16[2,96,1024]{2,1,0:T(8,128)(2,1)S(1)} %pad_maximum_fusion.5), channel_id=1, source_target_pairs={{0,1},{1,2},{2,3},{3,0},{4,5},{5,6},{6,7},{7,4},{8,9},{9,10},{10,1... | collective-permute-start | bytes 1179656 | tf_op jit(solution)/shard_map/ppermute | solution.py:55
  50.1 11.6 %collective-permute-start.2 = (bf16[2,96,1024]{2,1,0:T(8,128)(2,1)S(1)}, bf16[2,96,1024]{2,1,0:T(8,128)(2,1)}, u32[]{:S(2)}, u32[]{:S(2)}) collective-permute-start(bf16[2,96,1024]{2,1,0:T(8,128)(2,1)S(1)} %pad_maximum_fusion.6), channel_id=1, source_target_pairs={{0,3},{1,0},{2,1},{3,2},{4,7},{5,4},{6,5},{7,6},{8,11},{9,8},{10,9... | collective-permute-start | bytes 1179656 | tf_op jit(solution)/shard_map/ppermute | solution.py:58
  61.6 0.7 copy-start.12
  62.4 5.4 %collective-permute-start.3 = (bf16[384,1792]{1,0:T(8,128)(2,1)S(1)}, bf16[384,1792]{1,0:T(8,128)(2,1)S(1)}, u32[]{:S(2)}, u32[]{:S(2)}) collective-permute-start(bf16[384,1792]{1,0:T(8,128)(2,1)S(1)} %bitcast.182), channel_id=1, source_target_pairs={{0,4},{4,0},{8,12},{12,8},{16,20},{20,16},{24,28},{28,24},{32,36},... | collective-permute-start | bytes 4128776 | tf_op jit(solution)/shard_map/ppermute | solution.py:109
  62.4 5.0 %copy-start.4 = (bf16[1,96,1024]{2,1,0:T(8,128)(2,1)S(1)}, bf16[1,96,1024]{2,1,0:T(8,128)(2,1)}, u32[]{:S(2)}) copy-start(bf16[1,96,1024]{2,1,0:T(8,128)(2,1)} %get-tuple-element.69) | copy-start | bytes 589828
  62.4 5.0 %copy-start.13 = (bf16[2,96,1024]{2,1,0:T(8,128)(2,1)S(1)}, bf16[2,96,1024]{2,1,0:T(8,128)(2,1)}, u32[]{:S(2)}) copy-start(bf16[2,96,1024]{2,1,0:T(8,128)(2,1)} %copy-done.12) | copy-start | bytes 1179652
  64.8 30.5 %collective-permute-start.9 = (bf16[2,2,96,1024]{3,2,1,0:T(8,128)(2,1)S(1)}, bf16[2,2,96,1024]{3,2,1,0:T(8,128)(2,1)S(1)}, u32[]{:S(2)}, u32[]{:S(2)}) collective-permute-start(bf16[2,2,96,1024]{3,2,1,0:T(8,128)(2,1)S(1)} %pad_maximum_fusion.3), channel_id=1, source_target_pairs={{0,3},{1,0},{2,1},{3,2},{4,7},{5,4},{6,5},{7,6},{8,11},{9,8},{10,9... | collective-permute-start | bytes 2359304 | tf_op jit(solution)/shard_map/ppermute | solution.py:58
  67.6 2.0 %copy-start.15 = (bf16[1024,1792]{1,0:T(8,128)(2,1)S(1)}, bf16[1024,1792]{1,0:T(8,128)(2,1)}, u32[]{:S(2)}) copy-start(bf16[1024,1792]{1,0:T(8,128)(2,1)} %param.13) | copy-start | bytes 11010052
  67.6 27.7 %collective-permute-start.8 = (bf16[2,2,96,1024]{3,2,1,0:T(8,128)(2,1)S(1)}, bf16[2,2,96,1024]{3,2,1,0:T(8,128)(2,1)S(1)}, u32[]{:S(2)}, u32[]{:S(2)}) collective-permute-start(bf16[2,2,96,1024]{3,2,1,0:T(8,128)(2,1)S(1)} %maximum_maximum_fusion), channel_id=1, source_target_pairs={{0,1},{1,2},{2,3},{3,0},{4,5},{5,6},{6,7},{7,4},{8,9},{9,10},{10,1... | collective-permute-start | bytes 2359304 | tf_op jit(solution)/shard_map/ppermute | solution.py:55
  69.6 3.0 %copy-start.9 = (bf16[768,1792]{1,0:T(8,128)(2,1)}, bf16[768,1792]{1,0:T(8,128)(2,1)S(1)}, u32[]{:S(2)}) copy-start(bf16[768,1792]{1,0:T(8,128)(2,1)S(1)} %constant_dynamic-update-slice_fusion.4) | copy-start | bytes 8257540
  69.6 5.3 %copy-start.7 = (bf16[1,96,1024]{2,1,0:T(8,128)(2,1)S(1)}, bf16[1,96,1024]{2,1,0:T(8,128)(2,1)}, u32[]{:S(2)}) copy-start(bf16[1,96,1024]{2,1,0:T(8,128)(2,1)} %get-tuple-element.40) | copy-start | bytes 589828
  69.6 5.3 %copy-start.8 = (bf16[1,96,1024]{2,1,0:T(8,128)(2,1)S(1)}, bf16[1,96,1024]{2,1,0:T(8,128)(2,1)}, u32[]{:S(2)}) copy-start(bf16[1,96,1024]{2,1,0:T(8,128)(2,1)} %get-tuple-element.73) | copy-start | bytes 589828
  72.7 2.3 %copy-start.5 = (bf16[1,96,1024]{2,1,0:T(8,128)(2,1)S(1)}, bf16[1,96,1024]{2,1,0:T(8,128)(2,1)}, u32[]{:S(2)}) copy-start(bf16[1,96,1024]{2,1,0:T(8,128)(2,1)} %get-tuple-element.45) | copy-start | bytes 589828
  72.7 2.3 %copy-start.6 = (bf16[1,96,1024]{2,1,0:T(8,128)(2,1)S(1)}, bf16[1,96,1024]{2,1,0:T(8,128)(2,1)}, u32[]{:S(2)}) copy-start(bf16[1,96,1024]{2,1,0:T(8,128)(2,1)} %get-tuple-element.68) | copy-start | bytes 589828
  72.8 16.2 %collective-permute-start.6 = (bf16[1,96,1024]{2,1,0:T(8,128)(2,1)S(1)}, bf16[1,96,1024]{2,1,0:T(8,128)(2,1)S(1)}, u32[]{:S(2)}, u32[]{:S(2)}) collective-permute-start(bf16[1,96,1024]{2,1,0:T(8,128)(2,1)S(1)} %get-tuple-element.25), channel_id=1, source_target_pairs={{0,3},{1,0},{2,1},{3,2},{4,7},{5,4},{6,5},{7,6},{8,11},{9,8},{10,9... | collective-permute-start | bytes 589832 | tf_op jit(solution)/shard_map/ppermute | solution.py:58
  74.4 18.3 %collective-permute-start.4 = (bf16[1,96,1024]{2,1,0:T(8,128)(2,1)S(1)}, bf16[1,96,1024]{2,1,0:T(8,128)(2,1)S(1)}, u32[]{:S(2)}, u32[]{:S(2)}) collective-permute-start(bf16[1,96,1024]{2,1,0:T(8,128)(2,1)S(1)} %get-tuple-element.28), channel_id=1, source_target_pairs={{0,1},{1,2},{2,3},{3,0},{4,5},{5,6},{6,7},{7,4},{8,9},{9,10},{10,1... | collective-permute-start | bytes 589832 | tf_op jit(solution)/shard_map/ppermute | solution.py:55
  92.9 10.7 %collective-permute-start.7 = (bf16[1,2,96,1024]{3,2,1,0:T(8,128)(2,1)S(1)}, bf16[1,2,96,1024]{3,2,1,0:T(8,128)(2,1)S(1)}, u32[]{:S(2)}, u32[]{:S(2)}) collective-permute-start(bf16[1,2,96,1024]{3,2,1,0:T(8,128)(2,1)S(1)} %pad_maximum_fusion.9), channel_id=1, source_target_pairs={{0,3},{1,0},{2,1},{3,2},{4,7},{5,4},{6,5},{7,6},{8,11},{9,8},{10,9... | collective-permute-start | bytes 1179656 | tf_op jit(solution)/shard_map/ppermute | solution.py:58
  93.3 11.7 %collective-permute-start.5 = (bf16[1,2,96,1024]{3,2,1,0:T(8,128)(2,1)S(1)}, bf16[1,2,96,1024]{3,2,1,0:T(8,128)(2,1)S(1)}, u32[]{:S(2)}, u32[]{:S(2)}) collective-permute-start(bf16[1,2,96,1024]{3,2,1,0:T(8,128)(2,1)S(1)} %pad_maximum_fusion.8), channel_id=1, source_target_pairs={{0,1},{1,2},{2,3},{3,0},{4,5},{5,6},{6,7},{7,4},{8,9},{9,10},{10,1... | collective-permute-start | bytes 1179656 | tf_op jit(solution)/shard_map/ppermute | solution.py:55
  105.5 9.6 %collective-permute-start.11 = (bf16[2,96,1024]{2,1,0:T(8,128)(2,1)S(1)}, bf16[2,96,1024]{2,1,0:T(8,128)(2,1)S(1)}, u32[]{:S(2)}, u32[]{:S(2)}) collective-permute-start(bf16[2,96,1024]{2,1,0:T(8,128)(2,1)S(1)} %get-tuple-element.48), channel_id=1, source_target_pairs={{0,3},{1,0},{2,1},{3,2},{4,7},{5,4},{6,5},{7,6},{8,11},{9,8},{10,9... | collective-permute-start | bytes 1179656 | tf_op jit(solution)/shard_map/ppermute | solution.py:58
  105.8 10.7 %collective-permute-start.10 = (bf16[2,96,1024]{2,1,0:T(8,128)(2,1)S(1)}, bf16[2,96,1024]{2,1,0:T(8,128)(2,1)S(1)}, u32[]{:S(2)}, u32[]{:S(2)}) collective-permute-start(bf16[2,96,1024]{2,1,0:T(8,128)(2,1)S(1)} %get-tuple-element.48), channel_id=1, source_target_pairs={{0,1},{1,2},{2,3},{3,0},{4,5},{5,6},{6,7},{7,4},{8,9},{9,10},{10,1... | collective-permute-start | bytes 1179656 | tf_op jit(solution)/shard_map/ppermute | solution.py:55
  107.8 21.7 %copy-start.18 = (bf16[1792,1024]{1,0:T(8,128)(2,1)S(1)}, bf16[1792,1024]{1,0:T(8,128)(2,1)}, u32[]{:S(2)}) copy-start(bf16[1792,1024]{1,0:T(8,128)(2,1)} %param.12) | copy-start | bytes 11010052
  116.5 14.7 %collective-permute-start.12 = (bf16[2,96,1024]{2,1,0:T(8,128)(2,1)S(1)}, bf16[2,96,1024]{2,1,0:T(8,128)(2,1)S(1)}, u32[]{:S(2)}, u32[]{:S(2)}) collective-permute-start(bf16[2,96,1024]{2,1,0:T(8,128)(2,1)S(1)} %get-tuple-element.16), channel_id=1, source_target_pairs={{0,1},{1,2},{2,3},{3,0},{4,5},{5,6},{6,7},{7,4},{8,9},{9,10},{10,1... | collective-permute-start | bytes 1179656 | tf_op jit(solution)/shard_map/ppermute | solution.py:55
  117.0 8.8 %collective-permute-start.13 = (bf16[2,96,1024]{2,1,0:T(8,128)(2,1)S(1)}, bf16[2,96,1024]{2,1,0:T(8,128)(2,1)S(1)}, u32[]{:S(2)}, u32[]{:S(2)}) collective-permute-start(bf16[2,96,1024]{2,1,0:T(8,128)(2,1)S(1)} %collective-permute-done.11), channel_id=1, source_target_pairs={{0,3},{1,0},{2,1},{3,2},{4,7},{5,4},{6,5},{7,6},{8,11},{9,8},{10,9... | collective-permute-start | bytes 1179656 | tf_op jit(solution)/shard_map/ppermute | solution.py:58
  125.8 14.4 %collective-permute-start.14 = (bf16[2,96,1024]{2,1,0:T(8,128)(2,1)S(1)}, bf16[2,96,1024]{2,1,0:T(8,128)(2,1)S(1)}, u32[]{:S(2)}, u32[]{:S(2)}) collective-permute-start(bf16[2,96,1024]{2,1,0:T(8,128)(2,1)S(1)} %get-tuple-element.16), channel_id=1, source_target_pairs={{0,3},{1,0},{2,1},{3,2},{4,7},{5,4},{6,5},{7,6},{8,11},{9,8},{10,9... | collective-permute-start | bytes 1179656 | tf_op jit(solution)/shard_map/ppermute | solution.py:58
  129.5 2.0 %copy-start.17 = (bf16[1792,1024]{1,0:T(8,128)(2,1)S(1)}, bf16[1792,1024]{1,0:T(8,128)(2,1)}, u32[]{:S(2)}) copy-start(bf16[1792,1024]{1,0:T(8,128)(2,1)} %param.11) | copy-start | bytes 11010052
  131.2 9.1 %collective-permute-start.15 = (bf16[2,96,1024]{2,1,0:T(8,128)(2,1)S(1)}, bf16[2,96,1024]{2,1,0:T(8,128)(2,1)S(1)}, u32[]{:S(2)}, u32[]{:S(2)}) collective-permute-start(bf16[2,96,1024]{2,1,0:T(8,128)(2,1)S(1)} %collective-permute-done.12), channel_id=1, source_target_pairs={{0,1},{1,2},{2,3},{3,0},{4,5},{5,6},{6,7},{7,4},{8,9},{9,10},{10,1... | collective-permute-start | bytes 1179656 | tf_op jit(solution)/shard_map/ppermute | solution.py:55
  133.2 11.8 %collective-permute-start.16 = (bf16[384,1792]{1,0:T(8,128)(2,1)S(1)}, bf16[384,1792]{1,0:T(8,128)(2,1)S(1)}, u32[]{:S(2)}, u32[]{:S(2)}) collective-permute-start(bf16[384,1792]{1,0:T(8,128)(2,1)S(1)} %convolution_add_fusion.1), channel_id=1, source_target_pairs={{0,4},{4,0},{8,12},{12,8},{16,20},{20,16},{24,28},{28,24},{32,36},... | collective-permute-start | bytes 4128776 | tf_op jit(solution)/shard_map/ppermute | solution.py:109
  146.3 24.6 %collective-permute-start.18 = (bf16[2,96,1024]{2,1,0:T(8,128)(2,1)}, bf16[2,96,1024]{2,1,0:T(8,128)(2,1)S(1)}, u32[]{:S(2)}, u32[]{:S(2)}) collective-permute-start(bf16[2,96,1024]{2,1,0:T(8,128)(2,1)} %fusion.5), channel_id=1, source_target_pairs={{0,3},{1,0},{2,1},{3,2},{4,7},{5,4},{6,5},{7,6},{8,11},{9,8},{10,9... | collective-permute-start | bytes 1179656 | tf_op jit(solution)/shard_map/ppermute | solution.py:58
  146.3 26.0 %collective-permute-start.17 = (bf16[2,96,1024]{2,1,0:T(8,128)(2,1)}, bf16[2,96,1024]{2,1,0:T(8,128)(2,1)}, u32[]{:S(2)}, u32[]{:S(2)}) collective-permute-start(bf16[2,96,1024]{2,1,0:T(8,128)(2,1)} %fusion.5), channel_id=1, source_target_pairs={{0,1},{1,2},{2,3},{3,0},{4,5},{5,6},{6,7},{7,4},{8,9},{9,10},{10,1... | collective-permute-start | bytes 1179656 | tf_op jit(solution)/shard_map/ppermute | solution.py:55
  148.3 36.5 %all-to-all-start.2 = ((bf16[16,24,1792]{2,1,0:T(8,128)(2,1)}), bf16[16,24,1792]{2,1,0:T(8,128)(2,1)S(1)}, u32[]{:S(2)}, u32[]{:S(2)}) async-start(bf16[16,24,1792]{2,1,0:T(8,128)(2,1)} %bitcast.52), calls=%async_computation.2 | async-start | bytes 2752512 | tf_op jit(solution)/shard_map/all_to_all | solution.py:99
  155.6 7.2 %copy-start.3 = (bf16[16,24,1792]{2,1,0:T(8,128)(2,1)S(1)}, bf16[16,24,1792]{2,1,0:T(8,128)(2,1)}, u32[]{:S(2)}) copy-start(bf16[16,24,1792]{2,1,0:T(8,128)(2,1)} %copy-done.2) | copy-start | bytes 4128772
  168.7 11.5 %copy-start.10 = (bf16[768,1792]{1,0:T(8,128)(2,1)S(1)}, bf16[768,1792]{1,0:T(8,128)(2,1)}, u32[]{:S(2)}) copy-start(bf16[768,1792]{1,0:T(8,128)(2,1)} %copy-done.9) | copy-start | bytes 8257540
  171.0 9.2 %collective-permute-start.20 = (bf16[96,1024]{1,0:T(8,128)(2,1)S(1)}, bf16[96,1024]{1,0:T(8,128)(2,1)S(1)}, u32[]{:S(2)}, u32[]{:S(2)}) collective-permute-start(bf16[96,1024]{1,0:T(8,128)(2,1)S(1)} %slice_bitcast_fusion), channel_id=1, source_target_pairs={{0,3},{1,0},{2,1},{3,2},{4,7},{5,4},{6,5},{7,6},{8,11},{9,8},{10,9... | collective-permute-start | bytes 589832 | tf_op jit(solution)/shard_map/ppermute | solution.py:58
  173.2 7.0 %collective-permute-start.19 = (bf16[96,1024]{1,0:T(8,128)(2,1)S(1)}, bf16[96,1024]{1,0:T(8,128)(2,1)S(1)}, u32[]{:S(2)}, u32[]{:S(2)}) collective-permute-start(bf16[96,1024]{1,0:T(8,128)(2,1)S(1)} %slice_bitcast_fusion.3), channel_id=1, source_target_pairs={{0,1},{1,2},{2,3},{3,0},{4,5},{5,6},{6,7},{7,4},{8,9},{9,10},{10,1... | collective-permute-start | bytes 589832 | tf_op jit(solution)/shard_map/ppermute | solution.py:55
  180.2 5.8 %copy-start.1 = (bf16[128,1792]{1,0:T(8,128)(2,1)S(1)}, bf16[128,1792]{1,0:T(8,128)(2,1)}, u32[]{:S(2)}) copy-start(bf16[128,1792]{1,0:T(8,128)(2,1)} %param.7) | copy-start | bytes 1376260

commit v3 on v2

--- a/solution.py
+++ b/solution.py
@@ -156,7 +156,7 @@
     )
     d_gate, d_up = [after(jnp.concatenate(pair), total) for pair in zip(cots_own, cots_other)]
     grad_gate = contract(x_rows, d_gate, 0, 0, jnp.bfloat16)
-    grad_up = contract(x_rows, d_up, 0, 0, jnp.bfloat16)
+    grad_up = contract(x_rows, after(d_up, hid_left, hid_right), 0, 0, jnp.bfloat16)
     grad_down = contract(hidden, g_rows, 0, 0, jnp.bfloat16)
     grad_tokens = contract(choose, returned, 0, 0, jnp.bfloat16)
     return (grad_tokens, grad_gate, grad_up, grad_down)

time: 187 us -> 183 us (0.979)
  waiting for transfers between devices: 61.5 us -> 56.8 us
  starting transfers between devices: 36.9 us -> 40.1 us
    ppermute x9, waiting for transfers between devices: 33.8 us -> 17.3 us  [down(): lax.ppermute(array, self.axis, [(i, (i - 1) % self.size) for i in range(s...]
    ppermute x9, waiting for transfers between devices: 22.3 us -> 34.1 us  [up(): lax.ppermute(array, self.axis, [(i, (i + 1) % self.size) for i in range(s...]
    ppermute x9, starting transfers between devices: 14.7 us -> 19.3 us  [down(): lax.ppermute(array, self.axis, [(i, (i - 1) % self.size) for i in range(s...]
  transfers between devices with their start and end apart: 23 -> 23, of which waited for: 11 -> 10; matrix products, arithmetic and copies ran while one was open for 28% -> 28% of each run, Pallas kernels for 0% -> 0%
where the time goes in v3:
time: 183 us
  waiting for transfers between devices  56.8 us (31%)
  matrix products  40.6 us (22%)
  starting transfers between devices  40.1 us (22%)
  blocking collectives  26.6 us (15%)
  local copies, waits for them, and re-layouts  8.85 us (5%)
  other arithmetic  8.61 us (5%)
    dot_general x14, matrix products, contract(): lax.dot_general(first_arr, second_arr, (((first_dim,), (second_dim,)), ((...  40.6 us
    ppermute x9, waiting for transfers between devices, up(): lax.ppermute(array, self.axis, [(i, (i + 1) % self.size) for i in range(s...  34.1 us
    all_to_all x1, blocking collectives, exchange(): lax.all_to_all(rows.reshape(experts, -1, width), 'expert', split_axis=0,...  26.6 us
    ppermute x9, starting transfers between devices, down(): lax.ppermute(array, self.axis, [(i, (i - 1) % self.size) for i in range(s...  19.3 us
    ppermute x9, waiting for transfers between devices, down(): lax.ppermute(array, self.axis, [(i, (i - 1) % self.size) for i in range(s...  17.3 us
    all_to_all x2, starting transfers between devices, exchange(): lax.all_to_all(rows.reshape(experts, -1, width), 'expert', split_axis=0,...  12.2 us
    ppermute x9, starting transfers between devices, up(): lax.ppermute(array, self.axis, [(i, (i + 1) % self.size) for i in range(s...  8.49 us
    all_to_all x2, waiting for transfers between devices, exchange(): lax.all_to_all(rows.reshape(experts, -1, width), 'expert', split_axis=0,...  5.39 us
  transfers between devices with their start and end apart: 23, of which 10 were waited for; matrix products, arithmetic and copies ran while one was open for 28% of the time, Pallas kernels for 0%

profile of v3, /device:TPU:2, one launch (start us, length us, event | category | flops | bytes accessed | tf_op | source)
XLA Modules:
  0.0 182.8 jit_solution(7572794861519118300)
XLA Ops:
  0.7 0.9 copy.21
  1.5 0.1 eq.70
  1.7 0.2 fusion.4
  1.9 0.1 convert_element_type.155
  2.1 0.7 multiply_add_fusion
  2.9 0.5 convolution_convert_fusion.3
  3.4 26.6 %all_to_all.15 = bf16[16,24,1792]{2,1,0:T(8,128)(2,1)S(1)} all-to-all(bf16[16,24,1792]{2,1,0:T(8,128)(2,1)S(1)} %bitcast.185), channel_id=1, replica_groups={{0,8,16,24,32,40,48,56,64,72,80,88,96,104,112,120},{4,12,20,28,36,44,52..., dimensions={0} | all-to-all | bytes 2752512 | tf_op jit(solution)/shard_map/all_to_all | solution.py:99
  29.9 0.1 select_reduce_fusion
  30.1 1.6 fusion
  31.7 5.0 %all-to-all-start.1 = ((bf16[16,24,1792]{2,1,0:T(8,128)(2,1)}), bf16[16,24,1792]{2,1,0:T(8,128)(2,1)S(1)}, u32[]{:S(2)}, u32[]{:S(2)}) async-start(bf16[16,24,1792]{2,1,0:T(8,128)(2,1)} %bitcast.2), calls=%async_computation.1 | async-start | bytes 2752512 | tf_op jit(solution)/shard_map/all_to_all | solution.py:99
  36.7 5.6 %convolution_convert_fusion.6 = bf16[768,1024]{1,0:T(8,128)(2,1)S(1)} fusion(bf16[1792,1024]{1,0:T(8,128)(2,1)} %param.12, bf16[384,1792]{1,0:T(8,128)(2,1)} %collective-permute-done, bf16[384,1792]{1,0:T(8,128)(2,1)S(1)} %bitcast.187), kind=kOutput, calls=%fused_computation.12 | convolution fusion | flops 2824863744 | bytes 7995392 | tf_op jit(solution)/shard_map/dot_general | solution.py:8
  42.3 4.3 %convolution_convert_fusion.7 = bf16[768,1024]{1,0:T(8,128)(2,1)S(1)} fusion(bf16[1792,1024]{1,0:T(8,128)(2,1)S(1)} %copy-done.16, bf16[384,1792]{1,0:T(8,128)(2,1)} %collective-permute-done, bf16[384,1792]{1,0:T(8,128)(2,1)S(1)} %bitcast.188), kind=kOutput, calls=%fused_computation.13 | convolution fusion | flops 2824863744 | bytes 7995392 | tf_op jit(solution)/shard_map/dot_general | solution.py:8
  46.7 1.3 dynamic-slice_bitcast_fusion.10
  48.0 4.1 %collective-permute-start.2 = (bf16[2,96,1024]{2,1,0:T(8,128)(2,1)S(1)}, bf16[2,96,1024]{2,1,0:T(8,128)(2,1)}, u32[]{:S(2)}, u32[]{:S(2)}) collective-permute-start(bf16[2,96,1024]{2,1,0:T(8,128)(2,1)S(1)} %pad_maximum_fusion.6), channel_id=1, source_target_pairs={{0,3},{1,0},{2,1},{3,2},{4,7},{5,4},{6,5},{7,6},{8,11},{9,8},{10,9... | collective-permute-start | bytes 1179656 | tf_op jit(solution)/shard_map/ppermute | solution.py:58
  52.3 5.4 %all-to-all-done.1 = bf16[16,24,1792]{2,1,0:T(8,128)(2,1)S(1)} async-done(((bf16[16,24,1792]{2,1,0:T(8,128)(2,1)}), bf16[16,24,1792]{2,1,0:T(8,128)(2,1)S(1)}, u32[]{:S(2)}, u32[]{:S(2)}) %all-to-all-start.1) | async-done | bytes 1376288 | tf_op jit(solution)/shard_map/all_to_all | solution.py:99
  57.6 3.3 %collective-permute-done.2 = bf16[2,96,1024]{2,1,0:T(8,128)(2,1)} collective-permute-done((bf16[2,96,1024]{2,1,0:T(8,128)(2,1)S(1)}, bf16[2,96,1024]{2,1,0:T(8,128)(2,1)}, u32[]{:S(2)}, u32[]{:S(2)}) %collective-permute-start.2) | collective-permute-done | bytes 393248 | tf_op jit(solution)/shard_map/ppermute | solution.py:58
  60.9 3.5 %collective-permute-done.1 = bf16[2,96,1024]{2,1,0:T(8,128)(2,1)S(1)} collective-permute-done((bf16[2,96,1024]{2,1,0:T(8,128)(2,1)S(1)}, bf16[2,96,1024]{2,1,0:T(8,128)(2,1)S(1)}, u32[]{:S(2)}, u32[]{:S(2)}) %collective-permute-start.1) | collective-permute-done | bytes 393248 | tf_op jit(solution)/shard_map/ppermute | solution.py:55
  64.4 0.7 copy-done.12
  65.2 1.3 fusion.10
  66.5 1.1 pad_maximum_fusion.3
  67.6 0.3 collective-permute-start.9
  68.0 0.1 fusion.9
  68.2 1.8 collective-permute-start.8
  70.1 0.1 constant_dynamic-update-slice_fusion.4
  70.3 3.0 %convolution_convert_fusion.5 = bf16[768,1024]{1,0:T(8,128)(2,1)S(1)} fusion(bf16[768,1792]{1,0:T(8,128)(2,1)S(1)} %constant_dynamic-update-slice_fusion.4, bf16[1024,1792]{1,0:T(8,128)(2,1)S(1)} %copy-done.15), kind=kOutput, calls=%fused_computation.11 | convolution fusion | flops 2819358720 | bytes 7995392 | tf_op jit(solution)/shard_map/dot_general | solution.py:8
  73.3 0.1 dynamic-slice_bitcast_fusion.17
  73.5 1.8 collective-permute-start.4
  75.3 1.5 collective-permute-start.6
  76.9 16.5 %collective-permute-done.4 = bf16[1,96,1024]{2,1,0:T(8,128)(2,1)S(1)} collective-permute-done((bf16[1,96,1024]{2,1,0:T(8,128)(2,1)S(1)}, bf16[1,96,1024]{2,1,0:T(8,128)(2,1)S(1)}, u32[]{:S(2)}, u32[]{:S(2)}) %collective-permute-start.4) | collective-permute-done | bytes 196640 | tf_op jit(solution)/shard_map/ppermute | solution.py:55
  93.4 0.1 fusion.17
  93.6 0.3 collective-permute-start.7
  93.9 2.1 %collective-permute-start.5 = (bf16[1,2,96,1024]{3,2,1,0:T(8,128)(2,1)S(1)}, bf16[1,2,96,1024]{3,2,1,0:T(8,128)(2,1)S(1)}, u32[]{:S(2)}, u32[]{:S(2)}) collective-permute-start(bf16[1,2,96,1024]{3,2,1,0:T(8,128)(2,1)S(1)} %pad_maximum_fusion.8), channel_id=1, source_target_pairs={{0,1},{1,2},{2,3},{3,0},{4,5},{5,6},{6,7},{7,4},{8,9},{9,10},{10,1... | collective-permute-start | bytes 1179656 | tf_op jit(solution)/shard_map/ppermute | solution.py:55
  96.0 0.4 convert_add_fusion
  96.4 1.0 fusion.5
  97.4 6.9 %collective-permute-done.7 = bf16[1,2,96,1024]{3,2,1,0:T(8,128)(2,1)S(1)} collective-permute-done((bf16[1,2,96,1024]{3,2,1,0:T(8,128)(2,1)S(1)}, bf16[1,2,96,1024]{3,2,1,0:T(8,128)(2,1)S(1)}, u32[]{:S(2)}, u32[]{:S(2)}) %collective-permute-start.7) | collective-permute-done | bytes 393248 | tf_op jit(solution)/shard_map/ppermute | solution.py:58
  104.3 1.3 collective-permute-done.5
  105.7 0.5 multiply_convert_fusion
  106.2 0.6 collective-permute-start.10
  106.8 2.7 %collective-permute-start.11 = (bf16[2,96,1024]{2,1,0:T(8,128)(2,1)S(1)}, bf16[2,96,1024]{2,1,0:T(8,128)(2,1)S(1)}, u32[]{:S(2)}, u32[]{:S(2)}) collective-permute-start(bf16[2,96,1024]{2,1,0:T(8,128)(2,1)S(1)} %get-tuple-element.50), channel_id=1, source_target_pairs={{0,3},{1,0},{2,1},{3,2},{4,7},{5,4},{6,5},{7,6},{8,11},{9,8},{10,9... | collective-permute-start | bytes 1179656 | tf_op jit(solution)/shard_map/ppermute | solution.py:58
  109.8 7.3 %collective-permute-done.10 = bf16[2,96,1024]{2,1,0:T(8,128)(2,1)S(1)} collective-permute-done((bf16[2,96,1024]{2,1,0:T(8,128)(2,1)S(1)}, bf16[2,96,1024]{2,1,0:T(8,128)(2,1)S(1)}, u32[]{:S(2)}, u32[]{:S(2)}) %collective-permute-start.10) | collective-permute-done | bytes 393248 | tf_op jit(solution)/shard_map/ppermute | solution.py:55
  117.2 3.3 %collective-permute-start.13 = (bf16[2,96,1024]{2,1,0:T(8,128)(2,1)S(1)}, bf16[2,96,1024]{2,1,0:T(8,128)(2,1)S(1)}, u32[]{:S(2)}, u32[]{:S(2)}) collective-permute-start(bf16[2,96,1024]{2,1,0:T(8,128)(2,1)S(1)} %collective-permute-done.11), channel_id=1, source_target_pairs={{0,3},{1,0},{2,1},{3,2},{4,7},{5,4},{6,5},{7,6},{8,11},{9,8},{10,9... | collective-permute-start | bytes 1179656 | tf_op jit(solution)/shard_map/ppermute | solution.py:58
  120.7 5.7 %collective-permute-done.13 = bf16[2,96,1024]{2,1,0:T(8,128)(2,1)S(1)} collective-permute-done((bf16[2,96,1024]{2,1,0:T(8,128)(2,1)S(1)}, bf16[2,96,1024]{2,1,0:T(8,128)(2,1)S(1)}, u32[]{:S(2)}, u32[]{:S(2)}) %collective-permute-start.13) | collective-permute-done | bytes 393248 | tf_op jit(solution)/shard_map/ppermute | solution.py:58
  126.4 3.7 %collective-permute-start.14 = (bf16[2,96,1024]{2,1,0:T(8,128)(2,1)S(1)}, bf16[2,96,1024]{2,1,0:T(8,128)(2,1)S(1)}, u32[]{:S(2)}, u32[]{:S(2)}) collective-permute-start(bf16[2,96,1024]{2,1,0:T(8,128)(2,1)S(1)} %get-tuple-element.17), channel_id=1, source_target_pairs={{0,3},{1,0},{2,1},{3,2},{4,7},{5,4},{6,5},{7,6},{8,11},{9,8},{10,9... | collective-permute-start | bytes 1179656 | tf_op jit(solution)/shard_map/ppermute | solution.py:58
  130.1 1.6 fusion.33
  131.8 0.3 copy-done.17
  132.1 1.6 convolution_add_fusion.1
  133.9 1.4 collective-permute-done.14
  135.3 5.5 %collective-permute-done.15 = bf16[2,96,1024]{2,1,0:T(8,128)(2,1)S(1)} collective-permute-done((bf16[2,96,1024]{2,1,0:T(8,128)(2,1)S(1)}, bf16[2,96,1024]{2,1,0:T(8,128)(2,1)S(1)}, u32[]{:S(2)}, u32[]{:S(2)}) %collective-permute-start.15) | collective-permute-done | bytes 393248 | tf_op jit(solution)/shard_map/ppermute | solution.py:55
  140.9 1.3 pad_maximum_fusion.1
  142.2 0.1 pad_maximum_fusion.2
  142.3 1.6 fusion.34
  143.9 1.6 convolution_add_fusion
  145.6 1.3 add_convert_fusion
  146.9 3.2 %collective-permute-start.18 = (bf16[2,96,1024]{2,1,0:T(8,128)(2,1)}, bf16[2,96,1024]{2,1,0:T(8,128)(2,1)S(1)}, u32[]{:S(2)}, u32[]{:S(2)}) collective-permute-start(bf16[2,96,1024]{2,1,0:T(8,128)(2,1)} %fusion.5), channel_id=1, source_target_pairs={{0,3},{1,0},{2,1},{3,2},{4,7},{5,4},{6,5},{7,6},{8,11},{9,8},{10,9... | collective-permute-start | bytes 1179656 | tf_op jit(solution)/shard_map/ppermute | solution.py:58
  150.1 7.3 %all-to-all-start.2 = ((bf16[16,24,1792]{2,1,0:T(8,128)(2,1)}), bf16[16,24,1792]{2,1,0:T(8,128)(2,1)S(1)}, u32[]{:S(2)}, u32[]{:S(2)}) async-start(bf16[16,24,1792]{2,1,0:T(8,128)(2,1)} %bitcast.52), calls=%async_computation.2 | async-start | bytes 2752512 | tf_op jit(solution)/shard_map/all_to_all | solution.py:99
  157.4 7.1 %convolution_convert_fusion.2 = bf16[1792,1024]{1,0:T(8,128)(2,1)} fusion(bf16[768,1024]{1,0:T(8,128)(2,1)} %pad_maximum_fusion.1, bf16[384,1792]{1,0:T(8,128)(2,1)} %collective-permute-done, bf16[384,1792]{1,0:T(8,128)(2,1)} %bitcast.189), kind=kOutput, calls=%fused_computation.2 | convolution fusion | flops 2825912320 | bytes 7995392 | tf_op jit(solution)/shard_map/dot_general | solution.py:8
  164.7 1.0 bitcast_dynamic-update-slice_fusion.1
  165.8 0.9 bitcast_dynamic-update-slice_fusion
  166.9 0.9 slice_bitcast_fusion.3
  167.8 2.1 %collective-permute-start.19 = (bf16[96,1024]{1,0:T(8,128)(2,1)S(1)}, bf16[96,1024]{1,0:T(8,128)(2,1)S(1)}, u32[]{:S(2)}, u32[]{:S(2)}) collective-permute-start(bf16[96,1024]{1,0:T(8,128)(2,1)S(1)} %slice_bitcast_fusion.3), channel_id=1, source_target_pairs={{0,1},{1,2},{2,3},{3,0},{4,5},{5,6},{6,7},{7,4},{8,9},{9,10},{10,1... | collective-permute-start | bytes 589832 | tf_op jit(solution)/shard_map/ppermute | solution.py:55
  169.9 5.9 %convolution_convert_fusion.1 = bf16[1792,1024]{1,0:T(8,128)(2,1)} fusion(bf16[768,1024]{1,0:T(8,128)(2,1)S(1)} %pad_maximum_fusion.2, bf16[384,1792]{1,0:T(8,128)(2,1)} %collective-permute-done, bf16[384,1792]{1,0:T(8,128)(2,1)S(1)} %bitcast.190), kind=kOutput, calls=%fused_computation.1 | convolution fusion | flops 2825912320 | bytes 7995392 | tf_op jit(solution)/shard_map/dot_general | solution.py:8
  175.8 1.0 constant_dynamic-update-slice_fusion.3
  177.0 4.6 %convolution_convert_fusion = bf16[1024,1792]{1,0:T(8,128)(2,1)} fusion(bf16[768,1792]{1,0:T(8,128)(2,1)S(1)} %copy-done.10, bf16[384,1024]{1,0:T(8,128)(2,1)S(1)} %constant_dynamic-update-slice_fusion, bf16[384,1024]{1,0:T(8,128)(2,1)S(1)} %constant_dynamic-update-slice_fusion.2), kind=kOutput, calls=%fused_computation | convolution fusion | flops 2823553024 | bytes 7995392 | tf_op jit(solution)/shard_map/dot_general | solution.py:8
  181.6 1.2 convolution_convert_fusion.4
  (89 shorter events, 1.9 us)
Async XLA Ops:
  0.6 2.2 %copy-start = (bf16[128,1792]{1,0:T(8,128)(2,1)S(1)}, bf16[128,1792]{1,0:T(8,128)(2,1)}, u32[]{:S(2)}) copy-start(bf16[128,1792]{1,0:T(8,128)(2,1)} %param.7) | copy-start | bytes 1376260
  0.6 29.3 %copy-start.14 = (f32[128,2]{0,1:T(2,128)S(1)}, f32[128,2]{0,1:T(2,128)}, u32[]{:S(2)}) copy-start(f32[128,2]{0,1:T(2,128)} %param.10) | copy-start | bytes 3076
  0.7 29.4 %copy-start.11 = (bf16[128,1792]{1,0:T(8,128)(2,1)S(1)}, bf16[128,1792]{1,0:T(8,128)(2,1)}, u32[]{:S(2)}) copy-start(bf16[128,1792]{1,0:T(8,128)(2,1)} %param.8) | copy-start | bytes 1376260
  29.9 12.3 %copy-start.2 = (bf16[16,24,1792]{2,1,0:T(8,128)(2,1)}, bf16[16,24,1792]{2,1,0:T(8,128)(2,1)S(1)}, u32[]{:S(2)}) copy-start(bf16[16,24,1792]{2,1,0:T(8,128)(2,1)S(1)} %all_to_all.15) | copy-start | bytes 4128772
  29.9 6.7 %collective-permute-start = (bf16[384,1792]{1,0:T(8,128)(2,1)S(1)}, bf16[384,1792]{1,0:T(8,128)(2,1)}, u32[]{:S(2)}, u32[]{:S(2)}) collective-permute-start(bf16[384,1792]{1,0:T(8,128)(2,1)S(1)} %bitcast.186), channel_id=1, source_target_pairs={{0,4},{4,0},{8,12},{12,8},{16,20},{20,16},{24,28},{28,24},{32,36},... | collective-permute-start | bytes 4128776 | tf_op jit(solution)/shard_map/ppermute | solution.py:109
  31.7 25.9 %all-to-all-start.1 = ((bf16[16,24,1792]{2,1,0:T(8,128)(2,1)}), bf16[16,24,1792]{2,1,0:T(8,128)(2,1)S(1)}, u32[]{:S(2)}, u32[]{:S(2)}) async-start(bf16[16,24,1792]{2,1,0:T(8,128)(2,1)} %bitcast.2), calls=%async_computation.1 | async-start | bytes 2752512 | tf_op jit(solution)/shard_map/all_to_all | solution.py:99
  36.7 5.6 %copy-start.16 = (bf16[1792,1024]{1,0:T(8,128)(2,1)S(1)}, bf16[1792,1024]{1,0:T(8,128)(2,1)}, u32[]{:S(2)}) copy-start(bf16[1792,1024]{1,0:T(8,128)(2,1)} %param.11) | copy-start | bytes 11010052
  48.0 12.9 %collective-permute-start.2 = (bf16[2,96,1024]{2,1,0:T(8,128)(2,1)S(1)}, bf16[2,96,1024]{2,1,0:T(8,128)(2,1)}, u32[]{:S(2)}, u32[]{:S(2)}) collective-permute-start(bf16[2,96,1024]{2,1,0:T(8,128)(2,1)S(1)} %pad_maximum_fusion.6), channel_id=1, source_target_pairs={{0,3},{1,0},{2,1},{3,2},{4,7},{5,4},{6,5},{7,6},{8,11},{9,8},{10,9... | collective-permute-start | bytes 1179656 | tf_op jit(solution)/shard_map/ppermute | solution.py:58
  52.2 12.2 %collective-permute-start.1 = (bf16[2,96,1024]{2,1,0:T(8,128)(2,1)S(1)}, bf16[2,96,1024]{2,1,0:T(8,128)(2,1)S(1)}, u32[]{:S(2)}, u32[]{:S(2)}) collective-permute-start(bf16[2,96,1024]{2,1,0:T(8,128)(2,1)S(1)} %pad_maximum_fusion.5), channel_id=1, source_target_pairs={{0,1},{1,2},{2,3},{3,0},{4,5},{5,6},{6,7},{7,4},{8,9},{9,10},{10,1... | collective-permute-start | bytes 1179656 | tf_op jit(solution)/shard_map/ppermute | solution.py:55
  64.4 0.7 copy-start.12
  65.2 5.0 %collective-permute-start.3 = (bf16[384,1792]{1,0:T(8,128)(2,1)S(1)}, bf16[384,1792]{1,0:T(8,128)(2,1)S(1)}, u32[]{:S(2)}, u32[]{:S(2)}) collective-permute-start(bf16[384,1792]{1,0:T(8,128)(2,1)S(1)} %bitcast.182), channel_id=1, source_target_pairs={{0,4},{4,0},{8,12},{12,8},{16,20},{20,16},{24,28},{28,24},{32,36},... | collective-permute-start | bytes 4128776 | tf_op jit(solution)/shard_map/ppermute | solution.py:109
  65.2 2.8 %copy-start.4 = (bf16[1,96,1024]{2,1,0:T(8,128)(2,1)S(1)}, bf16[1,96,1024]{2,1,0:T(8,128)(2,1)}, u32[]{:S(2)}) copy-start(bf16[1,96,1024]{2,1,0:T(8,128)(2,1)} %get-tuple-element.71) | copy-start | bytes 589828
  65.2 2.8 %copy-start.13 = (bf16[2,96,1024]{2,1,0:T(8,128)(2,1)S(1)}, bf16[2,96,1024]{2,1,0:T(8,128)(2,1)}, u32[]{:S(2)}) copy-start(bf16[2,96,1024]{2,1,0:T(8,128)(2,1)} %copy-done.12) | copy-start | bytes 1179652
  67.6 28.4 %collective-permute-start.9 = (bf16[2,2,96,1024]{3,2,1,0:T(8,128)(2,1)S(1)}, bf16[2,2,96,1024]{3,2,1,0:T(8,128)(2,1)S(1)}, u32[]{:S(2)}, u32[]{:S(2)}) collective-permute-start(bf16[2,2,96,1024]{3,2,1,0:T(8,128)(2,1)S(1)} %pad_maximum_fusion.3), channel_id=1, source_target_pairs={{0,3},{1,0},{2,1},{3,2},{4,7},{5,4},{6,5},{7,6},{8,11},{9,8},{10,9... | collective-permute-start | bytes 2359304 | tf_op jit(solution)/shard_map/ppermute | solution.py:58
  68.2 2.0 %copy-start.15 = (bf16[1024,1792]{1,0:T(8,128)(2,1)S(1)}, bf16[1024,1792]{1,0:T(8,128)(2,1)}, u32[]{:S(2)}) copy-start(bf16[1024,1792]{1,0:T(8,128)(2,1)} %param.13) | copy-start | bytes 11010052
  68.2 27.8 %collective-permute-start.8 = (bf16[2,2,96,1024]{3,2,1,0:T(8,128)(2,1)S(1)}, bf16[2,2,96,1024]{3,2,1,0:T(8,128)(2,1)S(1)}, u32[]{:S(2)}, u32[]{:S(2)}) collective-permute-start(bf16[2,2,96,1024]{3,2,1,0:T(8,128)(2,1)S(1)} %maximum_maximum_fusion), channel_id=1, source_target_pairs={{0,1},{1,2},{2,3},{3,0},{4,5},{5,6},{6,7},{7,4},{8,9},{9,10},{10,1... | collective-permute-start | bytes 2359304 | tf_op jit(solution)/shard_map/ppermute | solution.py:55
  70.2 3.1 %copy-start.9 = (bf16[768,1792]{1,0:T(8,128)(2,1)}, bf16[768,1792]{1,0:T(8,128)(2,1)S(1)}, u32[]{:S(2)}) copy-start(bf16[768,1792]{1,0:T(8,128)(2,1)S(1)} %constant_dynamic-update-slice_fusion.4) | copy-start | bytes 8257540
  70.2 6.5 %copy-start.7 = (bf16[1,96,1024]{2,1,0:T(8,128)(2,1)S(1)}, bf16[1,96,1024]{2,1,0:T(8,128)(2,1)}, u32[]{:S(2)}) copy-start(bf16[1,96,1024]{2,1,0:T(8,128)(2,1)} %get-tuple-element.47) | copy-start | bytes 589828
  70.3 6.5 %copy-start.8 = (bf16[1,96,1024]{2,1,0:T(8,128)(2,1)S(1)}, bf16[1,96,1024]{2,1,0:T(8,128)(2,1)}, u32[]{:S(2)}) copy-start(bf16[1,96,1024]{2,1,0:T(8,128)(2,1)} %get-tuple-element.70) | copy-start | bytes 589828
  73.3 3.5 %copy-start.5 = (bf16[1,96,1024]{2,1,0:T(8,128)(2,1)S(1)}, bf16[1,96,1024]{2,1,0:T(8,128)(2,1)}, u32[]{:S(2)}) copy-start(bf16[1,96,1024]{2,1,0:T(8,128)(2,1)} %get-tuple-element.42) | copy-start | bytes 589828
  73.3 3.5 %copy-start.6 = (bf16[1,96,1024]{2,1,0:T(8,128)(2,1)S(1)}, bf16[1,96,1024]{2,1,0:T(8,128)(2,1)}, u32[]{:S(2)}) copy-start(bf16[1,96,1024]{2,1,0:T(8,128)(2,1)} %get-tuple-element.75) | copy-start | bytes 589828
  73.5 19.9 %collective-permute-start.4 = (bf16[1,96,1024]{2,1,0:T(8,128)(2,1)S(1)}, bf16[1,96,1024]{2,1,0:T(8,128)(2,1)S(1)}, u32[]{:S(2)}, u32[]{:S(2)}) collective-permute-start(bf16[1,96,1024]{2,1,0:T(8,128)(2,1)S(1)} %get-tuple-element.30), channel_id=1, source_target_pairs={{0,1},{1,2},{2,3},{3,0},{4,5},{5,6},{6,7},{7,4},{8,9},{9,10},{10,1... | collective-permute-start | bytes 589832 | tf_op jit(solution)/shard_map/ppermute | solution.py:55
  75.3 18.1 %collective-permute-start.6 = (bf16[1,96,1024]{2,1,0:T(8,128)(2,1)S(1)}, bf16[1,96,1024]{2,1,0:T(8,128)(2,1)S(1)}, u32[]{:S(2)}, u32[]{:S(2)}) collective-permute-start(bf16[1,96,1024]{2,1,0:T(8,128)(2,1)S(1)} %get-tuple-element.27), channel_id=1, source_target_pairs={{0,3},{1,0},{2,1},{3,2},{4,7},{5,4},{6,5},{7,6},{8,11},{9,8},{10,9... | collective-permute-start | bytes 589832 | tf_op jit(solution)/shard_map/ppermute | solution.py:58
  93.6 10.7 %collective-permute-start.7 = (bf16[1,2,96,1024]{3,2,1,0:T(8,128)(2,1)S(1)}, bf16[1,2,96,1024]{3,2,1,0:T(8,128)(2,1)S(1)}, u32[]{:S(2)}, u32[]{:S(2)}) collective-permute-start(bf16[1,2,96,1024]{3,2,1,0:T(8,128)(2,1)S(1)} %pad_maximum_fusion.9), channel_id=1, source_target_pairs={{0,3},{1,0},{2,1},{3,2},{4,7},{5,4},{6,5},{7,6},{8,11},{9,8},{10,9... | collective-permute-start | bytes 1179656 | tf_op jit(solution)/shard_map/ppermute | solution.py:58
  93.9 11.7 %collective-permute-start.5 = (bf16[1,2,96,1024]{3,2,1,0:T(8,128)(2,1)S(1)}, bf16[1,2,96,1024]{3,2,1,0:T(8,128)(2,1)S(1)}, u32[]{:S(2)}, u32[]{:S(2)}) collective-permute-start(bf16[1,2,96,1024]{3,2,1,0:T(8,128)(2,1)S(1)} %pad_maximum_fusion.8), channel_id=1, source_target_pairs={{0,1},{1,2},{2,3},{3,0},{4,5},{5,6},{6,7},{7,4},{8,9},{9,10},{10,1... | collective-permute-start | bytes 1179656 | tf_op jit(solution)/shard_map/ppermute | solution.py:55
  106.2 10.8 %collective-permute-start.10 = (bf16[2,96,1024]{2,1,0:T(8,128)(2,1)S(1)}, bf16[2,96,1024]{2,1,0:T(8,128)(2,1)S(1)}, u32[]{:S(2)}, u32[]{:S(2)}) collective-permute-start(bf16[2,96,1024]{2,1,0:T(8,128)(2,1)S(1)} %get-tuple-element.50), channel_id=1, source_target_pairs={{0,1},{1,2},{2,3},{3,0},{4,5},{5,6},{6,7},{7,4},{8,9},{9,10},{10,1... | collective-permute-start | bytes 1179656 | tf_op jit(solution)/shard_map/ppermute | solution.py:55
  106.8 10.2 %collective-permute-start.11 = (bf16[2,96,1024]{2,1,0:T(8,128)(2,1)S(1)}, bf16[2,96,1024]{2,1,0:T(8,128)(2,1)S(1)}, u32[]{:S(2)}, u32[]{:S(2)}) collective-permute-start(bf16[2,96,1024]{2,1,0:T(8,128)(2,1)S(1)} %get-tuple-element.50), channel_id=1, source_target_pairs={{0,3},{1,0},{2,1},{3,2},{4,7},{5,4},{6,5},{7,6},{8,11},{9,8},{10,9... | collective-permute-start | bytes 1179656 | tf_op jit(solution)/shard_map/ppermute | solution.py:58
  109.8 20.3 %copy-start.18 = (bf16[1792,1024]{1,0:T(8,128)(2,1)S(1)}, bf16[1792,1024]{1,0:T(8,128)(2,1)}, u32[]{:S(2)}) copy-start(bf16[1792,1024]{1,0:T(8,128)(2,1)} %param.12) | copy-start | bytes 11010052
  117.1 14.7 %collective-permute-start.12 = (bf16[2,96,1024]{2,1,0:T(8,128)(2,1)S(1)}, bf16[2,96,1024]{2,1,0:T(8,128)(2,1)S(1)}, u32[]{:S(2)}, u32[]{:S(2)}) collective-permute-start(bf16[2,96,1024]{2,1,0:T(8,128)(2,1)S(1)} %get-tuple-element.17), channel_id=1, source_target_pairs={{0,1},{1,2},{2,3},{3,0},{4,5},{5,6},{6,7},{7,4},{8,9},{9,10},{10,1... | collective-permute-start | bytes 1179656 | tf_op jit(solution)/shard_map/ppermute | solution.py:55
  117.2 9.2 %collective-permute-start.13 = (bf16[2,96,1024]{2,1,0:T(8,128)(2,1)S(1)}, bf16[2,96,1024]{2,1,0:T(8,128)(2,1)S(1)}, u32[]{:S(2)}, u32[]{:S(2)}) collective-permute-start(bf16[2,96,1024]{2,1,0:T(8,128)(2,1)S(1)} %collective-permute-done.11), channel_id=1, source_target_pairs={{0,3},{1,0},{2,1},{3,2},{4,7},{5,4},{6,5},{7,6},{8,11},{9,8},{10,9... | collective-permute-start | bytes 1179656 | tf_op jit(solution)/shard_map/ppermute | solution.py:58
  126.4 9.0 %collective-permute-start.14 = (bf16[2,96,1024]{2,1,0:T(8,128)(2,1)S(1)}, bf16[2,96,1024]{2,1,0:T(8,128)(2,1)S(1)}, u32[]{:S(2)}, u32[]{:S(2)}) collective-permute-start(bf16[2,96,1024]{2,1,0:T(8,128)(2,1)S(1)} %get-tuple-element.17), channel_id=1, source_target_pairs={{0,3},{1,0},{2,1},{3,2},{4,7},{5,4},{6,5},{7,6},{8,11},{9,8},{10,9... | collective-permute-start | bytes 1179656 | tf_op jit(solution)/shard_map/ppermute | solution.py:58
  130.1 2.0 %copy-start.17 = (bf16[1792,1024]{1,0:T(8,128)(2,1)S(1)}, bf16[1792,1024]{1,0:T(8,128)(2,1)}, u32[]{:S(2)}) copy-start(bf16[1792,1024]{1,0:T(8,128)(2,1)} %param.11) | copy-start | bytes 11010052
  131.8 9.1 %collective-permute-start.15 = (bf16[2,96,1024]{2,1,0:T(8,128)(2,1)S(1)}, bf16[2,96,1024]{2,1,0:T(8,128)(2,1)S(1)}, u32[]{:S(2)}, u32[]{:S(2)}) collective-permute-start(bf16[2,96,1024]{2,1,0:T(8,128)(2,1)S(1)} %collective-permute-done.12), channel_id=1, source_target_pairs={{0,1},{1,2},{2,3},{3,0},{4,5},{5,6},{6,7},{7,4},{8,9},{9,10},{10,1... | collective-permute-start | bytes 1179656 | tf_op jit(solution)/shard_map/ppermute | solution.py:55
  133.8 11.8 %collective-permute-start.16 = (bf16[384,1792]{1,0:T(8,128)(2,1)S(1)}, bf16[384,1792]{1,0:T(8,128)(2,1)S(1)}, u32[]{:S(2)}, u32[]{:S(2)}) collective-permute-start(bf16[384,1792]{1,0:T(8,128)(2,1)S(1)} %convolution_add_fusion.1), channel_id=1, source_target_pairs={{0,4},{4,0},{8,12},{12,8},{16,20},{20,16},{24,28},{28,24},{32,36},... | collective-permute-start | bytes 4128776 | tf_op jit(solution)/shard_map/ppermute | solution.py:109
  146.9 19.8 %collective-permute-start.17 = (bf16[2,96,1024]{2,1,0:T(8,128)(2,1)}, bf16[2,96,1024]{2,1,0:T(8,128)(2,1)}, u32[]{:S(2)}, u32[]{:S(2)}) collective-permute-start(bf16[2,96,1024]{2,1,0:T(8,128)(2,1)} %fusion.5), channel_id=1, source_target_pairs={{0,1},{1,2},{2,3},{3,0},{4,5},{5,6},{6,7},{7,4},{8,9},{9,10},{10,1... | collective-permute-start | bytes 1179656 | tf_op jit(solution)/shard_map/ppermute | solution.py:55
  146.9 19.8 %collective-permute-start.18 = (bf16[2,96,1024]{2,1,0:T(8,128)(2,1)}, bf16[2,96,1024]{2,1,0:T(8,128)(2,1)S(1)}, u32[]{:S(2)}, u32[]{:S(2)}) collective-permute-start(bf16[2,96,1024]{2,1,0:T(8,128)(2,1)} %fusion.5), channel_id=1, source_target_pairs={{0,3},{1,0},{2,1},{3,2},{4,7},{5,4},{6,5},{7,6},{8,11},{9,8},{10,9... | collective-permute-start | bytes 1179656 | tf_op jit(solution)/shard_map/ppermute | solution.py:58
  150.1 31.4 %all-to-all-start.2 = ((bf16[16,24,1792]{2,1,0:T(8,128)(2,1)}), bf16[16,24,1792]{2,1,0:T(8,128)(2,1)S(1)}, u32[]{:S(2)}, u32[]{:S(2)}) async-start(bf16[16,24,1792]{2,1,0:T(8,128)(2,1)} %bitcast.52), calls=%async_computation.2 | async-start | bytes 2752512 | tf_op jit(solution)/shard_map/all_to_all | solution.py:99
  164.6 5.3 %copy-start.3 = (bf16[16,24,1792]{2,1,0:T(8,128)(2,1)S(1)}, bf16[16,24,1792]{2,1,0:T(8,128)(2,1)}, u32[]{:S(2)}) copy-start(bf16[16,24,1792]{2,1,0:T(8,128)(2,1)} %copy-done.2) | copy-start | bytes 4128772
  166.8 10.1 %collective-permute-start.20 = (bf16[96,1024]{1,0:T(8,128)(2,1)S(1)}, bf16[96,1024]{1,0:T(8,128)(2,1)S(1)}, u32[]{:S(2)}, u32[]{:S(2)}) collective-permute-start(bf16[96,1024]{1,0:T(8,128)(2,1)S(1)} %slice_bitcast_fusion), channel_id=1, source_target_pairs={{0,3},{1,0},{2,1},{3,2},{4,7},{5,4},{6,5},{7,6},{8,11},{9,8},{10,9... | collective-permute-start | bytes 589832 | tf_op jit(solution)/shard_map/ppermute | solution.py:58
  167.8 9.1 %copy-start.10 = (bf16[768,1792]{1,0:T(8,128)(2,1)S(1)}, bf16[768,1792]{1,0:T(8,128)(2,1)}, u32[]{:S(2)}) copy-start(bf16[768,1792]{1,0:T(8,128)(2,1)} %copy-done.9) | copy-start | bytes 8257540
  167.8 9.1 %collective-permute-start.19 = (bf16[96,1024]{1,0:T(8,128)(2,1)S(1)}, bf16[96,1024]{1,0:T(8,128)(2,1)S(1)}, u32[]{:S(2)}, u32[]{:S(2)}) collective-permute-start(bf16[96,1024]{1,0:T(8,128)(2,1)S(1)} %slice_bitcast_fusion.3), channel_id=1, source_target_pairs={{0,1},{1,2},{2,3},{3,0},{4,5},{5,6},{6,7},{7,4},{8,9},{9,10},{10,1... | collective-permute-start | bytes 589832 | tf_op jit(solution)/shard_map/ppermute | solution.py:55
  176.9 5.8 %copy-start.1 = (bf16[128,1792]{1,0:T(8,128)(2,1)S(1)}, bf16[128,1792]{1,0:T(8,128)(2,1)}, u32[]{:S(2)}) copy-start(bf16[128,1792]{1,0:T(8,128)(2,1)} %param.7) | copy-start | bytes 1376260

commit v4 on v3

--- a/solution.py
+++ b/solution.py
@@ -60,22 +60,38 @@
     def place(self, offset, rows):
         return ((self.me + offset) % self.size) * rows
 
-    def scatter(self, arrays):
+    def part(self, arrays, offset, which):
         rows = arrays[0].shape[0] // 2
         block = rows // self.size
-
-        def part(offset, which):
-            start = which * rows + self.place(offset, block)
-            return jnp.stack([lax.dynamic_slice_in_dim(a, start, block, axis=0) for a in arrays])
-
-        far_own = self.up(part(2, 0))
-        far_other = self.down(part(2, 1))
-        to_right = [wide(part(1, 0)) + wide(far_own), wide(part(1, 1))]
-        to_left = [wide(part(3, 0)), wide(part(3, 1)) + wide(far_other)]
+        start = which * rows + self.place(offset, block)
+        return jnp.stack([lax.dynamic_slice_in_dim(a, start, block, axis=0) for a in arrays])
+
+    def send_far(self, arrays):
+        return self.up(self.part(arrays, 2, 0)), self.down(self.part(arrays, 2, 1))
+
+    def send_near(self, arrays, far):
+        far_own, far_other = far
+        to_right = [wide(self.part(arrays, 1, 0)) + wide(far_own), wide(self.part(arrays, 1, 1))]
+        to_left = [wide(self.part(arrays, 3, 0)), wide(self.part(arrays, 3, 1)) + wide(far_other)]
         from_left = self.up(jnp.stack(to_right, axis=1).astype(jnp.bfloat16))
         from_right = self.down(jnp.stack(to_left, axis=1).astype(jnp.bfloat16))
-        mine = jnp.stack([part(0, 0), part(0, 1)], axis=1)
-        return wide(mine) + wide(from_left) + wide(from_right), (far_own, far_other)
+        return from_left, from_right
+
+    def total(self, arrays, near):
+        mine = jnp.stack([self.part(arrays, 0, 0), self.part(arrays, 0, 1)], axis=1)
+        return wide(mine) + wide(near[0]) + wide(near[1])
+
+    def turned(self, rows):
+        block = rows.shape[0] // (2 * self.size)
+        return jnp.concatenate(
+            [
+                lax.dynamic_slice_in_dim(
+                    rows, which * block * self.size + self.place(offset, block), block, axis=0
+                )
+                for which in range(2)
+                for offset in range(self.size)
+            ]
+        )
 
     def assemble(self, pieces, i):
         block = pieces[0].shape[1]
@@ -120,10 +136,15 @@
     g_own = exchange(after(g_slots, x_own))
     part_gate = contract(x_rows, gate_weight, 1, 0, jnp.bfloat16)
     part_up = contract(x_rows, up_weight, 1, 0, jnp.bfloat16)
-    gate_up, mark = ring.scatter((part_gate, part_up))
-    g_own = after(g_own, *mark)
+    parts = part_gate, part_up
+    far = ring.send_far(parts)
+    near = ring.send_near(parts, far)
+    g_own = after(g_own, *far)
     g_rows = jnp.concatenate([g_own, swap_cores(g_own)])
-    back, _ = ring.scatter((contract(g_rows, down_weight, 1, 1, jnp.bfloat16),))
+    back_parts = (contract(g_rows, down_weight, 1, 1, jnp.bfloat16),)
+    back_far = ring.send_far(back_parts)
+    gate_up = ring.total(parts, [after(n, *back_far) for n in near])
+    back = ring.total(back_parts, ring.send_near(back_parts, back_far))
     hidden, d_gate, d_up = swiglu_backward(gate_up[0], gate_up[1], back[0])
 
     mine = jnp.stack([d_gate, d_up])
@@ -140,8 +161,9 @@
 
     cots_other, rows_other = input_grad((mine[:, 1], left_other, right_other, far_other))
     from_other = swap_cores(rows_other.astype(jnp.bfloat16))
+    g_turned = ring.turned(g_rows)
     cots_own, rows_own = input_grad(
-        (mine_own, left_own, after(right_own, rows_other), after(far_own, rows_other))
+        (mine_own, left_own, after(right_own, rows_other, g_turned), after(far_own, rows_other))
     )
     total = (rows_own + wide(from_other)).astype(jnp.bfloat16)
     returned = exchange(total)
@@ -149,15 +171,14 @@
     hid_left, hid_right = ring.up(hid_mine), ring.down(hid_mine)
     hid_far_own, hid_far_other = ring.up(hid_left[0]), ring.down(hid_right[1])
     hidden = jnp.concatenate(
-        [
-            ring.assemble([p[None] for p in (hid_mine[i], hid_left[i], hid_right[i], far)], 0)
-            for i, far in enumerate((hid_far_own, hid_far_other))
-        ]
-    )
-    d_gate, d_up = [after(jnp.concatenate(pair), total) for pair in zip(cots_own, cots_other)]
+        [hid_mine[0], hid_right[0], hid_far_own, hid_left[0]]
+        + [hid_mine[1], hid_right[1], hid_far_other, hid_left[1]]
+    )
+    cots_own = [after(c, total) for c in cots_own]
+    d_gate, d_up = [jnp.concatenate(pair) for pair in zip(cots_own, cots_other)]
     grad_gate = contract(x_rows, d_gate, 0, 0, jnp.bfloat16)
     grad_up = contract(x_rows, after(d_up, hid_left, hid_right), 0, 0, jnp.bfloat16)
-    grad_down = contract(hidden, g_rows, 0, 0, jnp.bfloat16)
+    grad_down = contract(hidden, g_turned, 0, 0, jnp.bfloat16)
     grad_tokens = contract(choose, returned, 0, 0, jnp.bfloat16)
     return (grad_tokens, grad_gate, grad_up, grad_down)
 

time: 183 us -> 183 us (level)
  starting transfers between devices: 40.1 us -> 35.2 us
  local copies, waits for them, and re-layouts: 8.85 us -> 13.4 us
    ppermute x9, waiting for transfers between devices: 34.1 us -> 18 us  [up(): lax.ppermute(array, self.axis, [(i, (i + 1) % self.size) for i in range(s...]
    ppermute x9, waiting for transfers between devices: 17.3 us -> 32.9 us  [down(): lax.ppermute(array, self.axis, [(i, (i - 1) % self.size) for i in range(s...]
    ppermute x9, starting transfers between devices: 19.3 us -> 12.4 us  [down(): lax.ppermute(array, self.axis, [(i, (i - 1) % self.size) for i in range(s...]
    unnamed x40 -> x56, local copies, waits for them, and re-layouts: 2.1 us -> 7.88 us
    dynamic_update_slice x16 -> x10, local copies, waits for them, and re-layouts: 3.4 us -> 0.3 us  [assemble(): lax.dynamic_update_slice_in_dim(full, rows[i], self.place(offset, block),...]
    another operation x9, other arithmetic: 2.94 us -> 4.97 us  [the longest x2 2.16 us: total(): mine = jnp.stack([self.part(arrays, 0, 0), self.part(arrays, 0, 1)], axis=1)]
    ppermute x9, starting transfers between devices: 8.49 us -> 10.5 us  [up(): lax.ppermute(array, self.axis, [(i, (i + 1) % self.size) for i in range(s...]
    squeeze x0 -> x2, local copies, waits for them, and re-layouts: none -> 1.97 us  [the longest x1 1.03 us: body(): hid_right[1]]
  transfers between devices with their start and end apart: 23 -> 23, of which waited for: 10 -> 11; matrix products, arithmetic and copies ran while one was open for 28% -> 29% of each run, Pallas kernels for 0% -> 0%
where the time goes in v4:
time: 183 us; the launch traced here: 182 us
  waiting for transfers between devices  56.2 us (31%)
  matrix products  40.5 us (22%)
  starting transfers between devices  35.2 us (19%)
  blocking collectives  26.6 us (15%)
  local copies, waits for them, and re-layouts  13.4 us (7%)
  other arithmetic  8.61 us (5%)
    dot_general x14, matrix products, contract(): lax.dot_general(first_arr, second_arr, (((first_dim,), (second_dim,)), ((...  40.5 us
    ppermute x9, waiting for transfers between devices, down(): lax.ppermute(array, self.axis, [(i, (i - 1) % self.size) for i in range(s...  32.9 us
    all_to_all x1, blocking collectives, exchange(): lax.all_to_all(rows.reshape(experts, -1, width), 'expert', split_axis=0,...  26.6 us
    ppermute x9, waiting for transfers between devices, up(): lax.ppermute(array, self.axis, [(i, (i + 1) % self.size) for i in range(s...  18 us
    ppermute x9, starting transfers between devices, down(): lax.ppermute(array, self.axis, [(i, (i - 1) % self.size) for i in range(s...  12.4 us
    all_to_all x2, starting transfers between devices, exchange(): lax.all_to_all(rows.reshape(experts, -1, width), 'expert', split_axis=0,...  12.2 us
    ppermute x9, starting transfers between devices, up(): lax.ppermute(array, self.axis, [(i, (i + 1) % self.size) for i in range(s...  10.5 us
    unnamed x56, local copies, waits for them, and re-layouts  7.88 us
  transfers between devices with their start and end apart: 23, of which 11 were waited for; matrix products, arithmetic and copies ran while one was open for 29% of the time, Pallas kernels for 0%

profile of v4, /device:TPU:2, one launch (start us, length us, event | category | flops | bytes accessed | tf_op | source)
XLA Modules:
  0.0 181.9 jit_solution(15180151355283961338)
XLA Ops:
  0.7 0.9 copy.21
  1.7 0.2 fusion.4
  2.1 0.7 multiply_add_fusion
  2.9 0.5 convolution_convert_fusion.3
  3.4 26.6 %all_to_all.15 = bf16[16,24,1792]{2,1,0:T(8,128)(2,1)S(1)} all-to-all(bf16[16,24,1792]{2,1,0:T(8,128)(2,1)S(1)} %bitcast.185), channel_id=1, replica_groups={{0,8,16,24,32,40,48,56,64,72,80,88,96,104,112,120},{4,12,20,28,36,44,52..., dimensions={0} | all-to-all | bytes 2752512 | tf_op jit(solution)/shard_map/all_to_all | solution.py:115
  29.9 0.1 select_reduce_fusion
  30.1 1.6 fusion
  31.7 5.0 %all-to-all-start.1 = ((bf16[16,24,1792]{2,1,0:T(8,128)(2,1)}), bf16[16,24,1792]{2,1,0:T(8,128)(2,1)S(1)}, u32[]{:S(2)}, u32[]{:S(2)}) async-start(bf16[16,24,1792]{2,1,0:T(8,128)(2,1)} %bitcast.2), calls=%async_computation.1 | async-start | bytes 2752512 | tf_op jit(solution)/shard_map/all_to_all | solution.py:115
  36.7 5.6 %convolution_convert_fusion.6 = bf16[768,1024]{1,0:T(8,128)(2,1)S(1)} fusion(bf16[1792,1024]{1,0:T(8,128)(2,1)} %param.12, bf16[384,1792]{1,0:T(8,128)(2,1)} %collective-permute-done, bf16[384,1792]{1,0:T(8,128)(2,1)S(1)} %bitcast.187), kind=kOutput, calls=%fused_computation.12 | convolution fusion | flops 2824863744 | bytes 7995392 | tf_op jit(solution)/shard_map/dot_general | solution.py:8
  42.3 4.3 %convolution_convert_fusion.7 = bf16[768,1024]{1,0:T(8,128)(2,1)S(1)} fusion(bf16[1792,1024]{1,0:T(8,128)(2,1)S(1)} %copy-done.17, bf16[384,1792]{1,0:T(8,128)(2,1)} %collective-permute-done, bf16[384,1792]{1,0:T(8,128)(2,1)S(1)} %bitcast.188), kind=kOutput, calls=%fused_computation.13 | convolution fusion | flops 2824863744 | bytes 7995392 | tf_op jit(solution)/shard_map/dot_general | solution.py:8
  46.7 1.4 dynamic-slice_bitcast_fusion.10
  48.1 2.0 %collective-permute-start.1 = (bf16[2,96,1024]{2,1,0:T(8,128)(2,1)S(1)}, bf16[2,96,1024]{2,1,0:T(8,128)(2,1)S(1)}, u32[]{:S(2)}, u32[]{:S(2)}) collective-permute-start(bf16[2,96,1024]{2,1,0:T(8,128)(2,1)S(1)} %pad_maximum_fusion.4), channel_id=1, source_target_pairs={{0,1},{1,2},{2,3},{3,0},{4,5},{5,6},{6,7},{7,4},{8,9},{9,10},{10,1... | collective-permute-start | bytes 1179656 | tf_op jit(solution)/shard_map/ppermute | solution.py:55
  50.1 2.2 %collective-permute-start.2 = (bf16[2,96,1024]{2,1,0:T(8,128)(2,1)S(1)}, bf16[2,96,1024]{2,1,0:T(8,128)(2,1)S(1)}, u32[]{:S(2)}, u32[]{:S(2)}) collective-permute-start(bf16[2,96,1024]{2,1,0:T(8,128)(2,1)S(1)} %pad_maximum_fusion.5), channel_id=1, source_target_pairs={{0,3},{1,0},{2,1},{3,2},{4,7},{5,4},{6,5},{7,6},{8,11},{9,8},{10,9... | collective-permute-start | bytes 1179656 | tf_op jit(solution)/shard_map/ppermute | solution.py:58
  52.3 5.3 %all-to-all-done.1 = bf16[16,24,1792]{2,1,0:T(8,128)(2,1)S(1)} async-done(((bf16[16,24,1792]{2,1,0:T(8,128)(2,1)}), bf16[16,24,1792]{2,1,0:T(8,128)(2,1)S(1)}, u32[]{:S(2)}, u32[]{:S(2)}) %all-to-all-start.1) | async-done | bytes 1376288 | tf_op jit(solution)/shard_map/all_to_all | solution.py:115
  57.6 4.0 %collective-permute-done.1 = bf16[2,96,1024]{2,1,0:T(8,128)(2,1)S(1)} collective-permute-done((bf16[2,96,1024]{2,1,0:T(8,128)(2,1)S(1)}, bf16[2,96,1024]{2,1,0:T(8,128)(2,1)S(1)}, u32[]{:S(2)}, u32[]{:S(2)}) %collective-permute-start.1) | collective-permute-done | bytes 393248 | tf_op jit(solution)/shard_map/ppermute | solution.py:55
  61.7 0.7 copy-done.10
  62.4 0.7 copy-done.12
  63.2 1.1 maximum_bitcast_fusion
  64.3 1.1 maximum_bitcast_fusion.1
  65.3 1.3 fusion.10
  66.7 2.4 %collective-permute-start.9 = (bf16[2,2,96,1024]{3,2,1,0:T(8,128)(2,1)S(1)}, bf16[2,2,96,1024]{3,2,1,0:T(8,128)(2,1)S(1)}, u32[]{:S(2)}, u32[]{:S(2)}) collective-permute-start(bf16[2,2,96,1024]{3,2,1,0:T(8,128)(2,1)S(1)} %pad_maximum_fusion.2), channel_id=1, source_target_pairs={{0,3},{1,0},{2,1},{3,2},{4,7},{5,4},{6,5},{7,6},{8,11},{9,8},{10,9... | collective-permute-start | bytes 2359304 | tf_op jit(solution)/shard_map/ppermute | solution.py:58
  69.1 1.2 fusion.9
  70.7 1.7 copy-done.16
  72.4 3.0 %convolution_convert_fusion.5 = bf16[768,1024]{1,0:T(8,128)(2,1)S(1)} fusion(bf16[768,1792]{1,0:T(8,128)(2,1)S(1)} %constant_dynamic-update-slice_fusion, bf16[1024,1792]{1,0:T(8,128)(2,1)S(1)} %copy-done.16), kind=kOutput, calls=%fused_computation.11 | convolution fusion | flops 2819358720 | bytes 7995392 | tf_op jit(solution)/shard_map/dot_general | solution.py:8
  75.6 1.6 collective-permute-start.6
  77.2 0.5 collective-permute-start.4
  78.0 9.2 %collective-permute-done.9 = bf16[2,2,96,1024]{3,2,1,0:T(8,128)(2,1)S(1)} collective-permute-done((bf16[2,2,96,1024]{3,2,1,0:T(8,128)(2,1)S(1)}, bf16[2,2,96,1024]{3,2,1,0:T(8,128)(2,1)S(1)}, u32[]{:S(2)}, u32[]{:S(2)}) %collective-permute-start.9) | collective-permute-done | bytes 786464 | tf_op jit(solution)/shard_map/ppermute | solution.py:58
  87.2 3.1 %collective-permute-done.6 = bf16[1,96,1024]{2,1,0:T(8,128)(2,1)S(1)} collective-permute-done((bf16[1,96,1024]{2,1,0:T(8,128)(2,1)S(1)}, bf16[1,96,1024]{2,1,0:T(8,128)(2,1)S(1)}, u32[]{:S(2)}, u32[]{:S(2)}) %collective-permute-start.6) | collective-permute-done | bytes 196640 | tf_op jit(solution)/shard_map/ppermute | solution.py:58
  90.3 4.6 %collective-permute-done.4 = bf16[1,96,1024]{2,1,0:T(8,128)(2,1)S(1)} collective-permute-done((bf16[1,96,1024]{2,1,0:T(8,128)(2,1)S(1)}, bf16[1,96,1024]{2,1,0:T(8,128)(2,1)S(1)}, u32[]{:S(2)}, u32[]{:S(2)}) %collective-permute-start.4) | collective-permute-done | bytes 196640 | tf_op jit(solution)/shard_map/ppermute | solution.py:55
  95.2 2.1 %collective-permute-start.5 = (bf16[1,2,96,1024]{3,2,1,0:T(8,128)(2,1)S(1)}, bf16[1,2,96,1024]{3,2,1,0:T(8,128)(2,1)S(1)}, u32[]{:S(2)}, u32[]{:S(2)}) collective-permute-start(bf16[1,2,96,1024]{3,2,1,0:T(8,128)(2,1)S(1)} %pad_maximum_fusion.7), channel_id=1, source_target_pairs={{0,1},{1,2},{2,3},{3,0},{4,5},{5,6},{6,7},{7,4},{8,9},{9,10},{10,1... | collective-permute-start | bytes 1179656 | tf_op jit(solution)/shard_map/ppermute | solution.py:55
  97.3 0.4 convert_add_fusion
  97.7 0.2 fusion.5
  98.0 6.9 %collective-permute-done.7 = bf16[1,2,96,1024]{3,2,1,0:T(8,128)(2,1)S(1)} collective-permute-done((bf16[1,2,96,1024]{3,2,1,0:T(8,128)(2,1)S(1)}, bf16[1,2,96,1024]{3,2,1,0:T(8,128)(2,1)S(1)}, u32[]{:S(2)}, u32[]{:S(2)}) %collective-permute-start.7) | collective-permute-done | bytes 393248 | tf_op jit(solution)/shard_map/ppermute | solution.py:58
  104.8 1.3 collective-permute-done.5
  106.2 0.5 multiply_convert_fusion
  106.8 0.2 collective-permute-start.11
  107.0 1.9 %collective-permute-start.10 = (bf16[2,96,1024]{2,1,0:T(8,128)(2,1)S(1)}, bf16[2,96,1024]{2,1,0:T(8,128)(2,1)S(1)}, u32[]{:S(2)}, u32[]{:S(2)}) collective-permute-start(bf16[2,96,1024]{2,1,0:T(8,128)(2,1)S(1)} %get-tuple-element.54), channel_id=1, source_target_pairs={{0,1},{1,2},{2,3},{3,0},{4,5},{5,6},{6,7},{7,4},{8,9},{9,10},{10,1... | collective-permute-start | bytes 1179656 | tf_op jit(solution)/shard_map/ppermute | solution.py:55
  109.1 6.5 %collective-permute-done.11 = bf16[2,96,1024]{2,1,0:T(8,128)(2,1)S(1)} collective-permute-done((bf16[2,96,1024]{2,1,0:T(8,128)(2,1)S(1)}, bf16[2,96,1024]{2,1,0:T(8,128)(2,1)S(1)}, u32[]{:S(2)}, u32[]{:S(2)}) %collective-permute-start.11) | collective-permute-done | bytes 393248 | tf_op jit(solution)/shard_map/ppermute | solution.py:58
  115.6 1.4 collective-permute-done.10
  116.9 1.0 collective-permute-start.12
  118.1 2.3 %collective-permute-start.13 = (bf16[2,96,1024]{2,1,0:T(8,128)(2,1)S(1)}, bf16[2,96,1024]{2,1,0:T(8,128)(2,1)S(1)}, u32[]{:S(2)}, u32[]{:S(2)}) collective-permute-start(bf16[2,96,1024]{2,1,0:T(8,128)(2,1)S(1)} %collective-permute-done.11), channel_id=1, source_target_pairs={{0,3},{1,0},{2,1},{3,2},{4,7},{5,4},{6,5},{7,6},{8,11},{9,8},{10,9... | collective-permute-start | bytes 1179656 | tf_op jit(solution)/shard_map/ppermute | solution.py:58
  120.6 7.3 %collective-permute-done.13 = bf16[2,96,1024]{2,1,0:T(8,128)(2,1)S(1)} collective-permute-done((bf16[2,96,1024]{2,1,0:T(8,128)(2,1)S(1)}, bf16[2,96,1024]{2,1,0:T(8,128)(2,1)S(1)}, u32[]{:S(2)}, u32[]{:S(2)}) %collective-permute-start.13) | collective-permute-done | bytes 393248 | tf_op jit(solution)/shard_map/ppermute | solution.py:58
  127.8 2.3 %collective-permute-start.14 = (bf16[2,96,1024]{2,1,0:T(8,128)(2,1)S(1)}, bf16[2,96,1024]{2,1,0:T(8,128)(2,1)S(1)}, u32[]{:S(2)}, u32[]{:S(2)}) collective-permute-start(bf16[2,96,1024]{2,1,0:T(8,128)(2,1)S(1)} %get-tuple-element.21), channel_id=1, source_target_pairs={{0,3},{1,0},{2,1},{3,2},{4,7},{5,4},{6,5},{7,6},{8,11},{9,8},{10,9... | collective-permute-start | bytes 1179656 | tf_op jit(solution)/shard_map/ppermute | solution.py:58
  130.2 1.6 fusion.33
  131.9 0.6 copy-done.18
  132.5 1.6 convolution_add_fusion.1
  134.3 6.6 %collective-permute-done.15 = bf16[2,96,1024]{2,1,0:T(8,128)(2,1)S(1)} collective-permute-done((bf16[2,96,1024]{2,1,0:T(8,128)(2,1)S(1)}, bf16[2,96,1024]{2,1,0:T(8,128)(2,1)S(1)}, u32[]{:S(2)}, u32[]{:S(2)}) %collective-permute-start.15) | collective-permute-done | bytes 393248 | tf_op jit(solution)/shard_map/ppermute | solution.py:55
  141.0 1.6 fusion.34
  142.6 1.6 convolution_add_fusion
  144.3 1.3 add_convert_fusion
  145.6 2.0 %collective-permute-start.17 = (bf16[2,96,1024]{2,1,0:T(8,128)(2,1)S(1)}, bf16[2,96,1024]{2,1,0:T(8,128)(2,1)}, u32[]{:S(2)}, u32[]{:S(2)}) collective-permute-start(bf16[2,96,1024]{2,1,0:T(8,128)(2,1)S(1)} %fusion.5), channel_id=1, source_target_pairs={{0,1},{1,2},{2,3},{3,0},{4,5},{5,6},{6,7},{7,4},{8,9},{9,10},{10,1... | collective-permute-start | bytes 1179656 | tf_op jit(solution)/shard_map/ppermute | solution.py:55
  147.6 7.3 %all-to-all-start.2 = ((bf16[16,24,1792]{2,1,0:T(8,128)(2,1)}), bf16[16,24,1792]{2,1,0:T(8,128)(2,1)S(1)}, u32[]{:S(2)}, u32[]{:S(2)}) async-start(bf16[16,24,1792]{2,1,0:T(8,128)(2,1)} %bitcast.52), calls=%async_computation.2 | async-start | bytes 2752512 | tf_op jit(solution)/shard_map/all_to_all | solution.py:115
  154.9 7.1 %convolution_convert_fusion.2 = bf16[1792,1024]{1,0:T(8,128)(2,1)} fusion(bf16[384,1024]{1,0:T(8,128)(2,1)} %copy-done.8, bf16[384,1024]{1,0:T(8,128)(2,1)} %copy-done.7, bf16[384,1792]{1,0:T(8,128)(2,1)} %collective-permute-done, bf16[384,1792]{1,0:T(8,128)(2,1)} %bitcast.189), kind=kOutput, calls=%fused_computation.2 | convolution fusion | flops 2829058048 | bytes 7995392 | tf_op jit(solution)/shard_map/dot_general | solution.py:8
  162.2 1.0 slice_bitcast_fusion.1
  163.2 1.3 collective-permute-start.20
  164.5 0.9 slice_bitcast_fusion.2
  165.4 0.9 collective-permute-start.19
  166.3 5.9 %convolution_convert_fusion.1 = bf16[1792,1024]{1,0:T(8,128)(2,1)} fusion(bf16[768,1024]{1,0:T(8,128)(2,1)S(1)} %pad_maximum_fusion.1, bf16[384,1792]{1,0:T(8,128)(2,1)} %collective-permute-done, bf16[384,1792]{1,0:T(8,128)(2,1)S(1)} %bitcast.190), kind=kOutput, calls=%fused_computation.1 | convolution fusion | flops 2825912320 | bytes 7995392 | tf_op jit(solution)/shard_map/dot_general | solution.py:8
  172.2 0.9 fusion.20
  173.1 0.9 constant_dynamic-update-slice_fusion.4
  174.1 0.9 constant_dynamic-update-slice_fusion.3
  175.1 0.9 fusion.19
  176.1 4.6 %convolution_convert_fusion = bf16[1024,1792]{1,0:T(8,128)(2,1)} fusion(bf16[768,1024]{1,0:T(8,128)(2,1)S(1)} %fusion.19, bf16[768,1792]{1,0:T(8,128)(2,1)S(1)} %copy-done.14), kind=kOutput, calls=%fused_computation | convolution fusion | flops 2820407296 | bytes 7995392 | tf_op jit(solution)/shard_map/dot_general | solution.py:8
  180.7 1.2 convolution_convert_fusion.4
  (98 shorter events, 2.7 us)
Async XLA Ops:
  0.6 2.2 %copy-start = (bf16[128,1792]{1,0:T(8,128)(2,1)S(1)}, bf16[128,1792]{1,0:T(8,128)(2,1)}, u32[]{:S(2)}) copy-start(bf16[128,1792]{1,0:T(8,128)(2,1)} %param.7) | copy-start | bytes 1376260
  0.6 29.3 %copy-start.15 = (f32[128,2]{0,1:T(2,128)S(1)}, f32[128,2]{0,1:T(2,128)}, u32[]{:S(2)}) copy-start(f32[128,2]{0,1:T(2,128)} %param.10) | copy-start | bytes 3076
  0.7 29.4 %copy-start.9 = (bf16[128,1792]{1,0:T(8,128)(2,1)S(1)}, bf16[128,1792]{1,0:T(8,128)(2,1)}, u32[]{:S(2)}) copy-start(bf16[128,1792]{1,0:T(8,128)(2,1)} %param.8) | copy-start | bytes 1376260
  29.9 12.3 %copy-start.2 = (bf16[16,24,1792]{2,1,0:T(8,128)(2,1)}, bf16[16,24,1792]{2,1,0:T(8,128)(2,1)S(1)}, u32[]{:S(2)}) copy-start(bf16[16,24,1792]{2,1,0:T(8,128)(2,1)S(1)} %all_to_all.15) | copy-start | bytes 4128772
  29.9 6.7 %collective-permute-start = (bf16[384,1792]{1,0:T(8,128)(2,1)S(1)}, bf16[384,1792]{1,0:T(8,128)(2,1)}, u32[]{:S(2)}, u32[]{:S(2)}) collective-permute-start(bf16[384,1792]{1,0:T(8,128)(2,1)S(1)} %bitcast.186), channel_id=1, source_target_pairs={{0,4},{4,0},{8,12},{12,8},{16,20},{20,16},{24,28},{28,24},{32,36},... | collective-permute-start | bytes 4128776 | tf_op jit(solution)/shard_map/ppermute | solution.py:125
  31.7 25.9 %all-to-all-start.1 = ((bf16[16,24,1792]{2,1,0:T(8,128)(2,1)}), bf16[16,24,1792]{2,1,0:T(8,128)(2,1)S(1)}, u32[]{:S(2)}, u32[]{:S(2)}) async-start(bf16[16,24,1792]{2,1,0:T(8,128)(2,1)} %bitcast.2), calls=%async_computation.1 | async-start | bytes 2752512 | tf_op jit(solution)/shard_map/all_to_all | solution.py:115
  36.7 5.6 %copy-start.17 = (bf16[1792,1024]{1,0:T(8,128)(2,1)S(1)}, bf16[1792,1024]{1,0:T(8,128)(2,1)}, u32[]{:S(2)}) copy-start(bf16[1792,1024]{1,0:T(8,128)(2,1)} %param.11) | copy-start | bytes 11010052
  48.1 13.6 %collective-permute-start.1 = (bf16[2,96,1024]{2,1,0:T(8,128)(2,1)S(1)}, bf16[2,96,1024]{2,1,0:T(8,128)(2,1)S(1)}, u32[]{:S(2)}, u32[]{:S(2)}) collective-permute-start(bf16[2,96,1024]{2,1,0:T(8,128)(2,1)S(1)} %pad_maximum_fusion.4), channel_id=1, source_target_pairs={{0,1},{1,2},{2,3},{3,0},{4,5},{5,6},{6,7},{7,4},{8,9},{9,10},{10,1... | collective-permute-start | bytes 1179656 | tf_op jit(solution)/shard_map/ppermute | solution.py:55
  50.1 11.6 %collective-permute-start.2 = (bf16[2,96,1024]{2,1,0:T(8,128)(2,1)S(1)}, bf16[2,96,1024]{2,1,0:T(8,128)(2,1)S(1)}, u32[]{:S(2)}, u32[]{:S(2)}) collective-permute-start(bf16[2,96,1024]{2,1,0:T(8,128)(2,1)S(1)} %pad_maximum_fusion.5), channel_id=1, source_target_pairs={{0,3},{1,0},{2,1},{3,2},{4,7},{5,4},{6,5},{7,6},{8,11},{9,8},{10,9... | collective-permute-start | bytes 1179656 | tf_op jit(solution)/shard_map/ppermute | solution.py:58
  61.7 0.7 copy-start.10
  62.4 0.7 copy-start.12
  62.4 8.2 %collective-permute-start.3 = (bf16[384,1792]{1,0:T(8,128)(2,1)S(1)}, bf16[384,1792]{1,0:T(8,128)(2,1)S(1)}, u32[]{:S(2)}, u32[]{:S(2)}) collective-permute-start(bf16[384,1792]{1,0:T(8,128)(2,1)S(1)} %bitcast.182), channel_id=1, source_target_pairs={{0,4},{4,0},{8,12},{12,8},{16,20},{20,16},{24,28},{28,24},{32,36},... | collective-permute-start | bytes 4128776 | tf_op jit(solution)/shard_map/ppermute | solution.py:125
  62.4 4.2 %copy-start.5 = (bf16[1,1,96,1024]{3,2,1,0:T(8,128)(2,1)S(1)}, bf16[1,1,96,1024]{3,2,1,0:T(8,128)(2,1)}, u32[]{:S(2)}) copy-start(bf16[1,1,96,1024]{3,2,1,0:T(8,128)(2,1)} %get-tuple-element.48) | copy-start | bytes 589828
  62.4 4.2 %copy-start.6 = (bf16[1,1,96,1024]{3,2,1,0:T(8,128)(2,1)S(1)}, bf16[1,1,96,1024]{3,2,1,0:T(8,128)(2,1)}, u32[]{:S(2)}) copy-start(bf16[1,1,96,1024]{3,2,1,0:T(8,128)(2,1)} %get-tuple-element.73) | copy-start | bytes 589828
  62.4 6.7 %copy-start.11 = (bf16[2,96,1024]{2,1,0:T(8,128)(2,1)S(1)}, bf16[2,96,1024]{2,1,0:T(8,128)(2,1)}, u32[]{:S(2)}) copy-start(bf16[2,96,1024]{2,1,0:T(8,128)(2,1)} %copy-done.10) | copy-start | bytes 1179652
  63.2 7.1 %copy-start.4 = (bf16[1,1,96,1024]{3,2,1,0:T(8,128)(2,1)S(1)}, bf16[1,1,96,1024]{3,2,1,0:T(8,128)(2,1)}, u32[]{:S(2)}) copy-start(bf16[1,1,96,1024]{3,2,1,0:T(8,128)(2,1)} %get-tuple-element.72) | copy-start | bytes 589828
  66.7 20.5 %collective-permute-start.9 = (bf16[2,2,96,1024]{3,2,1,0:T(8,128)(2,1)S(1)}, bf16[2,2,96,1024]{3,2,1,0:T(8,128)(2,1)S(1)}, u32[]{:S(2)}, u32[]{:S(2)}) collective-permute-start(bf16[2,2,96,1024]{3,2,1,0:T(8,128)(2,1)S(1)} %pad_maximum_fusion.2), channel_id=1, source_target_pairs={{0,3},{1,0},{2,1},{3,2},{4,7},{5,4},{6,5},{7,6},{8,11},{9,8},{10,9... | collective-permute-start | bytes 2359304 | tf_op jit(solution)/shard_map/ppermute | solution.py:58
  70.4 2.0 %copy-start.16 = (bf16[1024,1792]{1,0:T(8,128)(2,1)S(1)}, bf16[1024,1792]{1,0:T(8,128)(2,1)}, u32[]{:S(2)}) copy-start(bf16[1024,1792]{1,0:T(8,128)(2,1)} %param.13) | copy-start | bytes 11010052
  70.4 24.5 %collective-permute-start.8 = (bf16[2,2,96,1024]{3,2,1,0:T(8,128)(2,1)S(1)}, bf16[2,2,96,1024]{3,2,1,0:T(8,128)(2,1)S(1)}, u32[]{:S(2)}, u32[]{:S(2)}) collective-permute-start(bf16[2,2,96,1024]{3,2,1,0:T(8,128)(2,1)S(1)} %maximum_maximum_fusion), channel_id=1, source_target_pairs={{0,1},{1,2},{2,3},{3,0},{4,5},{5,6},{6,7},{7,4},{8,9},{9,10},{10,1... | collective-permute-start | bytes 2359304 | tf_op jit(solution)/shard_map/ppermute | solution.py:55
  75.6 14.7 %collective-permute-start.6 = (bf16[1,96,1024]{2,1,0:T(8,128)(2,1)S(1)}, bf16[1,96,1024]{2,1,0:T(8,128)(2,1)S(1)}, u32[]{:S(2)}, u32[]{:S(2)}) collective-permute-start(bf16[1,96,1024]{2,1,0:T(8,128)(2,1)S(1)} %get-tuple-element.31), channel_id=1, source_target_pairs={{0,3},{1,0},{2,1},{3,2},{4,7},{5,4},{6,5},{7,6},{8,11},{9,8},{10,9... | collective-permute-start | bytes 589832 | tf_op jit(solution)/shard_map/ppermute | solution.py:58
  77.2 17.7 %collective-permute-start.4 = (bf16[1,96,1024]{2,1,0:T(8,128)(2,1)S(1)}, bf16[1,96,1024]{2,1,0:T(8,128)(2,1)S(1)}, u32[]{:S(2)}, u32[]{:S(2)}) collective-permute-start(bf16[1,96,1024]{2,1,0:T(8,128)(2,1)S(1)} %get-tuple-element.34), channel_id=1, source_target_pairs={{0,1},{1,2},{2,3},{3,0},{4,5},{5,6},{6,7},{7,4},{8,9},{9,10},{10,1... | collective-permute-start | bytes 589832 | tf_op jit(solution)/shard_map/ppermute | solution.py:55
  78.0 19.7 %copy-start.13 = (bf16[768,1792]{1,0:T(8,128)(2,1)}, bf16[768,1792]{1,0:T(8,128)(2,1)S(1)}, u32[]{:S(2)}) copy-start(bf16[768,1792]{1,0:T(8,128)(2,1)S(1)} %dynamic-slice_dynamic-update-slice_fusion) | copy-start | bytes 8257540
  95.1 9.7 %collective-permute-start.7 = (bf16[1,2,96,1024]{3,2,1,0:T(8,128)(2,1)S(1)}, bf16[1,2,96,1024]{3,2,1,0:T(8,128)(2,1)S(1)}, u32[]{:S(2)}, u32[]{:S(2)}) collective-permute-start(bf16[1,2,96,1024]{3,2,1,0:T(8,128)(2,1)S(1)} %pad_maximum_fusion.8), channel_id=1, source_target_pairs={{0,3},{1,0},{2,1},{3,2},{4,7},{5,4},{6,5},{7,6},{8,11},{9,8},{10,9... | collective-permute-start | bytes 1179656 | tf_op jit(solution)/shard_map/ppermute | solution.py:58
  95.2 10.9 %collective-permute-start.5 = (bf16[1,2,96,1024]{3,2,1,0:T(8,128)(2,1)S(1)}, bf16[1,2,96,1024]{3,2,1,0:T(8,128)(2,1)S(1)}, u32[]{:S(2)}, u32[]{:S(2)}) collective-permute-start(bf16[1,2,96,1024]{3,2,1,0:T(8,128)(2,1)S(1)} %pad_maximum_fusion.7), channel_id=1, source_target_pairs={{0,1},{1,2},{2,3},{3,0},{4,5},{5,6},{6,7},{7,4},{8,9},{9,10},{10,1... | collective-permute-start | bytes 1179656 | tf_op jit(solution)/shard_map/ppermute | solution.py:55
  106.8 8.8 %collective-permute-start.11 = (bf16[2,96,1024]{2,1,0:T(8,128)(2,1)S(1)}, bf16[2,96,1024]{2,1,0:T(8,128)(2,1)S(1)}, u32[]{:S(2)}, u32[]{:S(2)}) collective-permute-start(bf16[2,96,1024]{2,1,0:T(8,128)(2,1)S(1)} %get-tuple-element.54), channel_id=1, source_target_pairs={{0,3},{1,0},{2,1},{3,2},{4,7},{5,4},{6,5},{7,6},{8,11},{9,8},{10,9... | collective-permute-start | bytes 1179656 | tf_op jit(solution)/shard_map/ppermute | solution.py:58
  107.0 9.9 %collective-permute-start.10 = (bf16[2,96,1024]{2,1,0:T(8,128)(2,1)S(1)}, bf16[2,96,1024]{2,1,0:T(8,128)(2,1)S(1)}, u32[]{:S(2)}, u32[]{:S(2)}) collective-permute-start(bf16[2,96,1024]{2,1,0:T(8,128)(2,1)S(1)} %get-tuple-element.54), channel_id=1, source_target_pairs={{0,1},{1,2},{2,3},{3,0},{4,5},{5,6},{6,7},{7,4},{8,9},{9,10},{10,1... | collective-permute-start | bytes 1179656 | tf_op jit(solution)/shard_map/ppermute | solution.py:55
  109.1 21.1 %copy-start.19 = (bf16[1792,1024]{1,0:T(8,128)(2,1)S(1)}, bf16[1792,1024]{1,0:T(8,128)(2,1)}, u32[]{:S(2)}) copy-start(bf16[1792,1024]{1,0:T(8,128)(2,1)} %param.12) | copy-start | bytes 11010052
  116.9 14.9 %collective-permute-start.12 = (bf16[2,96,1024]{2,1,0:T(8,128)(2,1)S(1)}, bf16[2,96,1024]{2,1,0:T(8,128)(2,1)S(1)}, u32[]{:S(2)}, u32[]{:S(2)}) collective-permute-start(bf16[2,96,1024]{2,1,0:T(8,128)(2,1)S(1)} %get-tuple-element.21), channel_id=1, source_target_pairs={{0,1},{1,2},{2,3},{3,0},{4,5},{5,6},{6,7},{7,4},{8,9},{9,10},{10,1... | collective-permute-start | bytes 1179656 | tf_op jit(solution)/shard_map/ppermute | solution.py:55
  118.1 9.8 %collective-permute-start.13 = (bf16[2,96,1024]{2,1,0:T(8,128)(2,1)S(1)}, bf16[2,96,1024]{2,1,0:T(8,128)(2,1)S(1)}, u32[]{:S(2)}, u32[]{:S(2)}) collective-permute-start(bf16[2,96,1024]{2,1,0:T(8,128)(2,1)S(1)} %collective-permute-done.11), channel_id=1, source_target_pairs={{0,3},{1,0},{2,1},{3,2},{4,7},{5,4},{6,5},{7,6},{8,11},{9,8},{10,9... | collective-permute-start | bytes 1179656 | tf_op jit(solution)/shard_map/ppermute | solution.py:58
  127.8 13.0 %collective-permute-start.14 = (bf16[2,96,1024]{2,1,0:T(8,128)(2,1)S(1)}, bf16[2,96,1024]{2,1,0:T(8,128)(2,1)S(1)}, u32[]{:S(2)}, u32[]{:S(2)}) collective-permute-start(bf16[2,96,1024]{2,1,0:T(8,128)(2,1)S(1)} %get-tuple-element.21), channel_id=1, source_target_pairs={{0,3},{1,0},{2,1},{3,2},{4,7},{5,4},{6,5},{7,6},{8,11},{9,8},{10,9... | collective-permute-start | bytes 1179656 | tf_op jit(solution)/shard_map/ppermute | solution.py:58
  130.1 1.8 copy-start.8
  130.2 2.3 %copy-start.18 = (bf16[1792,1024]{1,0:T(8,128)(2,1)S(1)}, bf16[1792,1024]{1,0:T(8,128)(2,1)}, u32[]{:S(2)}) copy-start(bf16[1792,1024]{1,0:T(8,128)(2,1)} %param.11) | copy-start | bytes 11010052
  131.8 9.1 %collective-permute-start.15 = (bf16[2,96,1024]{2,1,0:T(8,128)(2,1)S(1)}, bf16[2,96,1024]{2,1,0:T(8,128)(2,1)S(1)}, u32[]{:S(2)}, u32[]{:S(2)}) collective-permute-start(bf16[2,96,1024]{2,1,0:T(8,128)(2,1)S(1)} %collective-permute-done.12), channel_id=1, source_target_pairs={{0,1},{1,2},{2,3},{3,0},{4,5},{5,6},{6,7},{7,4},{8,9},{9,10},{10,1... | collective-permute-start | bytes 1179656 | tf_op jit(solution)/shard_map/ppermute | solution.py:55
  134.1 10.1 %collective-permute-start.16 = (bf16[384,1792]{1,0:T(8,128)(2,1)S(1)}, bf16[384,1792]{1,0:T(8,128)(2,1)S(1)}, u32[]{:S(2)}, u32[]{:S(2)}) collective-permute-start(bf16[384,1792]{1,0:T(8,128)(2,1)S(1)} %convolution_add_fusion.1), channel_id=1, source_target_pairs={{0,4},{4,0},{8,12},{12,8},{16,20},{20,16},{24,28},{28,24},{32,36},... | collective-permute-start | bytes 4128776 | tf_op jit(solution)/shard_map/ppermute | solution.py:125
  141.0 1.6 copy-start.7
  145.6 16.6 %collective-permute-start.18 = (bf16[2,96,1024]{2,1,0:T(8,128)(2,1)S(1)}, bf16[2,96,1024]{2,1,0:T(8,128)(2,1)}, u32[]{:S(2)}, u32[]{:S(2)}) collective-permute-start(bf16[2,96,1024]{2,1,0:T(8,128)(2,1)S(1)} %fusion.5), channel_id=1, source_target_pairs={{0,3},{1,0},{2,1},{3,2},{4,7},{5,4},{6,5},{7,6},{8,11},{9,8},{10,9... | collective-permute-start | bytes 1179656 | tf_op jit(solution)/shard_map/ppermute | solution.py:58
  145.6 18.9 %collective-permute-start.17 = (bf16[2,96,1024]{2,1,0:T(8,128)(2,1)S(1)}, bf16[2,96,1024]{2,1,0:T(8,128)(2,1)}, u32[]{:S(2)}, u32[]{:S(2)}) collective-permute-start(bf16[2,96,1024]{2,1,0:T(8,128)(2,1)S(1)} %fusion.5), channel_id=1, source_target_pairs={{0,1},{1,2},{2,3},{3,0},{4,5},{5,6},{6,7},{7,4},{8,9},{9,10},{10,1... | collective-permute-start | bytes 1179656 | tf_op jit(solution)/shard_map/ppermute | solution.py:55
  147.6 33.0 %all-to-all-start.2 = ((bf16[16,24,1792]{2,1,0:T(8,128)(2,1)}), bf16[16,24,1792]{2,1,0:T(8,128)(2,1)S(1)}, u32[]{:S(2)}, u32[]{:S(2)}) async-start(bf16[16,24,1792]{2,1,0:T(8,128)(2,1)} %bitcast.52), calls=%async_computation.2 | async-start | bytes 2752512 | tf_op jit(solution)/shard_map/all_to_all | solution.py:115
  162.0 4.3 %copy-start.3 = (bf16[16,24,1792]{2,1,0:T(8,128)(2,1)S(1)}, bf16[16,24,1792]{2,1,0:T(8,128)(2,1)}, u32[]{:S(2)}) copy-start(bf16[16,24,1792]{2,1,0:T(8,128)(2,1)} %copy-done.2) | copy-start | bytes 4128772
  163.2 11.9 %collective-permute-start.20 = (bf16[96,1024]{1,0:T(8,128)(2,1)S(1)}, bf16[96,1024]{1,0:T(8,128)(2,1)S(1)}, u32[]{:S(2)}, u32[]{:S(2)}) collective-permute-start(bf16[96,1024]{1,0:T(8,128)(2,1)S(1)} %slice_bitcast_fusion.1), channel_id=1, source_target_pairs={{0,3},{1,0},{2,1},{3,2},{4,7},{5,4},{6,5},{7,6},{8,11},{9,8},{10,9... | collective-permute-start | bytes 589832 | tf_op jit(solution)/shard_map/ppermute | solution.py:58
  165.4 10.6 %copy-start.14 = (bf16[768,1792]{1,0:T(8,128)(2,1)S(1)}, bf16[768,1792]{1,0:T(8,128)(2,1)}, u32[]{:S(2)}) copy-start(bf16[768,1792]{1,0:T(8,128)(2,1)} %copy-done.13) | copy-start | bytes 8257540
  165.4 7.7 %collective-permute-start.19 = (bf16[96,1024]{1,0:T(8,128)(2,1)S(1)}, bf16[96,1024]{1,0:T(8,128)(2,1)S(1)}, u32[]{:S(2)}, u32[]{:S(2)}) collective-permute-start(bf16[96,1024]{1,0:T(8,128)(2,1)S(1)} %slice_bitcast_fusion.2), channel_id=1, source_target_pairs={{0,1},{1,2},{2,3},{3,0},{4,5},{5,6},{6,7},{7,4},{8,9},{9,10},{10,1... | collective-permute-start | bytes 589832 | tf_op jit(solution)/shard_map/ppermute | solution.py:55
  176.0 5.8 %copy-start.1 = (bf16[128,1792]{1,0:T(8,128)(2,1)S(1)}, bf16[128,1792]{1,0:T(8,128)(2,1)}, u32[]{:S(2)}) copy-start(bf16[128,1792]{1,0:T(8,128)(2,1)} %param.7) | copy-start | bytes 1376260
